TPU v7x, 128 devices: a whole 4x4x4 slice. The times are simulated.
128 devices in a mesh: dp: 64 (over z_hi, x, y, core), tensor: 2 (over z_lo).
Axes of the slice: x: 4, y: 4, z: 4 (z_hi: 2, z_lo: 2; z = z_hi * 2 + z_lo), core: 2. Of those that a mesh axis runs over, the one named last changes fastest.
Arguments:
- hidden_in: bfloat16 [128, 192, 1152], P('dp'), may hold values from -6 to 6
- row_layout: int32 [128, 4], P('dp'), may hold values from 1 to 96, 192 in all within a row
- cotangent: bfloat16 [128, 192, 1152], P('dp'), may hold values from -6 to 6
- pre_gain: float32 [1152], replicated, may hold values from 0.1 to 1.9
- pre_shift: float32 [1152], replicated, may hold values from -4 to 4
- query_weight: bfloat16 [1152, 1152], P(None, 'tensor'), may hold values from -0.25 to 0.25
- query_bias: float32 [1152], P('tensor'), may hold values from -6 to 6
- key_weight: bfloat16 [1152, 1152], P(None, 'tensor'), may hold values from -0.25 to 0.25
- value_weight: bfloat16 [1152, 1152], P(None, 'tensor'), may hold values from -0.1875 to 0.1875
- value_bias: float32 [1152], P('tensor'), may hold values from -6 to 6
- out_weight: bfloat16 [1152, 1152], P('tensor'), may hold values from -0.75 to 0.75
- out_bias: float32 [1152], replicated, may hold values from -4 to 4
- mid_gain: float32 [1152], replicated, may hold values from 0.1 to 1.9
- mid_shift: float32 [1152], replicated, may hold values from -4 to 4
- up_weight: bfloat16 [1152, 4304], P(None, 'tensor'), may hold values from -0.1875 to 0.1875
- up_bias: float32 [4304], P('tensor'), may hold values from -6 to 6
- down_weight: bfloat16 [4304, 1152], P('tensor'), may hold values from -0.09375 to 0.09375
- down_bias: float32 [1152], replicated, may hold values from -4 to 4
Outputs:
- mixed: bfloat16 [128, 192, 1152], P('dp')
- input_grad: bfloat16 [128, 192, 1152], P('dp')
- pre_gain_grad: float32 [1152], replicated
- pre_shift_grad: float32 [1152], replicated
- query_weight_grad: float32 [1152, 1152], P(None, 'tensor')
- query_bias_grad: float32 [1152], P('tensor')
- key_weight_grad: float32 [1152, 1152], P(None, 'tensor')
- value_weight_grad: float32 [1152, 1152], P(None, 'tensor')
- value_bias_grad: float32 [1152], P('tensor')
- out_weight_grad: float32 [1152, 1152], P('tensor')
- out_bias_grad: float32 [1152], replicated
- mid_gain_grad: float32 [1152], replicated
- mid_shift_grad: float32 [1152], replicated
- up_weight_grad: float32 [1152, 4304], P(None, 'tensor')
- up_bias_grad: float32 [4304], P('tensor')
- down_weight_grad: float32 [4304, 1152], P('tensor')
- down_bias_grad: float32 [1152], replicated
Inputs may be any that keep to these rules, and one draw needn't show every extreme that they name: `row_layout`: each row's first 3 entries are its pictures' patch counts, the last entry the count of padding positions at the row's end; the entries of a row sum to 192, and the largest entry of each row is 96.
All inputs are finite; a program needn't handle non-finite values.
Results may differ from a plain program's by a relative error of at most 0.013.
The roundings to bfloat16 on the way count: a program that leaves them out, or rounds other values in their place, can miss the bound.
Values sent between devices are 32-bit elements; how exact they have to be, the bound alone decides.
No kernel may reach another device: no remote copies, remote signals or barrier semaphores. Data moves between devices by JAX's collectives and lax.ppermute only.
A program may use at most 192 MiB of HBM per device.

v0:
```python
import jax
import jax.numpy as jnp
from jax import lax
from jax.sharding import PartitionSpec as P

HEAD = 72


norm_epsilon = 1e-06


def layer_norm(values, norm_gain, norm_shift):
    center = values - jnp.mean(values, axis=-1, keepdims=True)
    spread = jnp.mean(center * center, axis=-1, keepdims=True)
    return center * lax.rsqrt(spread + norm_epsilon) * norm_gain + norm_shift


def gelu_tanh(values):
    return jax.nn.gelu(values, approximate=True)


def product(left, right):
    return jnp.dot(left, right, preferred_element_type=jnp.float32)


def inner_rows(left, right):
    return lax.dot_general(
        left, right, (((0,), (0,)), ((), ())), preferred_element_type=jnp.float32
    )


def against(left, right):
    return lax.dot_general(
        left, right, (((1,), (1,)), ((), ())), preferred_element_type=jnp.float32
    )


def segments(layout, length):
    bounds = jnp.cumsum(layout[:, :-1], axis=1)
    places = jnp.arange(length, dtype=jnp.int32)
    inside = (places[None, :, None] >= bounds[:, None, :]).astype(jnp.int32)
    return jnp.sum(inside, axis=2)


def head_scores(queries_heads, keys_heads, same_picture, scale_factor):
    raw = (
        jnp.einsum("qhd,khd->hqk", queries_heads, keys_heads, preferred_element_type=jnp.float32)
        * scale_factor
    )
    return jnp.where(same_picture[None], raw, -1000000000.0)


def add_terms(totals, terms):
    return tuple((total + term for total, term in zip(totals, terms)))


def zero_terms(members):
    return tuple((jnp.zeros(member.shape, jnp.float32) for member in members))


def shards(
    hidden_in,
    row_layout,
    cotangent,
    pre_gain,
    pre_shift,
    query_weight,
    query_bias,
    key_weight,
    value_weight,
    value_bias,
    out_weight,
    out_bias,
    mid_gain,
    mid_shift,
    up_weight,
    up_bias,
    down_weight,
    down_bias,
):
    row_count = hidden_in.shape[0]
    length = hidden_in.shape[1]
    heads_here = query_weight.shape[1] // HEAD
    scale_factor = HEAD ** (-0.5)
    head_shape = (length, heads_here, HEAD)

    def forward_row(row_index):
        inputs_row = lax.dynamic_index_in_dim(hidden_in, row_index, 0, keepdims=False).astype(
            jnp.float32
        )
        layout_row = lax.dynamic_index_in_dim(row_layout, row_index, 0, keepdims=True)
        segment_row = segments(layout_row, length)[0]
        same_picture = segment_row[:, None] == segment_row[None, :]
        normed = layer_norm(inputs_row, pre_gain, pre_shift).astype(jnp.bfloat16)
        queries = (
            (product(normed, query_weight) + query_bias).astype(jnp.bfloat16).reshape(head_shape)
        )
        keys_row = product(normed, key_weight).astype(jnp.bfloat16).reshape(head_shape)
        values_row = (
            (product(normed, value_weight) + value_bias).astype(jnp.bfloat16).reshape(head_shape)
        )
        scores = head_scores(queries, keys_row, same_picture, scale_factor)
        maximum = jnp.max(scores, axis=-1, keepdims=True)
        exponent = jnp.exp(scores - maximum)
        row_total = jnp.sum(exponent, axis=-1, keepdims=True)
        log_total = maximum + jnp.log(row_total)
        probs_low = (exponent / row_total).astype(jnp.bfloat16)
        attended = jnp.einsum(
            "hqk,khd->qhd", probs_low, values_row, preferred_element_type=jnp.float32
        )
        attended = attended.reshape(length, heads_here * HEAD).astype(jnp.bfloat16)
        branch = lax.psum(product(attended, out_weight), "tensor") + out_bias
        resid = inputs_row + branch
        middle = layer_norm(resid, mid_gain, mid_shift).astype(jnp.bfloat16)
        pre_act = product(middle, up_weight) + up_bias
        activ = gelu_tanh(pre_act).astype(jnp.bfloat16)
        output_row = resid + lax.psum(product(activ, down_weight), "tensor") + down_bias
        saved = (
            inputs_row,
            same_picture,
            normed,
            queries,
            keys_row,
            values_row,
            log_total,
            attended,
            resid,
            middle,
            pre_act,
            activ,
        )
        return (saved, output_row)

    def mlp_back(saved, row_index):
        (
            inputs_row,
            same_picture,
            normed,
            queries,
            keys_row,
            values_row,
            log_total,
            attended,
            resid,
            middle,
            pre_act,
            activ,
        ) = saved
        cot_row = lax.dynamic_index_in_dim(cotangent, row_index, 0, keepdims=False)
        cot_float = cot_row.astype(jnp.float32)
        down_grad = inner_rows(activ, cot_row)
        down_bias_term = jnp.sum(cot_float, axis=0)
        act_grad = against(cot_row, down_weight)
        gelu_pull = jax.vjp(gelu_tanh, pre_act)[1]
        pre_grad = gelu_pull(act_grad)[0].astype(jnp.bfloat16)
        up_grad = inner_rows(middle, pre_grad)
        up_bias_term = jnp.sum(pre_grad.astype(jnp.float32), axis=0)
        mid_grad = lax.psum(against(pre_grad, up_weight), "tensor")
        norm_pull = jax.vjp(layer_norm, resid, mid_gain, mid_shift)[1]
        resid_part, mid_gain_term, mid_shift_term = norm_pull(mid_grad)
        resid_grad = cot_float + resid_part
        return (
            resid_grad,
            (mid_gain_term, mid_shift_term, up_grad, up_bias_term, down_grad, down_bias_term),
        )

    def attn_back(saved, resid_grad):
        (
            inputs_row,
            same_picture,
            normed,
            queries,
            keys_row,
            values_row,
            log_total,
            attended,
            resid,
            middle,
            pre_act,
            activ,
        ) = saved
        branch_grad = resid_grad.astype(jnp.bfloat16)
        out_grad = inner_rows(attended, branch_grad)
        out_bias_term = jnp.sum(branch_grad.astype(jnp.float32), axis=0)
        attended_grad = against(branch_grad, out_weight).astype(jnp.bfloat16).reshape(head_shape)
        scores = head_scores(queries, keys_row, same_picture, scale_factor)
        probs = jnp.exp(scores - log_total)
        probs_low = probs.astype(jnp.bfloat16)
        value_grad = jnp.einsum(
            "hqk,qhd->khd", probs_low, attended_grad, preferred_element_type=jnp.float32
        ).astype(jnp.bfloat16)
        prob_grad = jnp.einsum(
            "qhd,khd->hqk", attended_grad, values_row, preferred_element_type=jnp.float32
        )
        score_grad = (
            probs * (prob_grad - jnp.sum(prob_grad * probs, axis=-1, keepdims=True))
        ).astype(jnp.bfloat16)
        query_grad = (
            jnp.einsum("hqk,khd->qhd", score_grad, keys_row, preferred_element_type=jnp.float32)
            * scale_factor
        ).astype(jnp.bfloat16)
        key_grad = (
            jnp.einsum("hqk,qhd->khd", score_grad, queries, preferred_element_type=jnp.float32)
            * scale_factor
        ).astype(jnp.bfloat16)
        query_grad = query_grad.reshape(length, heads_here * HEAD)
        key_grad = key_grad.reshape(length, heads_here * HEAD)
        value_grad = value_grad.reshape(length, heads_here * HEAD)
        query_weight_term = inner_rows(normed, query_grad)
        query_bias_term = jnp.sum(query_grad.astype(jnp.float32), axis=0)
        key_weight_term = inner_rows(normed, key_grad)
        value_weight_term = inner_rows(normed, value_grad)
        value_bias_term = jnp.sum(value_grad.astype(jnp.float32), axis=0)
        normed_part = (
            against(query_grad, query_weight)
            + against(key_grad, key_weight)
            + against(value_grad, value_weight)
        )
        normed_grad = lax.psum(normed_part, "tensor")
        norm_pull = jax.vjp(layer_norm, inputs_row, pre_gain, pre_shift)[1]
        input_part, pre_gain_term, pre_shift_term = norm_pull(normed_grad)
        input_row_grad = resid_grad + input_part
        return (
            input_row_grad,
            (
                pre_gain_term,
                pre_shift_term,
                query_weight_term,
                query_bias_term,
                key_weight_term,
                value_weight_term,
                value_bias_term,
                out_grad,
                out_bias_term,
            ),
        )

    attn_start = zero_terms(
        (
            pre_gain,
            pre_shift,
            query_weight,
            query_bias,
            key_weight,
            value_weight,
            value_bias,
            out_weight,
            out_bias,
        )
    )
    mlp_start = zero_terms((mid_gain, mid_shift, up_weight, up_bias, down_weight, down_bias))

    def full_step(row_index, carry):
        outputs_acc, inputs_acc, attn_acc, mlp_acc = carry
        saved, output_row = forward_row(row_index)
        resid_grad, mlp_terms = mlp_back(saved, row_index)
        input_row_grad, attn_terms = attn_back(saved, resid_grad)
        outputs_acc = lax.dynamic_update_index_in_dim(
            outputs_acc, output_row.astype(jnp.bfloat16), row_index, 0
        )
        inputs_acc = lax.dynamic_update_index_in_dim(
            inputs_acc, input_row_grad.astype(jnp.bfloat16), row_index, 0
        )
        return (
            outputs_acc,
            inputs_acc,
            add_terms(attn_acc, attn_terms),
            add_terms(mlp_acc, mlp_terms),
        )

    start = (
        jnp.zeros(hidden_in.shape, jnp.bfloat16),
        jnp.zeros(hidden_in.shape, jnp.bfloat16),
        attn_start,
        mlp_start,
    )
    outputs_acc, inputs_acc, attn_acc, mlp_acc = lax.fori_loop(0, row_count, full_step, start)
    (
        pre_gain_sum,
        pre_shift_sum,
        query_weight_sum,
        query_bias_sum,
        key_weight_sum,
        value_weight_sum,
        value_bias_sum,
        out_weight_sum,
        out_bias_sum,
    ) = attn_acc
    mid_gain_sum, mid_shift_sum, up_weight_sum, up_bias_sum, down_weight_sum, down_bias_sum = (
        mlp_acc
    )
    (
        pre_gain_sum,
        pre_shift_sum,
        query_weight_sum,
        query_bias_sum,
        key_weight_sum,
        value_weight_sum,
        value_bias_sum,
        out_weight_sum,
        out_bias_sum,
        mid_gain_sum,
        mid_shift_sum,
        up_weight_sum,
        up_bias_sum,
        down_weight_sum,
        down_bias_sum,
    ) = lax.psum(
        (
            pre_gain_sum,
            pre_shift_sum,
            query_weight_sum,
            query_bias_sum,
            key_weight_sum,
            value_weight_sum,
            value_bias_sum,
            out_weight_sum,
            out_bias_sum,
            mid_gain_sum,
            mid_shift_sum,
            up_weight_sum,
            up_bias_sum,
            down_weight_sum,
            down_bias_sum,
        ),
        "dp",
    )
    return (
        outputs_acc,
        inputs_acc,
        pre_gain_sum,
        pre_shift_sum,
        query_weight_sum,
        query_bias_sum,
        key_weight_sum,
        value_weight_sum,
        value_bias_sum,
        out_weight_sum,
        out_bias_sum,
        mid_gain_sum,
        mid_shift_sum,
        up_weight_sum,
        up_bias_sum,
        down_weight_sum,
        down_bias_sum,
    )


def solution(mesh):
    placed = (
        P("dp", None, None),
        P("dp", None),
        P("dp", None, None),
        P(),
        P(),
        P(None, "tensor"),
        P("tensor"),
        P(None, "tensor"),
        P(None, "tensor"),
        P("tensor"),
        P("tensor", None),
        P(),
        P(),
        P(),
        P(None, "tensor"),
        P("tensor"),
        P("tensor", None),
        P(),
    )
    return jax.shard_map(
        shards,
        mesh=mesh,
        in_specs=placed,
        out_specs=(
            P("dp", None, None),
            P("dp", None, None),
            P(),
            P(),
            P(None, "tensor"),
            P("tensor"),
            P(None, "tensor"),
            P(None, "tensor"),
            P("tensor"),
            P("tensor", None),
            P(),
            P(),
            P(),
            P(None, "tensor"),
            P("tensor"),
            P("tensor", None),
            P(),
        ),
        check_vma=False,
    )
```

profile of v0, /device:TPU:1, one launch (start us, length us, event | category | flops | bytes accessed | tf_op | source)
XLA Modules:
  0.0 1176.5 jit_solution(9495978037734269897)
XLA Ops:
  8.2 405.0 %while.48 = (s32[]{:T(128)}, bf16[2,192,1152]{2,1,0:T(8,128)(2,1)}, bf16[2,192,1152]{2,1,0:T(8,128)(2,1)}, f32[1152]{0:T(1024)S(1)}, f32[1152]{0:T(1024)S(1)}, /...) while((s32[]{:T(128)}, bf16[2,192,1152]{2,1,0:T(8,128)(2,1)}, ...), condition=%wide.region_27.28_spmd.clone, body=%wide.region_0.27_spmd.clone.sunk | while | flops 9089845248 | bytes 310861312 | solution.py:277
  21.2 46.5 %all-reduce.12.cloned.1.call-done = f32[192,1152]{1,0:T(8,128)} async-done(((f32[192,1152]{1,0:T(8,128)}), f32[192,1152]{1,0:T(8,128)}) %all-reduce.12.cloned.1.call-update) | async-done | bytes 884752 | tf_op jit(solution)/shard_map/while/body/eval_jaxpr/psum | solution.py:112
  69.4 4.3 convolution_add_fusion.20
  73.8 2.4 fusion.211
  81.5 7.5 convolution_add_fusion.28
  89.0 5.7 convolution_add_fusion.27
  94.8 31.0 %all-reduce.14.cloned.1.call-done = f32[192,1152]{1,0:T(8,128)} async-done(((f32[192,1152]{1,0:T(8,128)}), f32[192,1152]{1,0:T(8,128)}) %all-reduce.14.cloned.1.call-update) | async-done | bytes 884752 | tf_op jit(solution)/shard_map/while/body/eval_jaxpr/psum | solution.py:158
  151.4 54.8 %all-reduce.16.cloned.1.call-done = (f32[192,1152]{1,0:T(8,128)}, f32[192,1152]{1,0:T(8,128)}) async-done(((f32[192,1152]{1,0:T(8,128)}, f32[192,1152]{1,0:T(8,128)}), (f32[192,1152]{1,0:T(8,128)}, f32[192,1152]{1,0:T(8,128)})) %all-reduce.16.cloned.1.call-update) | async-done | bytes 1769488 | tf_op jit(solution)/shard_map/while/body/eval_jaxpr/psum | solution.py:117
  208.4 2.5 fusion.218
  224.8 44.2 %all-reduce.12.cloned.1.call-done = f32[192,1152]{1,0:T(8,128)} async-done(((f32[192,1152]{1,0:T(8,128)}), f32[192,1152]{1,0:T(8,128)}) %all-reduce.12.cloned.1.call-update) | async-done | bytes 884752 | tf_op jit(solution)/shard_map/while/body/eval_jaxpr/psum | solution.py:112
  270.7 4.3 convolution_add_fusion.20
  282.9 10.5 convolution_add_fusion.28
  293.3 9.5 convolution_add_fusion.27
  302.9 24.3 %all-reduce.14.cloned.1.call-done = f32[192,1152]{1,0:T(8,128)} async-done(((f32[192,1152]{1,0:T(8,128)}), f32[192,1152]{1,0:T(8,128)}) %all-reduce.14.cloned.1.call-update) | async-done | bytes 884752 | tf_op jit(solution)/shard_map/while/body/eval_jaxpr/psum | solution.py:158
  343.8 4.1 convolution_add_fusion.25
  350.4 4.0 convolution_add_fusion.23
  354.4 3.9 convolution_add_fusion.26
  358.3 49.3 %all-reduce.16.cloned.1.call-done = (f32[192,1152]{1,0:T(8,128)}, f32[192,1152]{1,0:T(8,128)}) async-done(((f32[192,1152]{1,0:T(8,128)}, f32[192,1152]{1,0:T(8,128)}), (f32[192,1152]{1,0:T(8,128)}, f32[192,1152]{1,0:T(8,128)})) %all-reduce.16.cloned.1.call-update) | async-done | bytes 1769488 | tf_op jit(solution)/shard_map/while/body/eval_jaxpr/psum | solution.py:117
  409.8 2.5 fusion.218
  413.8 322.7 %all-reduce.1 = (f32[1152]{0:T(1024)}, f32[1152]{0:T(1024)}, f32[576]{0:T(1024)}, f32[576]{0:T(1024)}, f32[1152]{0:T(1024)}, /*index=5*/f32[1152]{0:T(1024)}, f32[1152]{0:T(1024)}, f32[2152]{0:T(1024)}, f32[1152]{0:T(1024)}) all-reduce(f32[1152]{0:T(1024)S(1)} %get-tuple-element.849, ...), channel_id=1, replica_groups=mesh['dp'=64,'tensor'=2] {'dp'}, use_global_device_ids=true, to_apply=%region_28.29 | all-reduce | flops 10216 | bytes 81728 | tf_op jit(solution)/shard_map/psum | solution.py:308
  736.4 409.1 %all-reduce.10.cloned.1.call-done = (f32[1152,576]{0,1:T(8,128)}, f32[1152,576]{0,1:T(8,128)}, f32[1152,576]{0,1:T(8,128)}, f32[576,1152]{1,0:T(8,128)}, f32[1152,2152]{0,1:T(8,128)}, /*index=5*/f32[2152,1152]{1,0:T(8,128)}) async-done(((f32[1152,576]{0,1:T(8,128)}, f32[1152,576]{0,1:T(8,128)}, f32[1152,576]{0,1:T(8,128)}, f32[576,1152]{1,0:T(8,128)}, f32[1152,2152]{0,1:T(8,128)}, ...) | async-done | bytes 30449680 | tf_op jit(solution)/shard_map/psum | solution.py:308
  1145.5 3.6 copy.141
  1156.0 9.1 copy.145
  1165.1 3.9 copy.146
  (339 shorter events, 99.7 us)
Async XLA Ops:
  8.2 59.5 %all-reduce.12.cloned.1.call-start = ((), (), s32[]{:S(2)}) async-start(), calls=%async_computation.1 | async-start | bytes 1769472 | tf_op jit(solution)/shard_map/while/body/eval_jaxpr/psum | solution.py:112
  19.6 48.1 %copy-start.37 = (f32[1152]{0:T(1024)S(1)}, f32[1152]{0:T(1024)}, u32[]{:S(2)}) copy-start(f32[1152]{0:T(1024)} %get-tuple-element.1491) | copy-start | bytes 13828 | tf_op jit(solution)/shard_map/while
  21.1 48.2 %copy-start.31 = (f32[1152]{0:T(1024)S(1)}, f32[1152]{0:T(1024)}, u32[]{:S(2)}) copy-start(f32[1152]{0:T(1024)} %get-tuple-element.1492) | copy-start | bytes 13828 | tf_op jit(solution)/shard_map/while
  21.1 48.2 %copy-start.36 = (f32[1152]{0:T(1024)S(1)}, f32[1152]{0:T(1024)}, u32[]{:S(2)}) copy-start(f32[1152]{0:T(1024)} %get-tuple-element.1493) | copy-start | bytes 13828 | tf_op jit(solution)/shard_map/while
  21.1 48.2 %copy-start.41 = (f32[2152]{0:T(1024)S(1)}, f32[2152]{0:T(1024)}, u32[]{:S(2)}) copy-start(f32[2152]{0:T(1024)} %get-tuple-element.1495) | copy-start | bytes 25828 | tf_op jit(solution)/shard_map/while
  21.1 104.6 %all-reduce.14.cloned.1.call-start = ((), (), s32[]{:S(2)}) async-start(), calls=%async_computation.2 | async-start | bytes 1769472 | tf_op jit(solution)/shard_map/while/body/eval_jaxpr/psum | solution.py:158
  81.4 124.8 %all-reduce.16.cloned.1.call-start = ((), (), s32[]{:S(2)}) async-start(), calls=%async_computation.3 | async-start | bytes 3538944 | tf_op jit(solution)/shard_map/while/body/eval_jaxpr/psum | solution.py:117
  81.5 7.5 copy-start.29
  149.3 59.1 %copy-start.39 = (bf16[2,192,1152]{2,1,0:T(8,128)(2,1)S(1)}, bf16[2,192,1152]{2,1,0:T(8,128)(2,1)}, u32[]{:S(2)}) copy-start(bf16[2,192,1152]{2,1,0:T(8,128)(2,1)} %get-tuple-element.1427) | copy-start | bytes 2654212 | tf_op jit(solution)/shard_map/while
  151.4 57.0 %copy-start.38 = (f32[1152]{0:T(1024)S(1)}, f32[1152]{0:T(1024)}, u32[]{:S(2)}) copy-start(f32[1152]{0:T(1024)} %get-tuple-element.1497) | copy-start | bytes 13828 | tf_op jit(solution)/shard_map/while
  211.9 57.2 %all-reduce.12.cloned.1.call-start = ((), (), s32[]{:S(2)}) async-start(), calls=%async_computation.1 | async-start | bytes 1769472 | tf_op jit(solution)/shard_map/while/body/eval_jaxpr/psum | solution.py:112
  223.2 45.9 %copy-start.37 = (f32[1152]{0:T(1024)S(1)}, f32[1152]{0:T(1024)}, u32[]{:S(2)}) copy-start(f32[1152]{0:T(1024)} %get-tuple-element.1491) | copy-start | bytes 13828 | tf_op jit(solution)/shard_map/while
  224.7 46.0 %copy-start.31 = (f32[1152]{0:T(1024)S(1)}, f32[1152]{0:T(1024)}, u32[]{:S(2)}) copy-start(f32[1152]{0:T(1024)} %get-tuple-element.1492) | copy-start | bytes 13828 | tf_op jit(solution)/shard_map/while
  224.7 46.0 %copy-start.36 = (f32[1152]{0:T(1024)S(1)}, f32[1152]{0:T(1024)}, u32[]{:S(2)}) copy-start(f32[1152]{0:T(1024)} %get-tuple-element.1493) | copy-start | bytes 13828 | tf_op jit(solution)/shard_map/while
  224.7 46.0 %copy-start.41 = (f32[2152]{0:T(1024)S(1)}, f32[2152]{0:T(1024)}, u32[]{:S(2)}) copy-start(f32[2152]{0:T(1024)} %get-tuple-element.1495) | copy-start | bytes 25828 | tf_op jit(solution)/shard_map/while
  224.8 102.4 %all-reduce.14.cloned.1.call-start = ((), (), s32[]{:S(2)}) async-start(), calls=%async_computation.2 | async-start | bytes 1769472 | tf_op jit(solution)/shard_map/while/body/eval_jaxpr/psum | solution.py:158
  282.8 124.8 %all-reduce.16.cloned.1.call-start = ((), (), s32[]{:S(2)}) async-start(), calls=%async_computation.3 | async-start | bytes 3538944 | tf_op jit(solution)/shard_map/while/body/eval_jaxpr/psum | solution.py:117
  282.8 10.5 copy-start.29
  354.4 55.3 %copy-start.39 = (bf16[2,192,1152]{2,1,0:T(8,128)(2,1)S(1)}, bf16[2,192,1152]{2,1,0:T(8,128)(2,1)}, u32[]{:S(2)}) copy-start(bf16[2,192,1152]{2,1,0:T(8,128)(2,1)} %get-tuple-element.1427) | copy-start | bytes 2654212 | tf_op jit(solution)/shard_map/while
  358.3 51.5 %copy-start.38 = (f32[1152]{0:T(1024)S(1)}, f32[1152]{0:T(1024)}, u32[]{:S(2)}) copy-start(f32[1152]{0:T(1024)} %get-tuple-element.1497) | copy-start | bytes 13828 | tf_op jit(solution)/shard_map/while
  413.2 732.3 %all-reduce.10.cloned.1.call-start = ((), (), s32[]{:S(2)}) async-start(), calls=%async_computation | async-start | bytes 60899328 | tf_op jit(solution)/shard_map/psum | solution.py:308
  1154.5 10.6 slice-start
  1156.0 9.1 slice-start.1
  1156.0 9.1 slice-start.2
  (79 other events, 169.9 us)
Sparse Core Ops, SparseCore 0:
  21.2 46.4 all-reduce.11
  81.6 44.1 all-reduce.13
  142.5 63.6 all-reduce.15
  224.8 44.1 all-reduce.11
  282.9 44.1 all-reduce.13
  343.9 63.6 all-reduce.15
Sparse Core Ops, SparseCore 1:
  417.8 727.6 all-reduce.9
where the time goes:
time: 1180 us
  waiting for transfers between devices  660 us (56%)
  blocking collectives  323 us (27%)
  matrix products  108 us (9%)
  local copies, waits for them, and re-layouts  44.6 us (4%)
  other arithmetic  24 us (2%)
  between operations  15.6 us (1%)
    psum x1, waiting for transfers between devices, shards(): lax.psum((pre_gain_sum, pre_shift_sum, query_weight_sum, query_bias_sum,...  409 us
    psum x1, blocking collectives, shards(): lax.psum((pre_gain_sum, pre_shift_sum, query_weight_sum, query_bias_sum,...  323 us
    psum x2, waiting for transfers between devices, forward_row(): lax.psum(product(activ, down_weight), 'tensor')  104 us
    psum x2, waiting for transfers between devices, forward_row(): branch = lax.psum(product(attended, out_weight), 'tensor') + out_bias  90.7 us
    psum x2, waiting for transfers between devices, mlp_back(): mid_grad = lax.psum(against(pre_grad, up_weight), 'tensor')  55.3 us
    dot_general x12, matrix products, inner_rows(): lax.dot_general(left, right, (((0,), (0,)), ((), ())), preferred_element_...  53.6 us
    dot_general x12, matrix products, product(): return jnp.dot(left, right, preferred_element_type=jnp.float32)  26.6 us
  transfers between devices with their start and end apart: 7, of which 7 were waited for; matrix products, arithmetic and copies ran while one was open for 5% of the time, Pallas kernels for 0%

commit v1 on v0

v1 whole, which is shorter than its diff:
```python
import jax
import jax.numpy as jnp
from jax import lax
from jax.sharding import PartitionSpec as P

HEAD = 72
norm_epsilon = 1e-06


def partner_pairs(move):
    pairs = []
    for place in range(64):
        z_hi, x, y, core = place >> 5, (place >> 3) & 3, (place >> 1) & 3, place & 1
        z_hi, x, y, core = move(z_hi, x, y, core)
        pairs.append((place, ((z_hi * 4 + x) * 4 + y) * 2 + core))
    return pairs


PAIRS = {
    "core": partner_pairs(lambda z, x, y, c: (z, x, y, 1 - c)),
    "xa": partner_pairs(lambda z, x, y, c: (z, x ^ 1, y, c)),
    "xb": partner_pairs(lambda z, x, y, c: (z, x ^ 3, y, c)),
    "ya": partner_pairs(lambda z, x, y, c: (z, x, y ^ 1, c)),
    "yb": partner_pairs(lambda z, x, y, c: (z, x, y ^ 3, c)),
    "z": partner_pairs(lambda z, x, y, c: (1 - z, x, y, c)),
}
ORDERS = (
    ("xa", "ya", "xb", "yb"),
    ("ya", "xb", "yb", "xa"),
    ("xb", "yb", "xa", "ya"),
    ("yb", "xa", "ya", "xb"),
)


def sides():
    place = lax.axis_index("dp")
    x = (place >> 3) & 3
    y = (place >> 1) & 3
    return {
        "core": place & 1,
        "xa": (x ^ (x >> 1)) & 1,
        "xb": x >> 1,
        "ya": (y ^ (y >> 1)) & 1,
        "yb": y >> 1,
    }


def swap(values, pair):
    return lax.ppermute(values, "dp", PAIRS[pair])


def swap_tensor(values):
    return lax.ppermute(values, "tensor", [(0, 1), (1, 0)])


def half_of(values, side):
    count = values.shape[0] // 2
    return lax.dynamic_slice_in_dim(values, side * count, count, 0)


def scatter_step(values, pair, side):
    received = swap(half_of(values, 1 - side[pair]), pair)
    return half_of(values, side[pair]) + received


def joined(own, received, side):
    return jnp.where(
        side == 0,
        jnp.concatenate([own, received], 0),
        jnp.concatenate([received, own], 0),
    )


def gather_step(values, pair, side):
    return joined(values, swap(values, pair), side[pair])


def stream_sum(values, order, side):
    for pair in order[:3]:
        values = scatter_step(values, pair, side)
    values = values + swap(values, order[3])
    values = values + swap(values, "z")
    for pair in order[2::-1]:
        values = gather_step(values, pair, side)
    return values


def core_streams(send, keep, splits, first_order, side):
    rows, columns = keep.shape
    own = keep + swap(send, "core")
    parts = []
    begin = 0
    for number, block in enumerate(splits):
        part = own[begin : begin + 8 * block].reshape(8, block, columns)
        begin += 8 * block
        part = stream_sum(part, ORDERS[(first_order + number) % 4], side)
        parts.append(part.reshape(8 * block, columns))
    half = jnp.concatenate(parts, 0) if len(parts) > 1 else parts[0]
    return joined(half, swap(half, "core"), side["core"])


def normalized(values):
    center = values - jnp.mean(values, axis=-1, keepdims=True)
    spread = jnp.mean(center * center, axis=-1, keepdims=True)
    factor = lax.rsqrt(spread + norm_epsilon)
    return center * factor, factor


def norm_back(grad, normal, factor, gain):
    scaled = grad * gain
    mean_scaled = jnp.mean(scaled, axis=-1, keepdims=True)
    mean_normal = jnp.mean(scaled * normal, axis=-1, keepdims=True)
    return factor * (scaled - mean_scaled - normal * mean_normal)


def gelu_tanh(values):
    return jax.nn.gelu(values, approximate=True)


def product(left, right):
    return jnp.dot(left, right, preferred_element_type=jnp.float32)


def inner_rows(left, right):
    return lax.dot_general(
        left, right, (((0,), (0,)), ((), ())), preferred_element_type=jnp.float32
    )


def against(left, right):
    return lax.dot_general(
        left, right, (((1,), (1,)), ((), ())), preferred_element_type=jnp.float32
    )


def segments(layout, length):
    bounds = jnp.cumsum(layout[:, :-1], axis=1)
    places = jnp.arange(length, dtype=jnp.int32)
    inside = (places[None, :, None] >= bounds[:, None, :]).astype(jnp.int32)
    return jnp.sum(inside, axis=2)


def column_half(values, side):
    count = values.shape[1] // 2
    return jnp.where(side == 0, values[:, :count], values[:, count:])


def shards(
    hidden_in,
    row_layout,
    cotangent,
    pre_gain,
    pre_shift,
    query_weight,
    query_bias,
    key_weight,
    value_weight,
    value_bias,
    out_weight,
    out_bias,
    mid_gain,
    mid_shift,
    up_weight,
    up_bias,
    down_weight,
    down_bias,
):
    rows, length, width = hidden_in.shape
    tokens = rows * length
    heads_here = query_weight.shape[1] // HEAD
    hidden = up_weight.shape[1]
    scale_factor = HEAD ** (-0.5)
    head_shape = (rows, length, heads_here, HEAD)
    side = sides()
    core = side["core"]

    inputs = hidden_in.reshape(tokens, width).astype(jnp.float32)
    segment = segments(row_layout, length)
    same_picture = (segment[:, :, None] == segment[:, None, :])[:, None]
    pre_normal, pre_factor = normalized(inputs)
    normed = (pre_normal * pre_gain + pre_shift).astype(jnp.bfloat16)
    queries = (product(normed, query_weight) + query_bias).astype(jnp.bfloat16)
    keys = product(normed, key_weight).astype(jnp.bfloat16)
    values = (product(normed, value_weight) + value_bias).astype(jnp.bfloat16)
    queries = queries.reshape(head_shape)
    keys = keys.reshape(head_shape)
    values = values.reshape(head_shape)
    raw = jnp.einsum("bqhd,bkhd->bhqk", queries, keys, preferred_element_type=jnp.float32)
    scores = jnp.where(same_picture, raw * scale_factor, -1000000000.0)
    maximum = jnp.max(scores, axis=-1, keepdims=True)
    exponent = jnp.exp(scores - maximum)
    probs = exponent / jnp.sum(exponent, axis=-1, keepdims=True)
    probs_low = probs.astype(jnp.bfloat16)
    attended = jnp.einsum("bhqk,bkhd->bqhd", probs_low, values, preferred_element_type=jnp.float32)
    attended = attended.astype(jnp.bfloat16).reshape(tokens, heads_here * HEAD)
    branch = product(attended, out_weight)
    branch = branch + swap_tensor(branch)
    resid = inputs + (branch + out_bias)
    mid_normal, mid_factor = normalized(resid)
    middle = (mid_normal * mid_gain + mid_shift).astype(jnp.bfloat16)
    pre_act = product(middle, up_weight) + up_bias
    activ_float, gelu_pull = jax.vjp(gelu_tanh, pre_act)
    activ = activ_float.astype(jnp.bfloat16)

    cot_low = cotangent.reshape(tokens, width)
    cot_float = cot_low.astype(jnp.float32)
    down_bias_grad = jnp.sum(cot_float, axis=0)
    padded = -(-hidden // 128) * 128
    activ_wide = jnp.pad(activ, ((0, 0), (0, padded - hidden)))
    down_grad = core_streams(
        inner_rows(column_half(activ_wide, 1 - core), cot_low),
        inner_rows(column_half(activ_wide, core), cot_low),
        (72, 64),
        0,
        side,
    )[:hidden]
    act_grad = against(cot_low, down_weight)
    pre_grad = gelu_pull(act_grad)[0].astype(jnp.bfloat16)
    up_bias_grad = jnp.sum(pre_grad.astype(jnp.float32), axis=0)
    up_grad = core_streams(
        inner_rows(column_half(middle, 1 - core), pre_grad),
        inner_rows(column_half(middle, core), pre_grad),
        (40, 32),
        2,
        side,
    )
    mid_part = against(pre_grad, up_weight)
    mid_grad = mid_part + swap_tensor(mid_part)
    output_part = product(activ, down_weight)
    output = resid + (output_part + swap_tensor(output_part)) + down_bias
    mid_gain_grad = jnp.sum(mid_grad * mid_normal, axis=0)
    mid_shift_grad = jnp.sum(mid_grad, axis=0)
    resid_grad = cot_float + norm_back(mid_grad, mid_normal, mid_factor, mid_gain)

    branch_grad = resid_grad.astype(jnp.bfloat16)
    out_bias_grad = jnp.sum(branch_grad.astype(jnp.float32), axis=0)
    attended_wide = jnp.pad(attended, ((0, 0), (0, 640 - heads_here * HEAD)))
    out_grad = core_streams(
        inner_rows(column_half(attended_wide, 1 - core), branch_grad),
        inner_rows(column_half(attended_wide, core), branch_grad),
        (40,),
        3,
        side,
    )[: heads_here * HEAD]
    attended_grad = against(branch_grad, out_weight).astype(jnp.bfloat16).reshape(head_shape)
    value_grad = jnp.einsum(
        "bhqk,bqhd->bkhd", probs_low, attended_grad, preferred_element_type=jnp.float32
    ).astype(jnp.bfloat16)
    prob_grad = jnp.einsum(
        "bqhd,bkhd->bhqk", attended_grad, values, preferred_element_type=jnp.float32
    )
    score_grad = (
        probs * (prob_grad - jnp.sum(prob_grad * probs, axis=-1, keepdims=True))
    ).astype(jnp.bfloat16)
    query_grad = jnp.einsum("bhqk,bkhd->bqhd", score_grad, keys, preferred_element_type=jnp.float32)
    key_grad = jnp.einsum("bhqk,bqhd->bkhd", score_grad, queries, preferred_element_type=jnp.float32)
    query_grad = (query_grad * scale_factor).astype(jnp.bfloat16).reshape(tokens, -1)
    key_grad = (key_grad * scale_factor).astype(jnp.bfloat16).reshape(tokens, -1)
    value_grad = value_grad.reshape(tokens, -1)
    normed_send = column_half(normed, 1 - core)
    normed_keep = column_half(normed, core)
    weight_grads = [
        core_streams(
            inner_rows(normed_send, grad),
            inner_rows(normed_keep, grad),
            (72,),
            number,
            side,
        )
        for number, grad in enumerate((query_grad, key_grad, value_grad))
    ]
    query_bias_grad = jnp.sum(query_grad.astype(jnp.float32), axis=0)
    value_bias_grad = jnp.sum(value_grad.astype(jnp.float32), axis=0)
    normed_part = (
        against(query_grad, query_weight)
        + against(key_grad, key_weight)
        + against(value_grad, value_weight)
    )
    normed_grad = normed_part + swap_tensor(normed_part)
    pre_gain_grad = jnp.sum(normed_grad * pre_normal, axis=0)
    pre_shift_grad = jnp.sum(normed_grad, axis=0)
    input_grad = resid_grad + norm_back(normed_grad, pre_normal, pre_factor, pre_gain)

    small = jnp.concatenate(
        [
            pre_gain_grad,
            pre_shift_grad,
            out_bias_grad,
            mid_gain_grad,
            mid_shift_grad,
            down_bias_grad,
            query_bias_grad,
            value_bias_grad,
            up_bias_grad,
            jnp.zeros((2 * width - hidden,), jnp.float32),
        ]
    ).reshape(9, width)
    for pair in ("core", "xa", "ya", "xb", "yb", "z"):
        small = small + swap(small, pair)
    heads_wide = heads_here * HEAD
    return (
        output.astype(jnp.bfloat16).reshape(hidden_in.shape),
        input_grad.astype(jnp.bfloat16).reshape(hidden_in.shape),
        small[0],
        small[1],
        weight_grads[0],
        small[6, :heads_wide],
        weight_grads[1],
        weight_grads[2],
        small[6, heads_wide:],
        out_grad,
        small[2],
        small[3],
        small[4],
        up_grad,
        small[7:].reshape(-1)[:hidden],
        down_grad,
        small[5],
    )


def solution(mesh):
    placed = (
        P("dp", None, None),
        P("dp", None),
        P("dp", None, None),
        P(),
        P(),
        P(None, "tensor"),
        P("tensor"),
        P(None, "tensor"),
        P(None, "tensor"),
        P("tensor"),
        P("tensor", None),
        P(),
        P(),
        P(),
        P(None, "tensor"),
        P("tensor"),
        P("tensor", None),
        P(),
    )
    return jax.shard_map(
        shards,
        mesh=mesh,
        in_specs=placed,
        out_specs=(
            P("dp", None, None),
            P("dp", None, None),
            P(),
            P(),
            P(None, "tensor"),
            P("tensor"),
            P(None, "tensor"),
            P(None, "tensor"),
            P("tensor"),
            P("tensor", None),
            P(),
            P(),
            P(),
            P(None, "tensor"),
            P("tensor"),
            P("tensor", None),
            P(),
        ),
        check_vma=False,
    )
```

time: 1180 us -> 598 us (0.51)
  waiting for transfers between devices: 660 us -> 267 us
  blocking collectives: 323 us -> 0 us
  starting transfers between devices: 0.22 us -> 124 us
  other arithmetic: 24 us -> 81.4 us
  matrix products: 108 us -> 71.8 us
  between operations: 15.6 us -> 2.81 us
    psum x7 -> x0, waiting for transfers between devices: 659 us -> none  [the longest x1 409 us: shards(): lax.psum((pre_gain_sum, pre_shift_sum, query_weight_sum, query_bias_sum,...]
    psum x1 -> x0, blocking collectives: 323 us -> none  [shards(): lax.psum((pre_gain_sum, pre_shift_sum, query_weight_sum, query_bias_sum,...]
    ppermute x0 -> x86, waiting for transfers between devices: none -> 267 us  [the longest x82 156 us: swap(): return lax.ppermute(values, 'dp', PAIRS[pair])]
    ppermute x0 -> x86, starting transfers between devices: none -> 124 us  [the longest x82 119 us: swap(): return lax.ppermute(values, 'dp', PAIRS[pair])]
    select_n x0 -> x31, other arithmetic: none -> 47.3 us  [the longest x30 44.9 us: joined(): jnp.where(side == 0, jnp.concatenate([own, received], 0), jnp.concatenate...]
    dot_general x12, matrix products: 53.6 us -> 32.8 us  [inner_rows(): lax.dot_general(left, right, (((0,), (0,)), ((), ())), preferred_element_...]
    while x180 -> x0, local copies, waits for them, and re-layouts: 14.8 us -> none
    dot_general x12 -> x6, matrix products: 26.6 us -> 18.9 us  [product(): return jnp.dot(left, right, preferred_element_type=jnp.float32)]
  transfers between devices with their start and end apart: 7 -> 86, of which waited for: 7 -> 38; matrix products, arithmetic and copies ran while one was open for 5% -> 21% of each run, Pallas kernels for 0% -> 0%
where the time goes in v1:
time: 598 us; the launch traced here: 592 us
  waiting for transfers between devices  267 us (45%)
  starting transfers between devices  124 us (21%)
  other arithmetic  81.4 us (14%)
  matrix products  71.8 us (12%)
  local copies, waits for them, and re-layouts  44 us (7%)
    ppermute x82, waiting for transfers between devices, swap(): return lax.ppermute(values, 'dp', PAIRS[pair])  156 us
    ppermute x82, starting transfers between devices, swap(): return lax.ppermute(values, 'dp', PAIRS[pair])  119 us
    ppermute x4, waiting for transfers between devices, swap_tensor(): return lax.ppermute(values, 'tensor', [(0, 1), (1, 0)])  111 us
    select_n x30, other arithmetic, joined(): jnp.where(side == 0, jnp.concatenate([own, received], 0), jnp.concatenate...  44.9 us
    dot_general x12, matrix products, inner_rows(): lax.dot_general(left, right, (((0,), (0,)), ((), ())), preferred_element_...  32.8 us
    unnamed x186, local copies, waits for them, and re-layouts  28.8 us
    dot_general x6, matrix products, product(): return jnp.dot(left, right, preferred_element_type=jnp.float32)  18.9 us
    dot_general x6, matrix products, against(): lax.dot_general(left, right, (((1,), (1,)), ((), ())), preferred_element_...  13.7 us
  transfers between devices with their start and end apart: 86, of which 38 were waited for; matrix products, arithmetic and copies ran while one was open for 21% of the time, Pallas kernels for 0%

profile of v1, /device:TPU:1, one launch (start us, length us, event | category | flops | bytes accessed | tf_op | source)
XLA Modules:
  0.0 591.5 jit_solution(6370207861405753183)
XLA Ops:
  24.0 5.1 fusion.84
  29.2 33.2 %collective-permute-done = f32[384,1152]{1,0:T(8,128)S(1)} collective-permute-done((f32[384,1152]{1,0:T(8,128)S(1)}, f32[384,1152]{1,0:T(8,128)S(1)}, u32[]{:S(2)}, u32[]{:S(2)}) %collective-permute-start) | collective-permute-done | bytes 1769504 | tf_op jit(solution)/shard_map/ppermute | solution.py:53
  64.3 7.1 %convert_reduce_fusion = (f32[2152]{0:T(1024)}, bf16[384,2152]{0,1:T(8,128)(2,1)S(1)}, bf16[384,2152]{0,1:T(8,128)(2,1)S(1)}) fusion(f32[384,2152]{0,1:T(8,128)S(1)} %fusion.84, f32[2152]{0:T(1024)S(1)} %copy-done.84, bf16[384,1152]{1,0:T(8,128)(2,1)S(1)} %add_convert_fusion.1, bf16[1152,2152]{0,1:T(8,128)(2,1)S(1)} %bitcast.130), kind=kOutput, calls=%fused_computation.21 | convolution fusion | flops 1924608896 | bytes 12471104 | tf_op jit(solution)/shard_map/dot_general | solution.py:121
  89.3 25.1 %collective-permute-done.2 = f32[384,1152]{1,0:T(8,128)} collective-permute-done((f32[384,1152]{1,0:T(8,128)}, f32[384,1152]{1,0:T(8,128)}, u32[]{:S(2)}, u32[]{:S(2)}) %collective-permute-start.2) | collective-permute-done | bytes 1769504 | tf_op jit(solution)/shard_map/ppermute | solution.py:53
  117.9 34.4 %collective-permute-done.1 = f32[384,1152]{1,0:T(8,128)} collective-permute-done((f32[384,1152]{1,0:T(8,128)}, f32[384,1152]{1,0:T(8,128)}, u32[]{:S(2)}, u32[]{:S(2)}) %collective-permute-start.1) | collective-permute-done | bytes 1769504 | tf_op jit(solution)/shard_map/ppermute | solution.py:53
  152.3 5.1 convert_reduce_fusion.3
  205.7 18.2 %collective-permute-done.3 = f32[384,1152]{1,0:T(8,128)} collective-permute-done((f32[384,1152]{1,0:T(8,128)}, f32[384,1152]{1,0:T(8,128)}, u32[]{:S(2)}, u32[]{:S(2)}) %collective-permute-start.3) | collective-permute-done | bytes 1769504 | tf_op jit(solution)/shard_map/ppermute | solution.py:53
  236.7 12.5 %collective-permute-done.11 = f32[4,72,576]{2,1,0:T(8,128)S(1)} collective-permute-done((f32[4,72,576]{2,1,0:T(8,128)}, f32[4,72,576]{2,1,0:T(8,128)S(1)}, u32[]{:S(2)}, u32[]{:S(2)}) %collective-permute-start.11) | collective-permute-done | bytes 663584 | tf_op jit(solution)/shard_map/ppermute | solution.py:49
  261.9 5.2 collective-permute-done.12
  268.6 5.3 collective-permute-done.33
  324.8 9.3 %collective-permute-done.59 = f32[4,32,2152]{2,1,0:T(8,128)S(1)} collective-permute-done((f32[4,32,2152]{2,1,0:T(8,128)S(1)}, f32[4,32,2152]{2,1,0:T(8,128)S(1)}, u32[]{:S(2)}, u32[]{:S(2)}) %collective-permute-start.59) | collective-permute-done | bytes 1101856 | tf_op jit(solution)/shard_map/ppermute | solution.py:49
  334.3 8.0 %collective-permute-done.77 = f32[4,64,1152]{2,1,0:T(8,128)S(1)} collective-permute-done((f32[4,64,1152]{2,1,0:T(8,128)S(1)}, f32[4,64,1152]{2,1,0:T(8,128)S(1)}, u32[]{:S(2)}, u32[]{:S(2)}) %collective-permute-start.77) | collective-permute-done | bytes 1179680 | tf_op jit(solution)/shard_map/ppermute | solution.py:49
  355.7 9.2 %collective-permute-done.60 = f32[2,32,2152]{2,1,0:T(8,128)S(1)} collective-permute-done((f32[2,32,2152]{2,1,0:T(8,128)S(1)}, f32[2,32,2152]{2,1,0:T(8,128)S(1)}, u32[]{:S(2)}, u32[]{:S(2)}) %collective-permute-start.60) | collective-permute-done | bytes 550944 | tf_op jit(solution)/shard_map/ppermute | solution.py:49
  367.1 8.0 %collective-permute-done.70 = f32[2,72,1152]{2,1,0:T(8,128)S(1)} collective-permute-done((f32[2,72,1152]{2,1,0:T(8,128)S(1)}, f32[2,72,1152]{2,1,0:T(8,128)S(1)}, u32[]{:S(2)}, u32[]{:S(2)}) %collective-permute-start.70) | collective-permute-done | bytes 663584 | tf_op jit(solution)/shard_map/ppermute | solution.py:49
  389.8 5.3 collective-permute-done.80
  420.2 6.2 %collective-permute-done.55 = f32[1,40,2152]{2,1,0:T(8,128)S(1)} collective-permute-done((f32[1,40,2152]{2,1,0:T(8,128)S(1)}, f32[1,40,2152]{2,1,0:T(8,128)S(1)}, u32[]{:S(2)}, u32[]{:S(2)}) %collective-permute-start.55) | collective-permute-done | bytes 344352 | tf_op jit(solution)/shard_map/ppermute | solution.py:49
  437.0 5.9 collective-permute-done.75
  448.8 18.5 %collective-permute-done.84 = f32[4,64,1152]{2,1,0:T(8,128)S(1)} collective-permute-done((f32[4,64,1152]{2,1,0:T(8,128)S(1)}, f32[4,64,1152]{2,1,0:T(8,128)S(1)}, u32[]{:S(2)}, u32[]{:S(2)}) %collective-permute-start.84) | collective-permute-done | bytes 1179680 | tf_op jit(solution)/shard_map/ppermute | solution.py:49
  477.0 18.7 %collective-permute-start.85 = (f32[1088,1152]{1,0:T(8,128)}, f32[1088,1152]{1,0:T(8,128)}, u32[]{:S(2)}, u32[]{:S(2)}) collective-permute-start(f32[1088,1152]{1,0:T(8,128)} %pad_maximum_fusion.5), channel_id=1, source_target_pairs={{0,2},{2,0},{4,6},{6,4},{8,10},{10,8},{12,14},{14,12},{16,18},{18,... | collective-permute-start | bytes 15040520 | tf_op jit(solution)/shard_map/ppermute | solution.py:49
  502.2 12.3 %collective-permute-start.39 = (f32[576,576]{1,0:T(8,128)S(1)}, f32[576,576]{1,0:T(8,128)S(1)}, u32[]{:S(2)}, u32[]{:S(2)}) collective-permute-start(f32[576,576]{1,0:T(8,128)S(1)} %bitcast.144), channel_id=1, source_target_pairs={{0,2},{2,0},{4,6},{6,4},{8,10},{10,8},{12,14},{14,12},{16,18},{18,... | collective-permute-start | bytes 3981320 | tf_op jit(solution)/shard_map/ppermute | solution.py:49
  530.9 5.0 maximum_select_fusion.3
  560.3 9.2 %fusion.1 = f32[2152,1152]{1,0:T(8,128)} fusion(f32[1088,1152]{1,0:T(8,128)} %collective-permute-done.85, f32[512,1152]{1,0:T(8,128)S(1)} %bitcast.126, f32[576,1152]{1,0:T(8,128)S(1)} %bitcast.124, pred[]{:T(512)S(6)} %eq.25), kind=kLoop, calls=%fused_computation.4 | loop fusion | flops 12395520 | bytes 19943424 | tf_op jit(solution)/shard_map/jit(_where)/select_n | solution.py:67
  569.5 9.2 %maximum_select_fusion = f32[1152,2152]{1,0:T(8,128)} fusion(f32[576,2152]{1,0:T(8,128)} %collective-permute-done.67, f32[256,2152]{1,0:T(8,128)S(1)} %bitcast.128, f32[320,2152]{1,0:T(8,128)S(1)} %bitcast.122, pred[]{:T(512)S(6)} %eq.25), kind=kLoop, calls=%fused_computation.2 | loop fusion | flops 12395520 | bytes 19832832 | tf_op jit(solution)/shard_map/jit(_where)/select_n | solution.py:67
  578.7 12.3 %copy.92 = f32[1152,2152]{0,1:T(8,128)} copy(f32[1152,2152]{1,0:T(8,128)} %maximum_select_fusion) | data formatting | bytes 19832832
  (520 shorter events, 300.4 us)
Async XLA Ops:
  21.3 41.0 %collective-permute-start = (f32[384,1152]{1,0:T(8,128)S(1)}, f32[384,1152]{1,0:T(8,128)S(1)}, u32[]{:S(2)}, u32[]{:S(2)}) collective-permute-start(f32[384,1152]{1,0:T(8,128)S(1)} %fusion.82), channel_id=1, source_target_pairs={{0,1},{1,0},{2,3},{3,2},{4,5},{5,4},{6,7},{7,6},{8,9},{9,8},{10,11... | collective-permute-start | bytes 5308424 | tf_op jit(solution)/shard_map/ppermute | solution.py:53
  75.2 39.2 %collective-permute-start.2 = (f32[384,1152]{1,0:T(8,128)}, f32[384,1152]{1,0:T(8,128)}, u32[]{:S(2)}, u32[]{:S(2)}) collective-permute-start(f32[384,1152]{1,0:T(8,128)} %fusion.85), channel_id=1, source_target_pairs={{0,1},{1,0},{2,3},{3,2},{4,5},{5,4},{6,7},{7,6},{8,9},{9,8},{10,11... | collective-permute-start | bytes 5308424 | tf_op jit(solution)/shard_map/ppermute | solution.py:53
  80.2 72.2 %collective-permute-start.1 = (f32[384,1152]{1,0:T(8,128)}, f32[384,1152]{1,0:T(8,128)}, u32[]{:S(2)}, u32[]{:S(2)}) collective-permute-start(f32[384,1152]{1,0:T(8,128)} %fusion.83), channel_id=1, source_target_pairs={{0,1},{1,0},{2,3},{3,2},{4,5},{5,4},{6,7},{7,6},{8,9},{9,8},{10,11... | collective-permute-start | bytes 5308424 | tf_op jit(solution)/shard_map/ppermute | solution.py:53
  167.5 33.7 %collective-permute-start.40 = (f32[320,1152]{1,0:T(8,128)}, f32[320,1152]{1,0:T(8,128)}, u32[]{:S(2)}, u32[]{:S(2)}) collective-permute-start(f32[320,1152]{1,0:T(8,128)} %fusion.65), channel_id=1, source_target_pairs={{0,2},{2,0},{4,6},{6,4},{8,10},{10,8},{12,14},{14,12},{16,18},{18,... | collective-permute-start | bytes 4423688 | tf_op jit(solution)/shard_map/ppermute | solution.py:49
  183.5 40.4 %collective-permute-start.3 = (f32[384,1152]{1,0:T(8,128)}, f32[384,1152]{1,0:T(8,128)}, u32[]{:S(2)}, u32[]{:S(2)}) collective-permute-start(f32[384,1152]{1,0:T(8,128)} %convolution_add_fusion.3), channel_id=1, source_target_pairs={{0,1},{1,0},{2,3},{3,2},{4,5},{5,4},{6,7},{7,6},{8,9},{9,8},{10,11... | collective-permute-start | bytes 5308424 | tf_op jit(solution)/shard_map/ppermute | solution.py:53
  188.7 131.5 %collective-permute-start.68 = (f32[1088,1152]{1,0:T(8,128)}, f32[1088,1152]{1,0:T(8,128)}, u32[]{:S(2)}, u32[]{:S(2)}) collective-permute-start(f32[1088,1152]{1,0:T(8,128)} %fusion.37), channel_id=1, source_target_pairs={{0,2},{2,0},{4,6},{6,4},{8,10},{10,8},{12,14},{14,12},{16,18},{18,... | collective-permute-start | bytes 15040520 | tf_op jit(solution)/shard_map/ppermute | solution.py:49
  192.2 120.3 %collective-permute-start.50 = (f32[576,2152]{1,0:T(8,128)}, f32[576,2152]{1,0:T(8,128)}, u32[]{:S(2)}, u32[]{:S(2)}) collective-permute-start(f32[576,2152]{1,0:T(8,128)} %fusion.56), channel_id=1, source_target_pairs={{0,2},{2,0},{4,6},{6,4},{8,10},{10,8},{12,14},{14,12},{16,18},{18,... | collective-permute-start | bytes 14874632 | tf_op jit(solution)/shard_map/ppermute | solution.py:49
  195.7 36.4 %collective-permute-start.31 = (f32[4,72,576]{2,1,0:T(8,128)}, f32[4,72,576]{2,1,0:T(8,128)S(1)}, u32[]{:S(2)}, u32[]{:S(2)}) collective-permute-start(f32[4,72,576]{2,1,0:T(8,128)} %constant_dynamic-slice_fusion.17), channel_id=1, source_target_pairs={{0,48},{2,50},{4,52},{6,54},{8,56},{10,58},{12,60},{14,62},{16,32}... | collective-permute-start | bytes 1990664 | tf_op jit(solution)/shard_map/ppermute | solution.py:49
  201.2 33.8 %collective-permute-start.21 = (f32[4,72,576]{2,1,0:T(8,128)}, f32[4,72,576]{2,1,0:T(8,128)}, u32[]{:S(2)}, u32[]{:S(2)}) collective-permute-start(f32[4,72,576]{2,1,0:T(8,128)} %constant_dynamic-slice_fusion.20), channel_id=1, source_target_pairs={{0,4},{2,6},{4,0},{6,2},{8,12},{10,14},{12,8},{14,10},{16,20},{18,... | collective-permute-start | bytes 1990664 | tf_op jit(solution)/shard_map/ppermute | solution.py:49
  234.9 47.4 %collective-permute-start.5 = (f32[9,1152]{1,0:T(8,128)S(1)}, f32[9,1152]{1,0:T(8,128)S(1)}, u32[]{:S(2)}, u32[]{:S(2)}) collective-permute-start(f32[9,1152]{1,0:T(8,128)S(1)} %add.398), channel_id=1, source_target_pairs={{0,16},{2,18},{4,20},{6,22},{8,24},{10,26},{12,28},{14,30},{16,0},... | collective-permute-start | bytes 124424 | tf_op jit(solution)/shard_map/ppermute | solution.py:49
  307.5 92.8 %collective-permute-start.7 = (f32[9,1152]{1,0:T(8,128)S(1)}, f32[9,1152]{1,0:T(8,128)S(1)}, u32[]{:S(2)}, u32[]{:S(2)}) collective-permute-start(f32[9,1152]{1,0:T(8,128)S(1)} %add.400), channel_id=1, source_target_pairs={{0,48},{2,50},{4,52},{6,54},{8,56},{10,58},{12,60},{14,62},{16,32}... | collective-permute-start | bytes 124424 | tf_op jit(solution)/shard_map/ppermute | solution.py:49
  308.8 94.5 %collective-permute-start.16 = (f32[1,72,576]{2,1,0:T(8,128)S(1)}, f32[1,72,576]{2,1,0:T(8,128)S(1)}, u32[]{:S(2)}, u32[]{:S(2)}) collective-permute-start(f32[1,72,576]{2,1,0:T(8,128)S(1)} %add.415), channel_id=1, source_target_pairs={{0,48},{2,50},{4,52},{6,54},{8,56},{10,58},{12,60},{14,62},{16,32}... | collective-permute-start | bytes 497672 | tf_op jit(solution)/shard_map/ppermute | solution.py:49
  318.9 27.1 %collective-permute-start.51 = (f32[4,40,2152]{2,1,0:T(8,128)S(1)}, f32[4,40,2152]{2,1,0:T(8,128)S(1)}, u32[]{:S(2)}, u32[]{:S(2)}) collective-permute-start(f32[4,40,2152]{2,1,0:T(8,128)S(1)} %constant_dynamic-slice_fusion.11), channel_id=1, source_target_pairs={{0,48},{2,50},{4,52},{6,54},{8,56},{10,58},{12,60},{14,62},{16,32}... | collective-permute-start | bytes 4131848 | tf_op jit(solution)/shard_map/ppermute | solution.py:49
  352.9 24.9 %collective-permute-start.52 = (f32[2,40,2152]{2,1,0:T(8,128)S(1)}, f32[2,40,2152]{2,1,0:T(8,128)S(1)}, u32[]{:S(2)}, u32[]{:S(2)}) collective-permute-start(f32[2,40,2152]{2,1,0:T(8,128)S(1)} %constant_dynamic-slice_fusion.10), channel_id=1, source_target_pairs={{0,12},{2,14},{4,8},{6,10},{8,4},{10,6},{12,0},{14,2},{16,28},{18,... | collective-permute-start | bytes 2065928 | tf_op jit(solution)/shard_map/ppermute | solution.py:49
  411.8 65.2 %collective-permute-start.17 = (f32[2,72,576]{2,1,0:T(8,128)S(1)}, f32[2,72,576]{2,1,0:T(8,128)S(1)}, u32[]{:S(2)}, u32[]{:S(2)}) collective-permute-start(f32[2,72,576]{2,1,0:T(8,128)S(1)} %maximum_select_fusion.24), channel_id=1, source_target_pairs={{0,4},{2,6},{4,0},{6,2},{8,12},{10,14},{12,8},{14,10},{16,20},{18,... | collective-permute-start | bytes 995336 | tf_op jit(solution)/shard_map/ppermute | solution.py:49
  417.7 25.5 %collective-permute-start.46 = (f32[1,40,1152]{2,1,0:T(8,128)S(1)}, f32[1,40,1152]{2,1,0:T(8,128)S(1)}, u32[]{:S(2)}, u32[]{:S(2)}) collective-permute-start(f32[1,40,1152]{2,1,0:T(8,128)S(1)} %add.451), channel_id=1, source_target_pairs={{0,4},{2,6},{4,0},{6,2},{8,12},{10,14},{12,8},{14,10},{16,20},{18,... | collective-permute-start | bytes 552968 | tf_op jit(solution)/shard_map/ppermute | solution.py:49
  443.3 26.7 %collective-permute-start.76 = (f32[4,72,1152]{2,1,0:T(8,128)S(1)}, f32[4,72,1152]{2,1,0:T(8,128)S(1)}, u32[]{:S(2)}, u32[]{:S(2)}) collective-permute-start(f32[4,72,1152]{2,1,0:T(8,128)S(1)} %maximum_select_fusion.13), channel_id=1, source_target_pairs={{0,16},{2,18},{4,20},{6,22},{8,24},{10,26},{12,28},{14,30},{16,0},... | collective-permute-start | bytes 3981320 | tf_op jit(solution)/shard_map/ppermute | solution.py:49
  444.7 51.6 %collective-permute-start.38 = (f32[4,72,576]{2,1,0:T(8,128)S(1)}, f32[4,72,576]{2,1,0:T(8,128)S(1)}, u32[]{:S(2)}, u32[]{:S(2)}) collective-permute-start(f32[4,72,576]{2,1,0:T(8,128)S(1)} %maximum_select_fusion.18), channel_id=1, source_target_pairs={{0,48},{2,50},{4,52},{6,54},{8,56},{10,58},{12,60},{14,62},{16,32}... | collective-permute-start | bytes 1990664 | tf_op jit(solution)/shard_map/ppermute | solution.py:49
  448.0 47.7 %collective-permute-start.47 = (f32[2,40,1152]{2,1,0:T(8,128)S(1)}, f32[2,40,1152]{2,1,0:T(8,128)S(1)}, u32[]{:S(2)}, u32[]{:S(2)}) collective-permute-start(f32[2,40,1152]{2,1,0:T(8,128)S(1)} %maximum_select_fusion.27), channel_id=1, source_target_pairs={{0,16},{2,18},{4,20},{6,22},{8,24},{10,26},{12,28},{14,30},{16,0},... | collective-permute-start | bytes 1105928 | tf_op jit(solution)/shard_map/ppermute | solution.py:49
  467.3 29.3 %collective-permute-start.66 = (f32[4,32,2152]{2,1,0:T(8,128)S(1)}, f32[4,32,2152]{2,1,0:T(8,128)S(1)}, u32[]{:S(2)}, u32[]{:S(2)}) collective-permute-start(f32[4,32,2152]{2,1,0:T(8,128)S(1)} %maximum_select_fusion.15), channel_id=1, source_target_pairs={{0,12},{2,14},{4,8},{6,10},{8,4},{10,6},{12,0},{14,2},{16,28},{18,... | collective-permute-start | bytes 3305480 | tf_op jit(solution)/shard_map/ppermute | solution.py:49
  469.9 31.7 %collective-permute-start.58 = (f32[4,40,2152]{2,1,0:T(8,128)S(1)}, f32[4,40,2152]{2,1,0:T(8,128)S(1)}, u32[]{:S(2)}, u32[]{:S(2)}) collective-permute-start(f32[4,40,2152]{2,1,0:T(8,128)S(1)} %maximum_select_fusion.12), channel_id=1, source_target_pairs={{0,48},{2,50},{4,52},{6,54},{8,56},{10,58},{12,60},{14,62},{16,32}... | collective-permute-start | bytes 4131848 | tf_op jit(solution)/shard_map/ppermute | solution.py:49
  477.0 83.3 %collective-permute-start.85 = (f32[1088,1152]{1,0:T(8,128)}, f32[1088,1152]{1,0:T(8,128)}, u32[]{:S(2)}, u32[]{:S(2)}) collective-permute-start(f32[1088,1152]{1,0:T(8,128)} %pad_maximum_fusion.5), channel_id=1, source_target_pairs={{0,2},{2,0},{4,6},{6,4},{8,10},{10,8},{12,14},{14,12},{16,18},{18,... | collective-permute-start | bytes 15040520 | tf_op jit(solution)/shard_map/ppermute | solution.py:49
  517.1 52.4 %collective-permute-start.67 = (f32[576,2152]{1,0:T(8,128)}, f32[576,2152]{1,0:T(8,128)}, u32[]{:S(2)}, u32[]{:S(2)}) collective-permute-start(f32[576,2152]{1,0:T(8,128)} %pad_maximum_fusion.4), channel_id=1, source_target_pairs={{0,2},{2,0},{4,6},{6,4},{8,10},{10,8},{12,14},{14,12},{16,18},{18,... | collective-permute-start | bytes 14874632 | tf_op jit(solution)/shard_map/ppermute | solution.py:49
  526.8 29.0 %collective-permute-start.49 = (f32[320,1152]{1,0:T(8,128)}, f32[320,1152]{1,0:T(8,128)}, u32[]{:S(2)}, u32[]{:S(2)}) collective-permute-start(f32[320,1152]{1,0:T(8,128)} %bitcast.15), channel_id=1, source_target_pairs={{0,2},{2,0},{4,6},{6,4},{8,10},{10,8},{12,14},{14,12},{16,18},{18,... | collective-permute-start | bytes 4423688 | tf_op jit(solution)/shard_map/ppermute | solution.py:49
  (153 other events, 1809.1 us)

commit v2 on v1

v2 whole, which is shorter than its diff:
```python
import jax
import jax.numpy as jnp
from jax import lax
from jax.experimental import pallas as pl
from jax.experimental.pallas import tpu as pltpu
from jax.sharding import PartitionSpec as P

HEAD = 72
norm_epsilon = 1e-06


def partner_pairs(move):
    pairs = []
    for place in range(64):
        z_hi, x, y, core = place >> 5, (place >> 3) & 3, (place >> 1) & 3, place & 1
        z_hi, x, y, core = move(z_hi, x, y, core)
        pairs.append((place, ((z_hi * 4 + x) * 4 + y) * 2 + core))
    return pairs


PAIRS = {
    "core": partner_pairs(lambda z, x, y, c: (z, x, y, 1 - c)),
    "xa": partner_pairs(lambda z, x, y, c: (z, x ^ 1, y, c)),
    "xb": partner_pairs(lambda z, x, y, c: (z, x ^ 3, y, c)),
    "ya": partner_pairs(lambda z, x, y, c: (z, x, y ^ 1, c)),
    "yb": partner_pairs(lambda z, x, y, c: (z, x, y ^ 3, c)),
    "z": partner_pairs(lambda z, x, y, c: (1 - z, x, y, c)),
}
PLANES = [
    [((z_hi * 4 + x) * 4 + y) * 2 + core for x in range(4) for y in range(4)]
    for z_hi in range(2)
    for core in range(2)
]
ORDERS = (
    ("xa", "ya", "xb", "yb"),
    ("ya", "xb", "yb", "xa"),
    ("xb", "yb", "xa", "ya"),
    ("yb", "xa", "ya", "xb"),
)


def sides():
    place = lax.axis_index("dp")
    x = (place >> 3) & 3
    y = (place >> 1) & 3
    return {
        "core": place & 1,
        "xa": (x ^ (x >> 1)) & 1,
        "xb": x >> 1,
        "ya": (y ^ (y >> 1)) & 1,
        "yb": y >> 1,
    }


def swap(values, pair):
    return lax.ppermute(values, "dp", PAIRS[pair])


def swap_tensor(values):
    return lax.ppermute(values, "tensor", [(0, 1), (1, 0)])


class Cell:
    def __init__(self, value):
        self.value = value


class Order:
    def __init__(self):
        self.last = None

    def run(self, operation, ready):
        if self.last is not None:
            self.last.value, ready = lax.optimization_barrier((self.last.value, ready))
        self.last = Cell(operation(ready))
        return self.last


def half_of(values, side):
    count = values.shape[0] // 2
    return lax.dynamic_slice_in_dim(values, side * count, count, 0)


def row_half_of(values, side):
    count = values.shape[1] // 2
    return jnp.where(side == 0, values[:, :count], values[:, count:])


def joined(own, received, side, axis):
    return jnp.where(
        side == 0,
        jnp.concatenate([own, received], axis),
        jnp.concatenate([received, own], axis),
    )


class Stream:
    def __init__(self, name, order, pairs, side):
        self.name = name
        self.order = order
        self.pairs = pairs
        self.side = side
        self.stage = 0
        self.keep = None
        self.sent = None

    def begin(self, send, keep):
        four = (4, send.shape[0] // 4, send.shape[1])
        self.sent = Cell(send.reshape(four))
        self.order.last = self.sent
        self.keep = keep.reshape(four)
        self.stage = 1

    def step(self):
        pairs = self.pairs
        stage = self.stage
        self.stage += 1
        keep = self.keep
        with jax.named_scope(self.name + "_move_" + str(stage)):
            if stage <= 4:
                received = swap(self.sent.value, pairs[stage - 1])
            elif stage == 5:
                received = swap(self.sent.value, "z")
            else:
                pair = pairs[9 - stage]
                received = swap(self.sent.value, pair)
        with jax.named_scope(self.name + "_sum_" + str(stage)):
            if stage <= 3:
                take = half_of if stage < 3 else row_half_of
                side = self.side[pairs[stage]]
                self.keep = take(keep, side) + take(received, side)
                self.sent = self.order.run(
                    lambda ready: take(ready, 1 - side) + take(received, 1 - side), keep
                )
            elif stage == 4:
                self.sent = self.order.run(lambda ready: ready + received, keep)
            elif stage == 5:
                self.sent = self.order.run(lambda ready: ready + received, self.sent.value)
            else:
                axis = 1 if stage == 6 else 0
                self.sent = self.order.run(
                    lambda ready: joined(ready, received, self.side[pair], axis), self.sent.value
                )

    def pieces(self):
        whole = self.sent.value
        whole = whole.reshape(-1, whole.shape[2])
        with jax.named_scope(self.name + "_core"):
            return whole, swap(whole, "core")


def sent_gradient(left, right, parts):
    tokens, count = left.shape
    columns = right.shape[1]
    piece = count // (4 * parts)

    def kernel(left_ref, right_ref, *refs):
        turned_ref = refs[parts]
        step = pl.program_id(0)

        @pl.when(step == 0)
        def _():
            turned_ref[...] = left_ref[...].T

        rows = turned_ref[pl.ds(pl.multiple_of(step * piece, 16), piece), :]
        result = jnp.dot(rows, right_ref[...], preferred_element_type=jnp.float32)
        for part in range(parts):

            @pl.when(step // 4 == part)
            def _():
                refs[part][...] = result

    def place(part):
        return pl.BlockSpec(
            (piece, columns), lambda step: (jnp.clip(step - 4 * part, 0, 3), 0)
        )

    return pl.pallas_call(
        kernel,
        grid=(4 * parts,),
        in_specs=[
            pl.BlockSpec((tokens, count), lambda step: (0, 0)),
            pl.BlockSpec((tokens, columns), lambda step: (0, 0)),
        ],
        out_specs=[place(part) for part in range(parts)],
        out_shape=[jax.ShapeDtypeStruct((count // parts, columns), jnp.float32)] * parts,
        scratch_shapes=[pltpu.VMEM((count, tokens), jnp.bfloat16)],
        compiler_params=pltpu.CompilerParams(vmem_limit_bytes=40 * 1024 * 1024),
        cost_estimate=pl.CostEstimate(
            flops=2 * tokens * count * columns,
            bytes_accessed=4 * count * columns,
            transcendentals=0,
        ),
    )(left, right)


def whole_gradient(left, right, received):
    tokens, count = left.shape
    columns = right.shape[1]
    parts = len(received)
    piece = count // (4 * parts)

    def kernel(left_ref, right_ref, *refs):
        out_ref, turned_ref = refs[parts:]
        step = pl.program_id(0)

        @pl.when(step == 0)
        def _():
            turned_ref[...] = left_ref[...].T

        rows = turned_ref[pl.ds(pl.multiple_of(step * piece, 16), piece), :]
        result = jnp.dot(rows, right_ref[...], preferred_element_type=jnp.float32)
        for part in range(parts):

            @pl.when(step // 4 == part)
            def _():
                out_ref[...] = result + refs[part][...]

    def place(part):
        return pl.BlockSpec(
            (piece, columns), lambda step: (jnp.clip(step - 4 * part, 0, 3), 0)
        )

    return pl.pallas_call(
        kernel,
        grid=(4 * parts,),
        in_specs=[
            pl.BlockSpec((tokens, count), lambda step: (0, 0)),
            pl.BlockSpec((tokens, columns), lambda step: (0, 0)),
        ]
        + [place(part) for part in range(parts)],
        out_specs=pl.BlockSpec((piece, columns), lambda step: (step, 0)),
        out_shape=jax.ShapeDtypeStruct((count, columns), jnp.float32),
        scratch_shapes=[pltpu.VMEM((count, tokens), jnp.bfloat16)],
        compiler_params=pltpu.CompilerParams(vmem_limit_bytes=48 * 1024 * 1024),
        cost_estimate=pl.CostEstimate(
            flops=2 * tokens * count * columns,
            bytes_accessed=8 * count * columns,
            transcendentals=0,
        ),
    )(left, right, *received)


def own_gradient(left, right, received, side, first, count):
    tokens, wide = left.shape
    columns = right.shape[1]
    piece = count // 4

    def place(step, here):
        return jnp.where(step < 2, (1 - here) * 2 + step, here * 2 + step - 2)

    def kernel(side_ref, left_ref, right_ref, received_ref, send_ref, keep_ref, turned_ref):
        step = pl.program_id(0)

        @pl.when(step == 0)
        def _():
            turned_ref[...] = left_ref[...].T

        begin = pl.multiple_of(first + place(step, side_ref[0]) * piece, 16)
        rows = turned_ref[pl.ds(begin, piece), :]
        total = jnp.dot(rows, right_ref[...], preferred_element_type=jnp.float32)
        total = total + received_ref[...]

        @pl.when(step < 2)
        def _():
            send_ref[...] = total

        @pl.when(step >= 2)
        def _():
            keep_ref[...] = total

    half = jax.ShapeDtypeStruct((count // 2, columns), jnp.float32)
    return pl.pallas_call(
        kernel,
        grid_spec=pltpu.PrefetchScalarGridSpec(
            num_scalar_prefetch=1,
            grid=(4,),
            in_specs=[
                pl.BlockSpec((tokens, wide), lambda step, here: (0, 0)),
                pl.BlockSpec((tokens, columns), lambda step, here: (0, 0)),
                pl.BlockSpec(
                    (piece, columns),
                    lambda step, here: (first // piece + place(step, here[0]), 0),
                ),
            ],
            out_specs=(
                pl.BlockSpec((piece, columns), lambda step, here: (jnp.minimum(step, 1), 0)),
                pl.BlockSpec((piece, columns), lambda step, here: (jnp.maximum(step - 2, 0), 0)),
            ),
            scratch_shapes=[pltpu.VMEM((wide, tokens), jnp.bfloat16)],
        ),
        out_shape=(half, half),
        compiler_params=pltpu.CompilerParams(vmem_limit_bytes=32 * 1024 * 1024),
        cost_estimate=pl.CostEstimate(
            flops=2 * tokens * count * columns,
            bytes_accessed=8 * count * columns,
            transcendentals=0,
        ),
    )(side.reshape(1), left, right, received)


def pick_rows(core, pieces, rows, block):
    columns = pieces[0][0].shape[1]
    counts = [own.shape[0] // block for own, _ in pieces]
    firsts = [sum(counts[:number]) for number in range(len(counts))]

    def kernel(core_ref, *refs):
        first_ref, second_ref = refs[-2:]
        here = pl.program_id(0)
        for number, (first, count) in enumerate(zip(firsts, counts)):
            own_ref, other_ref = refs[2 * number : 2 * number + 2]
            inside = (here >= first) & (here < first + count)

            @pl.when(inside & (core_ref[0] == 0))
            def _():
                first_ref[...] = own_ref[...]
                second_ref[...] = other_ref[...]

            @pl.when(inside & (core_ref[0] != 0))
            def _():
                first_ref[...] = other_ref[...]
                second_ref[...] = own_ref[...]

    def place(first, count):
        return pl.BlockSpec(
            (block, columns), lambda i, core_ref: (jnp.clip(i - first, 0, count - 1), 0)
        )

    specs = [place(first, count) for first, count in zip(firsts, counts) for _ in range(2)]
    shape = jax.ShapeDtypeStruct((rows, columns), jnp.float32)
    out_spec = pl.BlockSpec((block, columns), lambda i, core_ref: (i, 0))
    return pl.pallas_call(
        kernel,
        grid_spec=pltpu.PrefetchScalarGridSpec(
            num_scalar_prefetch=1,
            grid=(sum(counts),),
            in_specs=specs,
            out_specs=(out_spec, out_spec),
        ),
        out_shape=(shape, shape),
        compiler_params=pltpu.CompilerParams(vmem_limit_bytes=40 * 1024 * 1024),
        cost_estimate=pl.CostEstimate(
            flops=0, bytes_accessed=16 * rows * columns, transcendentals=0
        ),
    )(core.reshape(1), *[part for pair in pieces for part in pair])


def normalized(values):
    center = values - jnp.mean(values, axis=-1, keepdims=True)
    spread = jnp.mean(center * center, axis=-1, keepdims=True)
    factor = lax.rsqrt(spread + norm_epsilon)
    return center * factor, factor


def norm_back(grad, normal, factor, gain):
    scaled = grad * gain
    mean_scaled = jnp.mean(scaled, axis=-1, keepdims=True)
    mean_normal = jnp.mean(scaled * normal, axis=-1, keepdims=True)
    return factor * (scaled - mean_scaled - normal * mean_normal)


def gelu_tanh(values):
    return jax.nn.gelu(values, approximate=True)


def product(left, right):
    return jnp.dot(left, right, preferred_element_type=jnp.float32)


def inner_rows(left, right):
    return lax.dot_general(
        left, right, (((0,), (0,)), ((), ())), preferred_element_type=jnp.float32
    )


def against(left, right):
    return lax.dot_general(
        left, right, (((1,), (1,)), ((), ())), preferred_element_type=jnp.float32
    )


def segments(layout, length):
    bounds = jnp.cumsum(layout[:, :-1], axis=1)
    places = jnp.arange(length, dtype=jnp.int32)
    inside = (places[None, :, None] >= bounds[:, None, :]).astype(jnp.int32)
    return jnp.sum(inside, axis=2)


def shards(
    hidden_in,
    row_layout,
    cotangent,
    pre_gain,
    pre_shift,
    query_weight,
    query_bias,
    key_weight,
    value_weight,
    value_bias,
    out_weight,
    out_bias,
    mid_gain,
    mid_shift,
    up_weight,
    up_bias,
    down_weight,
    down_bias,
):
    rows, length, width = hidden_in.shape
    tokens = rows * length
    heads_wide = query_weight.shape[1]
    heads_here = heads_wide // HEAD
    hidden = up_weight.shape[1]
    padded = -(-hidden // 128) * 128
    scale_factor = HEAD ** (-0.5)
    head_shape = (length, heads_here, HEAD)
    side = sides()
    core = side["core"]
    order = Order()

    def row_of(values, row):
        return values[row * length : (row + 1) * length]

    inputs = hidden_in.reshape(tokens, width).astype(jnp.float32)
    segment = segments(row_layout, length)
    same_picture = (segment[:, :, None] == segment[:, None, :])[:, None]
    pre_normal, pre_factor = normalized(inputs)
    normed = (pre_normal * pre_gain + pre_shift).astype(jnp.bfloat16)
    queries = (product(normed, query_weight) + query_bias).astype(jnp.bfloat16)
    keys = product(normed, key_weight).astype(jnp.bfloat16)
    values = (product(normed, value_weight) + value_bias).astype(jnp.bfloat16)
    cot_low = cotangent.reshape(tokens, width)
    cot_float = cot_low.astype(jnp.float32)

    heads = []
    probs = []
    attended = []
    branch = []
    for row in range(rows):
        q, k, v = (row_of(part, row).reshape(head_shape) for part in (queries, keys, values))
        heads.append((q, k, v))
        raw = jnp.einsum("qhd,khd->hqk", q, k, preferred_element_type=jnp.float32)
        scores = jnp.where(same_picture[row], raw * scale_factor, -1000000000.0)
        maximum = jnp.max(scores, axis=-1, keepdims=True)
        exponent = jnp.exp(scores - maximum)
        probs.append(exponent / jnp.sum(exponent, axis=-1, keepdims=True))
        mixed = jnp.einsum(
            "hqk,khd->qhd",
            probs[row].astype(jnp.bfloat16),
            v,
            preferred_element_type=jnp.float32,
        )
        attended.append(mixed.astype(jnp.bfloat16).reshape(length, heads_wide))
        branch.append(order.run(lambda ready: product(ready, out_weight), attended[row]))
    act_grad = order.run(lambda ready: against(ready, down_weight), cot_low)

    resid = []
    mid_normal = []
    mid_factor = []
    middle = []
    activ = []
    pre_grad = []
    mid_part = []
    for row in range(rows):
        with jax.named_scope("branch_move_" + str(row)):
            received = swap_tensor(branch[row].value)
        resid.append(
            order.run(
                lambda ready: row_of(inputs, row) + ((ready + received) + out_bias),
                branch[row].value,
            )
        )
        normal, factor = normalized(resid[row].value)
        mid_normal.append(normal)
        mid_factor.append(factor)
        middle.append((normal * mid_gain + mid_shift).astype(jnp.bfloat16))
        pre_act = product(middle[row], up_weight) + up_bias
        activ_float, gelu_pull = jax.vjp(gelu_tanh, pre_act)
        activ.append(activ_float.astype(jnp.bfloat16))
        pre_grad.append(gelu_pull(row_of(act_grad.value, row))[0].astype(jnp.bfloat16))
        mid_part.append(order.run(lambda ready: against(ready, up_weight), pre_grad[row]))

    is_first = core == 0
    activ_all = jnp.concatenate(activ, 0)
    pre_grad_all = jnp.concatenate(pre_grad, 0)
    middle_all = jnp.concatenate(middle, 0)
    keep_right = jnp.where(is_first, cot_low, middle_all)
    send_right = jnp.where(is_first, middle_all, cot_low)
    widen = ((0, 0), (0, padded - hidden))
    m_send_left = jnp.pad(jnp.where(is_first, pre_grad_all, activ_all), widen)
    m_keep_left = jnp.pad(jnp.where(is_first, activ_all, pre_grad_all), widen)
    m_sends = order.run(lambda ready: sent_gradient(ready, send_right, 2), m_send_left)

    resid_grad = []
    branch_grad = []
    gain_terms = []
    row_grads = []

    def mid_back(row):
        with jax.named_scope("mid_move_" + str(row)):
            received = swap_tensor(mid_part[row].value)
        mid_grad = order.run(lambda ready: ready + received, mid_part[row].value).value
        gain_terms.append(
            (jnp.sum(mid_grad * mid_normal[row], axis=0), jnp.sum(mid_grad, axis=0))
        )
        resid_grad.append(
            row_of(cot_float, row) + norm_back(mid_grad, mid_normal[row], mid_factor[row], mid_gain)
        )
        branch_grad.append(resid_grad[row].astype(jnp.bfloat16))

    def attention_back(row, meanwhile):
        attended_grad = order.run(
            lambda ready: against(ready, out_weight).astype(jnp.bfloat16), branch_grad[row]
        )
        attended_grad = attended_grad.value.reshape(head_shape)
        q, k, v = heads[row]
        prob_grad = jnp.einsum("qhd,khd->hqk", attended_grad, v, preferred_element_type=jnp.float32)
        score_grad = order.run(
            lambda ready: (
                ready * (prob_grad - jnp.sum(prob_grad * ready, axis=-1, keepdims=True))
            ).astype(jnp.bfloat16),
            probs[row],
        )
        meanwhile()
        value_grad = jnp.einsum(
            "hqk,qhd->khd",
            probs[row].astype(jnp.bfloat16),
            attended_grad,
            preferred_element_type=jnp.float32,
        )
        query_grad = jnp.einsum(
            "hqk,khd->qhd", score_grad.value, k, preferred_element_type=jnp.float32
        )
        key_grad = jnp.einsum(
            "hqk,qhd->khd", score_grad.value, q, preferred_element_type=jnp.float32
        )
        row_grads.append(
            tuple(
                part.astype(jnp.bfloat16).reshape(length, heads_wide)
                for part in (query_grad * scale_factor, key_grad * scale_factor, value_grad)
            )
        )

    output_part = order.run(lambda ready: product(ready, down_weight), activ_all)
    m_received = []
    for number, part in enumerate(m_sends.value):
        with jax.named_scope("ff_core_move_" + str(number)):
            m_received.append(swap(part, "core"))
    m_own = order.run(lambda ready: whole_gradient(ready, keep_right, m_received), m_keep_left)
    with jax.named_scope("ff_scatter"):
        m_block = lax.psum_scatter(
            m_own.value, "dp", axis_index_groups=PLANES, scatter_dimension=0, tiled=True
        )
    mid_back(0)
    attention_back(0, lambda: None)
    mid_back(1)
    attention_back(1, lambda: None)
    mid_gain_grad = gain_terms[0][0] + gain_terms[1][0]
    mid_shift_grad = gain_terms[0][1] + gain_terms[1][1]

    query_grad, key_grad, value_grad = (
        jnp.concatenate([row_grads[row][place] for row in range(rows)], 0) for place in range(3)
    )
    attended_all = jnp.concatenate(attended, 0)
    branch_grad_all = jnp.concatenate(branch_grad, 0)
    n_streams = [Stream("at" + str(n), order, ORDERS[n], side) for n in (2, 3, 0, 1)]
    n_keep = (
        (jnp.where(is_first, query_grad, value_grad), normed),
        (
            jnp.where(is_first, key_grad, attended_all),
            jnp.where(is_first, normed, branch_grad_all),
        ),
    )
    n_send = (
        (jnp.where(is_first, value_grad, query_grad), normed),
        (
            jnp.where(is_first, attended_all, key_grad),
            jnp.where(is_first, branch_grad_all, normed),
        ),
    )
    with jax.named_scope("output_move"):
        received = swap_tensor(output_part.value)
    output = order.run(
        lambda ready: (
            jnp.concatenate([part.value for part in resid], 0) + (ready + received) + down_bias
        ).astype(jnp.bfloat16),
        output_part.value,
    )
    n_sends = []
    for left, right in n_send:
        n_sends.append(order.run(lambda ready: sent_gradient(ready, right, 1)[0], left))
    for n in range(2):
        left, right = n_keep[n]
        with jax.named_scope("at" + str(n) + "_core_move"):
            received = swap(n_sends[n].value, "core")
        for stream, first, count in (
            (n_streams[2 * n], 0, 320),
            (n_streams[2 * n + 1], 320, 256),
        ):
            here = side[stream.pairs[0]]
            halves = order.run(
                lambda ready: own_gradient(left, ready, received, here, first, count), right
            )
            stream.begin(*halves.value)
    normed_part = order.run(
        lambda ready: against(ready, query_weight)
        + against(key_grad, key_weight)
        + against(value_grad, value_weight),
        query_grad,
    )

    def n_step():
        for stream in n_streams:
            stream.step()

    n_step()
    m_block = order.run(lambda ready: ready + 0.0, m_block)
    with jax.named_scope("ff_z_move"):
        received = swap(m_block.value, "z")
    m_block = order.run(lambda ready: ready + received, m_block.value)
    with jax.named_scope("ff_gather"):
        m_whole = lax.all_gather(
            m_block.value, "dp", axis_index_groups=PLANES, axis=0, tiled=True
        )
    n_step()
    n_step()
    n_step()
    with jax.named_scope("normed_move"):
        received = swap_tensor(normed_part.value)
    normed_grad = order.run(lambda ready: ready + received, normed_part.value)
    pre_gain_grad = jnp.sum(normed_grad.value * pre_normal, axis=0)
    pre_shift_grad = jnp.sum(normed_grad.value, axis=0)
    input_grad = jnp.concatenate(resid_grad, 0) + norm_back(
        normed_grad.value, pre_normal, pre_factor, pre_gain
    )
    small = jnp.concatenate(
        [
            pre_gain_grad,
            pre_shift_grad,
            jnp.sum(branch_grad_all.astype(jnp.float32), axis=0),
            mid_gain_grad,
            mid_shift_grad,
            jnp.sum(cot_float, axis=0),
            jnp.sum(query_grad.astype(jnp.float32), axis=0),
            jnp.sum(value_grad.astype(jnp.float32), axis=0),
            jnp.sum(pre_grad_all.astype(jnp.float32), axis=0),
            jnp.zeros((2 * width - hidden,), jnp.float32),
        ]
    ).reshape(9, width)
    small = order.run(lambda ready: ready, small)

    def small_step(small, pair):
        with jax.named_scope("small_move_" + pair):
            received = swap(small.value, pair)
        return order.run(lambda ready: ready + received, small.value)

    small = small_step(small, "core")
    n_step()
    small = small_step(small, "z")
    n_step()
    m_whole = order.run(lambda ready: ready, m_whole)
    small = small_step(small, "xa")
    with jax.named_scope("ff_core_back"):
        received = swap(m_whole.value, "core")
    small = small_step(small, "ya")
    n_step()
    small = small_step(small, "xb")
    small = small_step(small, "yb")
    n_step()
    small = small.value
    picked = order.run(
        lambda ready: pick_rows(core, [(ready, received)], hidden, 128), m_whole.value
    )
    n_step()
    down_grad, up_grad = picked.value
    pieces = [stream.pieces() for stream in n_streams]
    query_weight_grad, value_weight_grad = pick_rows(core, pieces[:2], heads_wide, 64)
    key_weight_grad, out_grad = pick_rows(core, pieces[2:], heads_wide, 64)
    return (
        output.value.reshape(hidden_in.shape),
        input_grad.astype(jnp.bfloat16).reshape(hidden_in.shape),
        small[0],
        small[1],
        query_weight_grad.T,
        small[6, :heads_wide],
        key_weight_grad.T,
        value_weight_grad.T,
        small[6, heads_wide:],
        out_grad,
        small[2],
        small[3],
        small[4],
        up_grad.T,
        small[7:].reshape(-1)[:hidden],
        down_grad,
        small[5],
    )


def solution(mesh):
    placed = (
        P("dp", None, None),
        P("dp", None),
        P("dp", None, None),
        P(),
        P(),
        P(None, "tensor"),
        P("tensor"),
        P(None, "tensor"),
        P(None, "tensor"),
        P("tensor"),
        P("tensor", None),
        P(),
        P(),
        P(),
        P(None, "tensor"),
        P("tensor"),
        P("tensor", None),
        P(),
    )
    return jax.shard_map(
        shards,
        mesh=mesh,
        in_specs=placed,
        out_specs=(
            P("dp", None, None),
            P("dp", None, None),
            P(),
            P(),
            P(None, "tensor"),
            P("tensor"),
            P(None, "tensor"),
            P(None, "tensor"),
            P("tensor"),
            P("tensor", None),
            P(),
            P(),
            P(),
            P(None, "tensor"),
            P("tensor"),
            P("tensor", None),
            P(),
        ),
        check_vma=False,
    )
```

time: 598 us -> 463 us (0.77)
  waiting for transfers between devices: 267 us -> 146 us
  Pallas kernels: 0 us -> 66.9 us
  starting transfers between devices: 124 us -> 76.9 us
  other arithmetic: 81.4 us -> 57 us
  matrix products: 71.8 us -> 54.7 us
  between operations: 2.81 us -> 15.7 us
  local copies, waits for them, and re-layouts: 44 us -> 37.9 us
    ppermute x82 -> x52, waiting for transfers between devices: 156 us -> 72.4 us  [swap(): return lax.ppermute(values, 'dp', PAIRS[pair])]
    pallas_call x0 -> x11, Pallas kernels: none -> 66.9 us  [the longest x3 30.5 us: pick_rows(): pl.pallas_call(kernel, grid_spec=pltpu.PrefetchScalarGridSpec(num_scalar_...]
    ppermute x4 -> x6, waiting for transfers between devices: 111 us -> 55.8 us  [swap_tensor(): return lax.ppermute(values, 'tensor', [(0, 1), (1, 0)])]
    ppermute x82 -> x52, starting transfers between devices: 119 us -> 69.9 us  [swap(): return lax.ppermute(values, 'dp', PAIRS[pair])]
    select_n x31 -> x21, other arithmetic: 47.3 us -> 15.1 us  [the longest x16 8.79 us: joined(): jnp.where(side == 0, jnp.concatenate([own, received], axis), jnp.concaten...]
    dot_general x18 -> x10, matrix products: 39.2 us -> 12.2 us  [the longest x2 4.27 us: attention_back(): jnp.einsum('qhd,khd->hqk', attended_grad, v, preferred_element_type=jnp.f...]
    all_gather x0 -> x1, waiting for transfers between devices: none -> 17.5 us  [shards(): lax.all_gather(m_block.value, 'dp', axis_index_groups=PLANES, axis=0, til...]
    unnamed x186 -> x196, local copies, waits for them, and re-layouts: 28.8 us -> 17.1 us
  transfers between devices with their start and end apart: 86 -> 60, of which waited for: 38 -> 27; matrix products, arithmetic and copies ran while one was open for 21% -> 22% of each run, Pallas kernels for 0% -> 9%
where the time goes in v2:
time: 463 us; the launch traced here: 455 us
  waiting for transfers between devices  146 us (32%)
  starting transfers between devices  76.9 us (17%)
  Pallas kernels  66.9 us (14%)
  other arithmetic  57 us (12%)
  matrix products  54.7 us (12%)
  local copies, waits for them, and re-layouts  37.9 us (8%)
  between operations  15.7 us (3%)
    ppermute x52, waiting for transfers between devices, swap(): return lax.ppermute(values, 'dp', PAIRS[pair])  72.4 us
    ppermute x52, starting transfers between devices, swap(): return lax.ppermute(values, 'dp', PAIRS[pair])  69.9 us
    ppermute x6, waiting for transfers between devices, swap_tensor(): return lax.ppermute(values, 'tensor', [(0, 1), (1, 0)])  55.8 us
    pallas_call x3, Pallas kernels, pick_rows(): pl.pallas_call(kernel, grid_spec=pltpu.PrefetchScalarGridSpec(num_scalar_...  30.5 us
    dot_general x8, matrix products, product(): return jnp.dot(left, right, preferred_element_type=jnp.float32)  18.4 us
    dot_general x8, matrix products, against(): lax.dot_general(left, right, (((1,), (1,)), ((), ())), preferred_element_...  18.4 us
    all_gather x1, waiting for transfers between devices, shards(): lax.all_gather(m_block.value, 'dp', axis_index_groups=PLANES, axis=0, til...  17.5 us
    unnamed x196, local copies, waits for them, and re-layouts  17.1 us
  transfers between devices with their start and end apart: 60, of which 27 were waited for; matrix products, arithmetic and copies ran while one was open for 22% of the time, Pallas kernels for 9%

profile of v2, /device:TPU:1, one launch (start us, length us, event | category | flops | bytes accessed | tf_op | source)
XLA Modules:
  0.0 454.9 jit_solution(5275381994948758441)
XLA Ops:
  34.4 7.2 %fusion.61 = f32[384,2152]{0,1:T(8,128)} fusion(bf16[384,1152]{1,0:T(8,128)(2,1)S(1)} %bitcast.152, bf16[2152,1152]{1,0:T(8,128)(2,1)} %param.34), kind=kOutput, calls=%fused_computation.203 | convolution fusion | flops 1903951872 | bytes 9148416 | tf_op jit(solution)/shard_map/dot_general | solution.py:377
  41.6 5.0 %copy.100 = f32[384,2152]{1,0:T(8,128)} copy(f32[384,2152]{0,1:T(8,128)} %fusion.61) | data formatting | bytes 6610944 | tf_op jit(solution)/shard_map/optimization_barrier | solution.py:74
  46.6 4.4 collective-permute-done
  54.0 4.7 %multiply_convert_fusion.1 = (bf16[192,2152]{1,0:T(8,128)(2,1)S(1)}, bf16[192,2152]{1,0:T(8,128)(2,1)S(1)}) fusion(f32[384,2152]{1,0:T(8,128)S(1)} %copy-done.40, f32[2152]{0:T(1024)S(1)} %copy-done.93, bf16[192,1152]{1,0:T(8,128)(2,1)S(1)} %add_convert_fusion.2, bf16[1152,2152]{0,1:T(8,128)(2,1)} %param.32), kind=kOutput, calls=%fused_computation.43 | convolution fusion | flops 961479168 | bytes 8714656 | tf_op jit(solution)/shard_map/dot_general | solution.py:367
  60.9 9.1 %collective-permute-done.1 = f32[192,1152]{1,0:T(8,128)} collective-permute-done((f32[192,1152]{1,0:T(8,128)}, f32[192,1152]{1,0:T(8,128)}, u32[]{:S(2)}, u32[]{:S(2)}) %collective-permute-start.1) | collective-permute-done | bytes 884768 | tf_op jit(solution)/shard_map/branch_move_1/ppermute | solution.py:60
  79.5 5.3 %shard_map.305 = (f32[1088,1152]{1,0:T(8,128)S(1)}, f32[1088,1152]{1,0:T(8,128)S(1)}) custom-call(bf16[384,2176]{1,0:T(8,128)(2,1)S(1)} %pad.7.left_ref, bf16[384,1152]{1,0:T(8,128)(2,1)S(1)} %get-tuple-element.347.right_ref), custom_call_target="tpu_custom_call" | custom-call | flops 1925185536 | bytes 10027008 | tf_op jit(solution)/shard_map/pallas_call | solution.py:178
  87.9 6.0 %fusion.64 = f32[384,1152]{1,0:T(8,128)} fusion(bf16[384,2152]{1,0:T(8,128)(2,1)S(1)} %copy-done.54, bf16[2152,1152]{1,0:T(8,128)(2,1)} %param.34), kind=kOutput, calls=%fused_computation.206 | convolution fusion | flops 1903951872 | bytes 8380416 | tf_op jit(solution)/shard_map/dot_general | solution.py:367
  94.3 7.2 %collective-permute-done.3.refs_1_ = f32[1088,1152]{1,0:T(8,128)S(1)} collective-permute-done((f32[1088,1152]{1,0:T(8,128)S(1)}, f32[1088,1152]{1,0:T(8,128)S(1)}, u32[]{:S(2)}, u32[]{:S(2)}) %collective-permute-start.3) | collective-permute-done | bytes 5013536 | tf_op jit(solution)/shard_map/ff_core_move_1/ppermute | solution.py:56
  103.8 12.2 %shard_map.306 = f32[2176,1152]{1,0:T(8,128)} custom-call(bf16[384,2176]{1,0:T(8,128)(2,1)S(1)} %pad.8.left_ref, bf16[384,1152]{1,0:T(8,128)(2,1)S(1)} %get-tuple-element.346.right_ref, f32[1088,1152]{1,0:T(8,128)} %copy-done.31, f32[1088,1152]{1,0:T(8,128)} %copy-done.32), custom_call_target="tpu_custom_call" | custom-call | flops 1925185536 | bytes 20054016 | tf_op jit(solution)/shard_map/pallas_call | solution.py:224
  123.6 13.7 %collective-permute-done.4 = f32[192,1152]{1,0:T(8,128)} collective-permute-done((f32[192,1152]{1,0:T(8,128)}, f32[192,1152]{1,0:T(8,128)}, u32[]{:S(2)}, u32[]{:S(2)}) %collective-permute-start.4) | collective-permute-done | bytes 884768 | tf_op jit(solution)/shard_map/mid_move_0/ppermute | solution.py:60
  148.2 8.0 %collective-permute-done.5 = f32[192,1152]{1,0:T(8,128)} collective-permute-done((f32[192,1152]{1,0:T(8,128)}, f32[192,1152]{1,0:T(8,128)}, u32[]{:S(2)}, u32[]{:S(2)}) %collective-permute-start.5) | collective-permute-done | bytes 884768 | tf_op jit(solution)/shard_map/mid_move_1/ppermute | solution.py:60
  179.3 14.9 %collective-permute-done.6 = f32[384,1152]{1,0:T(8,128)} collective-permute-done((f32[384,1152]{1,0:T(8,128)}, f32[384,1152]{1,0:T(8,128)}, u32[]{:S(2)}, u32[]{:S(2)}) %collective-permute-start.6) | collective-permute-done | bytes 1769504 | tf_op jit(solution)/shard_map/output_move/ppermute | solution.py:60
  235.3 11.4 %collective-permute-done.9 = f32[4,40,1152]{2,1,0:T(8,128)S(1)} collective-permute-done((f32[4,40,1152]{2,1,0:T(8,128)S(1)}, f32[4,40,1152]{2,1,0:T(8,128)S(1)}, u32[]{:S(2)}, u32[]{:S(2)}) %collective-permute-start.9) | collective-permute-done | bytes 737312 | tf_op jit(solution)/shard_map/at2_move_1/ppermute | solution.py:56
  253.9 12.5 %collective-permute-done.13 = f32[136,1152]{1,0:T(8,128)S(1)} collective-permute-done((f32[136,1152]{1,0:T(8,128)}, f32[136,1152]{1,0:T(8,128)S(1)}, u32[]{:S(2)}, u32[]{:S(2)}) %collective-permute-start.13) | collective-permute-done | bytes 626720 | tf_op jit(solution)/shard_map/ff_z_move/ppermute | solution.py:56
  302.7 5.6 %collective-permute-done.26 = f32[384,1152]{1,0:T(8,128)S(1)} collective-permute-done((f32[384,1152]{1,0:T(8,128)}, f32[384,1152]{1,0:T(8,128)S(1)}, u32[]{:S(2)}, u32[]{:S(2)}) %collective-permute-start.26) | collective-permute-done | bytes 1769504 | tf_op jit(solution)/shard_map/normed_move/ppermute | solution.py:60
  311.1 5.3 %collective-permute-start.27 = (f32[9,1152]{1,0:T(8,128)S(1)}, f32[9,1152]{1,0:T(8,128)S(1)}, u32[]{:S(2)}, u32[]{:S(2)}) collective-permute-start(f32[9,1152]{1,0:T(8,128)S(1)} %reshape.499), channel_id=1, source_target_pairs={{0,2},{2,0},{4,6},{6,4},{8,10},{10,8},{12,14},{14,12},{16,18},{18,... | collective-permute-start | bytes 124424 | tf_op jit(solution)/shard_map/small_move_core/ppermute | solution.py:56
  331.5 4.5 collective-permute-done.34
  336.1 17.5 %all-gather.2.cloned.1.call-done.refs_0_ = f32[2176,1152]{1,0:T(8,128)} async-done(((f32[136,1152]{1,0:T(8,128)}), f32[2176,1152]{1,0:T(8,128)}) %all-gather.2.cloned.1.call-update) | async-done | bytes 10027024 | tf_op jit(solution)/shard_map/ff_gather/all_gather | solution.py:622
  355.8 6.4 %collective-permute-done.37 = f32[9,1152]{1,0:T(8,128)S(1)} collective-permute-done((f32[9,1152]{1,0:T(8,128)S(1)}, f32[9,1152]{1,0:T(8,128)S(1)}, u32[]{:S(2)}, u32[]{:S(2)}) %collective-permute-start.37) | collective-permute-done | bytes 41504 | tf_op jit(solution)/shard_map/small_move_xa/ppermute | solution.py:56
  376.6 4.6 %collective-permute-done.44 = f32[9,1152]{1,0:T(8,128)S(1)} collective-permute-done((f32[9,1152]{1,0:T(8,128)S(1)}, f32[9,1152]{1,0:T(8,128)S(1)}, u32[]{:S(2)}, u32[]{:S(2)}) %collective-permute-start.44) | collective-permute-done | bytes 41504 | tf_op jit(solution)/shard_map/small_move_yb/ppermute | solution.py:56
  396.1 15.3 %shard_map.313 = (f32[2152,1152]{1,0:T(8,128)}, f32[2152,1152]{1,0:T(8,128)}) custom-call(s32[1]{0:T(128)} %bitcast.46.core_ref, f32[2176,1152]{1,0:T(8,128)S(1)} %copy-done.2, f32[2176,1152]{1,0:T(8,128)} %copy-done.18), custom_call_target="tpu_custom_call" | custom-call | bytes 39665664 | tf_op jit(solution)/shard_map/pallas_call | solution.py:332
  412.9 7.3 %collective-permute-start.51 = (f32[320,1152]{1,0:T(8,128)S(1)}, f32[320,1152]{1,0:T(8,128)}, u32[]{:S(2)}, u32[]{:S(2)}) collective-permute-start(f32[320,1152]{1,0:T(8,128)S(1)} %bitcast.140), channel_id=1, source_target_pairs={{0,2},{2,0},{4,6},{6,4},{8,10},{10,8},{12,14},{14,12},{16,18},{18,... | collective-permute-start | bytes 4423688 | tf_op jit(solution)/shard_map/at2_core/ppermute | solution.py:56
  432.7 7.2 %shard_map.314 = (f32[576,1152]{1,0:T(8,128)}, f32[576,1152]{1,0:T(8,128)}) custom-call(s32[1]{0:T(128)} %bitcast.46.core_ref, f32[320,1152]{1,0:T(8,128)S(1)} %bitcast.141, f32[320,1152]{1,0:T(8,128)} %collective-permute-done.51.refs_1_, f32[256,1152]{1,0:T(8,128)S(1)} %bitcast.143, f32[256,1152]{1,0:T(8,128)} %collective-permute-done.53.refs_3_), custom_call_target="tpu_custom_call" | custom-call | bytes 10616832 | tf_op jit(solution)/shard_map/pallas_call | solution.py:332
  439.8 8.0 %shard_map.315 = (f32[576,1152]{1,0:T(8,128)}, f32[576,1152]{1,0:T(8,128)}) custom-call(s32[1]{0:T(128)} %bitcast.46.core_ref, f32[320,1152]{1,0:T(8,128)} %bitcast.50.refs_0_, f32[320,1152]{1,0:T(8,128)} %collective-permute-done.55.refs_1_, f32[256,1152]{1,0:T(8,128)} %bitcast.51.refs_2_, f32[256,1152]{1,0:T(8,128)} %collective-permute-done.57.refs_3_), custom_call_target="tpu_custom_call" | custom-call | bytes 10616832 | tf_op jit(solution)/shard_map/pallas_call | solution.py:332
  (452 shorter events, 235.8 us)
Async XLA Ops:
  7.3 243.2 %reduce-scatter.4.cloned.1.call-start = ((), (), s32[]{:S(2)}) async-start(), calls=%async_computation.2 | async-start | bytes 10653696
  28.8 22.2 %collective-permute-start = (f32[192,1152]{1,0:T(8,128)}, f32[192,1152]{1,0:T(8,128)}, u32[]{:S(2)}, u32[]{:S(2)}) collective-permute-start(f32[192,1152]{1,0:T(8,128)} %fusion.59), channel_id=1, source_target_pairs={{0,1},{1,0},{2,3},{3,2},{4,5},{5,4},{6,7},{7,6},{8,9},{9,8},{10,11... | collective-permute-start | bytes 2654216 | tf_op jit(solution)/shard_map/branch_move_0/ppermute | solution.py:60
  32.9 37.1 %collective-permute-start.1 = (f32[192,1152]{1,0:T(8,128)}, f32[192,1152]{1,0:T(8,128)}, u32[]{:S(2)}, u32[]{:S(2)}) collective-permute-start(f32[192,1152]{1,0:T(8,128)} %fusion.60), channel_id=1, source_target_pairs={{0,1},{1,0},{2,3},{3,2},{4,5},{5,4},{6,7},{7,6},{8,9},{9,8},{10,11... | collective-permute-start | bytes 2654216 | tf_op jit(solution)/shard_map/branch_move_1/ppermute | solution.py:60
  86.4 15.1 %collective-permute-start.3 = (f32[1088,1152]{1,0:T(8,128)S(1)}, f32[1088,1152]{1,0:T(8,128)S(1)}, u32[]{:S(2)}, u32[]{:S(2)}) collective-permute-start(f32[1088,1152]{1,0:T(8,128)S(1)} %get-tuple-element.181), channel_id=1, source_target_pairs={{0,2},{2,0},{4,6},{6,4},{8,10},{10,8},{12,14},{14,12},{16,18},{18,... | collective-permute-start | bytes 15040520 | tf_op jit(solution)/shard_map/ff_core_move_1/ppermute | solution.py:56
  116.0 237.6 %all-gather.2.cloned.1.call-start = ((), (), s32[]{:S(2)}) async-start(), calls=%async_computation.1 | async-start | bytes 10653696 | tf_op jit(solution)/shard_map/ff_gather/all_gather | solution.py:622
  116.1 21.3 %collective-permute-start.4 = (f32[192,1152]{1,0:T(8,128)}, f32[192,1152]{1,0:T(8,128)}, u32[]{:S(2)}, u32[]{:S(2)}) collective-permute-start(f32[192,1152]{1,0:T(8,128)} %fusion.62), channel_id=1, source_target_pairs={{0,1},{1,0},{2,3},{3,2},{4,5},{5,4},{6,7},{7,6},{8,9},{9,8},{10,11... | collective-permute-start | bytes 2654216 | tf_op jit(solution)/shard_map/mid_move_0/ppermute | solution.py:60
  121.6 34.6 %collective-permute-start.5 = (f32[192,1152]{1,0:T(8,128)}, f32[192,1152]{1,0:T(8,128)}, u32[]{:S(2)}, u32[]{:S(2)}) collective-permute-start(f32[192,1152]{1,0:T(8,128)} %fusion.63), channel_id=1, source_target_pairs={{0,1},{1,0},{2,3},{3,2},{4,5},{5,4},{6,7},{7,6},{8,9},{9,8},{10,11... | collective-permute-start | bytes 2654216 | tf_op jit(solution)/shard_map/mid_move_1/ppermute | solution.py:60
  121.7 72.5 %collective-permute-start.6 = (f32[384,1152]{1,0:T(8,128)}, f32[384,1152]{1,0:T(8,128)}, u32[]{:S(2)}, u32[]{:S(2)}) collective-permute-start(f32[384,1152]{1,0:T(8,128)} %fusion.64), channel_id=1, source_target_pairs={{0,1},{1,0},{2,3},{3,2},{4,5},{5,4},{6,7},{7,6},{8,9},{9,8},{10,11... | collective-permute-start | bytes 5308424 | tf_op jit(solution)/shard_map/output_move/ppermute | solution.py:60
  224.1 25.5 %collective-permute-start.12 = (f32[4,32,1152]{2,1,0:T(8,128)S(1)}, f32[4,32,1152]{2,1,0:T(8,128)S(1)}, u32[]{:S(2)}, u32[]{:S(2)}) collective-permute-start(f32[4,32,1152]{2,1,0:T(8,128)S(1)} %bitcast.150), channel_id=1, source_target_pairs={{0,4},{2,6},{4,0},{6,2},{8,12},{10,14},{12,8},{14,10},{16,20},{18,... | collective-permute-start | bytes 1769480 | tf_op jit(solution)/shard_map/at1_move_1/ppermute | solution.py:56
  225.5 23.1 %collective-permute-start.11 = (f32[4,40,1152]{2,1,0:T(8,128)S(1)}, f32[4,40,1152]{2,1,0:T(8,128)S(1)}, u32[]{:S(2)}, u32[]{:S(2)}) collective-permute-start(f32[4,40,1152]{2,1,0:T(8,128)S(1)} %bitcast.148), channel_id=1, source_target_pairs={{0,16},{2,18},{4,20},{6,22},{8,24},{10,26},{12,28},{14,30},{16,0},... | collective-permute-start | bytes 2211848 | tf_op jit(solution)/shard_map/at0_move_1/ppermute | solution.py:56
  226.7 21.0 %collective-permute-start.10 = (f32[4,32,1152]{2,1,0:T(8,128)S(1)}, f32[4,32,1152]{2,1,0:T(8,128)S(1)}, u32[]{:S(2)}, u32[]{:S(2)}) collective-permute-start(f32[4,32,1152]{2,1,0:T(8,128)S(1)} %bitcast.151), channel_id=1, source_target_pairs={{0,12},{2,14},{4,8},{6,10},{8,4},{10,6},{12,0},{14,2},{16,28},{18,... | collective-permute-start | bytes 1769480 | tf_op jit(solution)/shard_map/at3_move_1/ppermute | solution.py:56
  228.6 18.1 %collective-permute-start.9 = (f32[4,40,1152]{2,1,0:T(8,128)S(1)}, f32[4,40,1152]{2,1,0:T(8,128)S(1)}, u32[]{:S(2)}, u32[]{:S(2)}) collective-permute-start(f32[4,40,1152]{2,1,0:T(8,128)S(1)} %bitcast.149), channel_id=1, source_target_pairs={{0,48},{2,50},{4,52},{6,54},{8,56},{10,58},{12,60},{14,62},{16,32}... | collective-permute-start | bytes 2211848 | tf_op jit(solution)/shard_map/at2_move_1/ppermute | solution.py:56
  250.5 15.9 %collective-permute-start.13 = (f32[136,1152]{1,0:T(8,128)}, f32[136,1152]{1,0:T(8,128)S(1)}, u32[]{:S(2)}, u32[]{:S(2)}) collective-permute-start(f32[136,1152]{1,0:T(8,128)} %reduce-scatter.4.cloned.1.call-done), channel_id=1, source_target_pairs={{0,64},{2,66},{4,68},{6,70},{8,72},{10,74},{12,76},{14,78},{16,80}... | collective-permute-start | bytes 1880072 | tf_op jit(solution)/shard_map/ff_z_move/ppermute | solution.py:56
  271.0 37.3 %collective-permute-start.26 = (f32[384,1152]{1,0:T(8,128)}, f32[384,1152]{1,0:T(8,128)S(1)}, u32[]{:S(2)}, u32[]{:S(2)}) collective-permute-start(f32[384,1152]{1,0:T(8,128)} %convolution_add_fusion.2), channel_id=1, source_target_pairs={{0,1},{1,0},{2,3},{3,2},{4,5},{5,4},{6,7},{7,6},{8,9},{9,8},{10,11... | collective-permute-start | bytes 5308424 | tf_op jit(solution)/shard_map/normed_move/ppermute | solution.py:60
  299.3 19.7 %collective-permute-start.28 = (f32[1,20,1152]{2,1,0:T(8,128)S(1)}, f32[1,20,1152]{2,1,0:T(8,128)S(1)}, u32[]{:S(2)}, u32[]{:S(2)}) collective-permute-start(f32[1,20,1152]{2,1,0:T(8,128)S(1)} %add.430), channel_id=1, source_target_pairs={{0,64},{2,66},{4,68},{6,70},{8,72},{10,74},{12,76},{14,78},{16,80}... | collective-permute-start | bytes 276488 | tf_op jit(solution)/shard_map/at2_move_5/ppermute | solution.py:56
  353.6 34.9 %collective-permute-start.49 = (f32[2176,1152]{1,0:T(8,128)}, f32[2176,1152]{1,0:T(8,128)S(1)}, u32[]{:S(2)}, u32[]{:S(2)}) collective-permute-start(f32[2176,1152]{1,0:T(8,128)} %all-gather.2.cloned.1.call-done.refs_0_), channel_id=1, source_target_pairs={{0,2},{2,0},{4,6},{6,4},{8,10},{10,8},{12,14},{14,12},{16,18},{18,... | collective-permute-start | bytes 30081032 | tf_op jit(solution)/shard_map/ff_core_back/ppermute | solution.py:56
  354.3 12.8 %collective-permute-start.39 = (f32[1,40,1152]{2,1,0:T(8,128)S(1)}, f32[1,40,1152]{2,1,0:T(8,128)S(1)}, u32[]{:S(2)}, u32[]{:S(2)}) collective-permute-start(f32[1,40,1152]{2,1,0:T(8,128)S(1)} %maximum_select_fusion.12), channel_id=1, source_target_pairs={{0,16},{2,18},{4,20},{6,22},{8,24},{10,26},{12,28},{14,30},{16,0},... | collective-permute-start | bytes 552968 | tf_op jit(solution)/shard_map/at2_move_7/ppermute | solution.py:56
  369.1 15.1 %collective-permute-start.45 = (f32[2,40,1152]{2,1,0:T(8,128)S(1)}, f32[2,40,1152]{2,1,0:T(8,128)S(1)}, u32[]{:S(2)}, u32[]{:S(2)}) collective-permute-start(f32[2,40,1152]{2,1,0:T(8,128)S(1)} %maximum_select_fusion.8), channel_id=1, source_target_pairs={{0,12},{2,14},{4,8},{6,10},{8,4},{10,6},{12,0},{14,2},{16,28},{18,... | collective-permute-start | bytes 1105928 | tf_op jit(solution)/shard_map/at2_move_8/ppermute | solution.py:56
  384.3 27.1 %collective-permute-start.50 = (f32[4,40,1152]{2,1,0:T(8,128)S(1)}, f32[4,40,1152]{2,1,0:T(8,128)}, u32[]{:S(2)}, u32[]{:S(2)}) collective-permute-start(f32[4,40,1152]{2,1,0:T(8,128)S(1)} %maximum_select_fusion.4), channel_id=1, source_target_pairs={{0,48},{2,50},{4,52},{6,54},{8,56},{10,58},{12,60},{14,62},{16,32}... | collective-permute-start | bytes 2211848 | tf_op jit(solution)/shard_map/at2_move_9/ppermute | solution.py:56
  384.4 35.7 %collective-permute-start.52 = (f32[4,32,1152]{2,1,0:T(8,128)S(1)}, f32[4,32,1152]{2,1,0:T(8,128)}, u32[]{:S(2)}, u32[]{:S(2)}) collective-permute-start(f32[4,32,1152]{2,1,0:T(8,128)S(1)} %maximum_select_fusion.6), channel_id=1, source_target_pairs={{0,12},{2,14},{4,8},{6,10},{8,4},{10,6},{12,0},{14,2},{16,28},{18,... | collective-permute-start | bytes 1769480 | tf_op jit(solution)/shard_map/at3_move_9/ppermute | solution.py:56
  385.3 36.4 %collective-permute-start.54 = (f32[4,40,1152]{2,1,0:T(8,128)S(1)}, f32[4,40,1152]{2,1,0:T(8,128)}, u32[]{:S(2)}, u32[]{:S(2)}) collective-permute-start(f32[4,40,1152]{2,1,0:T(8,128)S(1)} %maximum_select_fusion.5), channel_id=1, source_target_pairs={{0,16},{2,18},{4,20},{6,22},{8,24},{10,26},{12,28},{14,30},{16,0},... | collective-permute-start | bytes 2211848 | tf_op jit(solution)/shard_map/at0_move_9/ppermute | solution.py:56
  388.4 36.6 %collective-permute-start.56 = (f32[4,32,1152]{2,1,0:T(8,128)S(1)}, f32[4,32,1152]{2,1,0:T(8,128)}, u32[]{:S(2)}, u32[]{:S(2)}) collective-permute-start(f32[4,32,1152]{2,1,0:T(8,128)S(1)} %maximum_select_fusion.7), channel_id=1, source_target_pairs={{0,4},{2,6},{4,0},{6,2},{8,12},{10,14},{12,8},{14,10},{16,20},{18,... | collective-permute-start | bytes 1769480 | tf_op jit(solution)/shard_map/at1_move_9/ppermute | solution.py:56
  412.9 18.5 %collective-permute-start.51 = (f32[320,1152]{1,0:T(8,128)S(1)}, f32[320,1152]{1,0:T(8,128)}, u32[]{:S(2)}, u32[]{:S(2)}) collective-permute-start(f32[320,1152]{1,0:T(8,128)S(1)} %bitcast.140), channel_id=1, source_target_pairs={{0,2},{2,0},{4,6},{6,4},{8,10},{10,8},{12,14},{14,12},{16,18},{18,... | collective-permute-start | bytes 4423688 | tf_op jit(solution)/shard_map/at2_core/ppermute | solution.py:56
  424.6 15.2 %collective-permute-start.55 = (f32[320,1152]{1,0:T(8,128)}, f32[320,1152]{1,0:T(8,128)}, u32[]{:S(2)}, u32[]{:S(2)}) collective-permute-start(f32[320,1152]{1,0:T(8,128)} %bitcast.50.refs_0_), channel_id=1, source_target_pairs={{0,2},{2,0},{4,6},{6,4},{8,10},{10,8},{12,14},{14,12},{16,18},{18,... | collective-permute-start | bytes 4423688 | tf_op jit(solution)/shard_map/at0_core/ppermute | solution.py:56
  (134 other events, 1084.6 us)
Sparse Core Ops, SparseCore 0:
  116.1 92.9 reduce-scatter.3
  268.5 85.0 all-gather.1

commit v3 on v1

v3 whole, which is shorter than its diff:
```python
import jax
import jax.numpy as jnp
from jax import lax
from jax.experimental import pallas as pl
from jax.experimental.pallas import tpu as pltpu
from jax.sharding import PartitionSpec as P

HEAD = 72
norm_epsilon = 1e-06


def partner_pairs(move):
    pairs = []
    for place in range(64):
        z_hi, x, y, core = place >> 5, (place >> 3) & 3, (place >> 1) & 3, place & 1
        z_hi, x, y, core = move(z_hi, x, y, core)
        pairs.append((place, ((z_hi * 4 + x) * 4 + y) * 2 + core))
    return pairs


PAIRS = {
    "core": partner_pairs(lambda z, x, y, c: (z, x, y, 1 - c)),
    "xa": partner_pairs(lambda z, x, y, c: (z, x ^ 1, y, c)),
    "xb": partner_pairs(lambda z, x, y, c: (z, x ^ 3, y, c)),
    "ya": partner_pairs(lambda z, x, y, c: (z, x, y ^ 1, c)),
    "yb": partner_pairs(lambda z, x, y, c: (z, x, y ^ 3, c)),
    "z": partner_pairs(lambda z, x, y, c: (1 - z, x, y, c)),
}
PLANES = [
    [((z_hi * 4 + x) * 4 + y) * 2 + core for x in range(4) for y in range(4)]
    for z_hi in range(2)
    for core in range(2)
]
ORDERS = (
    ("xa", "ya", "xb", "yb"),
    ("ya", "xb", "yb", "xa"),
    ("xb", "yb", "xa", "ya"),
    ("yb", "xa", "ya", "xb"),
)


def sides():
    place = lax.axis_index("dp")
    x = (place >> 3) & 3
    y = (place >> 1) & 3
    return {
        "core": place & 1,
        "xa": (x ^ (x >> 1)) & 1,
        "xb": x >> 1,
        "ya": (y ^ (y >> 1)) & 1,
        "yb": y >> 1,
    }


def swap(values, pair):
    return lax.ppermute(values, "dp", PAIRS[pair])


def swap_tensor(values):
    return lax.ppermute(values, "tensor", [(0, 1), (1, 0)])


class Cell:
    def __init__(self, value):
        self.value = value


class Order:
    def __init__(self):
        self.last = None

    def run(self, operation, ready):
        if self.last is not None:
            self.last.value, ready = lax.optimization_barrier((self.last.value, ready))
        self.last = Cell(operation(ready))
        return self.last

    def settle(self, value):
        self.last.value, value = lax.optimization_barrier((self.last.value, value))
        return value


def half_of(values, side):
    count = values.shape[0] // 2
    return lax.dynamic_slice_in_dim(values, side * count, count, 0)


def row_half_of(values, side):
    count = values.shape[1] // 2
    return jnp.where(side == 0, values[:, :count], values[:, count:])


def joined(own, received, side, axis):
    return jnp.where(
        side == 0,
        jnp.concatenate([own, received], axis),
        jnp.concatenate([received, own], axis),
    )


class Stream:
    def __init__(self, name, order, pairs, side):
        self.name = name
        self.order = order
        self.pairs = pairs
        self.side = side
        self.stage = 0
        self.keep = None
        self.sent = None

    def begin(self, send, keep):
        four = (4, send.shape[0] // 4, send.shape[1])
        self.sent = Cell(send.reshape(four))
        self.order.last = self.sent
        self.keep = keep.reshape(four)
        self.stage = 1

    def moved(self):
        pairs = self.pairs
        stage = self.stage
        with jax.named_scope(self.name + "_move_" + str(stage)):
            if stage <= 4:
                return swap(self.sent.value, pairs[stage - 1])
            if stage == 5:
                return swap(self.sent.value, "z")
            return swap(self.sent.value, pairs[9 - stage])

    def step(self, received):
        pairs = self.pairs
        stage = self.stage
        self.stage += 1
        keep = self.keep
        with jax.named_scope(self.name + "_sum_" + str(stage)):
            if stage <= 3:
                take = half_of if stage < 3 else row_half_of
                side = self.side[pairs[stage]]
                self.keep = take(keep, side) + take(received, side)
                self.sent = self.order.run(
                    lambda ready: take(ready, 1 - side) + take(received, 1 - side), keep
                )
            elif stage == 4:
                self.sent = self.order.run(lambda ready: ready + received, keep)
            elif stage == 5:
                self.sent = self.order.run(lambda ready: ready + received, self.sent.value)
            else:
                axis = 1 if stage == 6 else 0
                pair = pairs[9 - stage]
                self.sent = self.order.run(
                    lambda ready: joined(ready, received, self.side[pair], axis), self.sent.value
                )

    def halves(self):
        here = self.sent.value
        flat = (-1, here.shape[2])
        return here.reshape(flat), self.moved().reshape(flat)


def pick_rows(core, own, other, rows, block, skipped, first, total, kept=()):
    columns = own.shape[1]
    before, start = skipped // block, first // block

    def kernel(core_ref, own_ref, other_ref, *refs):
        first_ref, second_ref = refs[-2:]

        @pl.when(core_ref[0] == 0)
        def _():
            first_ref[...] = own_ref[...]
            second_ref[...] = other_ref[...]

        @pl.when(core_ref[0] != 0)
        def _():
            first_ref[...] = other_ref[...]
            second_ref[...] = own_ref[...]

    shape = jax.ShapeDtypeStruct((total, columns), jnp.float32)
    in_spec = pl.BlockSpec((block, columns), lambda i, core_ref: (before + i, 0))
    out_spec = pl.BlockSpec((block, columns), lambda i, core_ref: (start + i, 0))
    return pl.pallas_call(
        kernel,
        grid_spec=pltpu.PrefetchScalarGridSpec(
            num_scalar_prefetch=1,
            grid=(-(-rows // block),),
            in_specs=[in_spec, in_spec] + [pl.BlockSpec(memory_space=pl.ANY)] * len(kept),
            out_specs=(out_spec, out_spec),
        ),
        out_shape=(shape, shape),
        input_output_aliases={3 + number: number for number in range(len(kept))},
        compiler_params=limit(20),
        cost_estimate=estimate(0.02),
    )(core.reshape(1), own, other, *kept)


def pick_halves(core, sides, pieces, rows, first, before):
    half, columns = pieces[0].shape
    block = half // 2
    start = first // block

    def kernel(core_ref, sides_ref, *refs):
        first_ref, second_ref = refs[-2:]
        here = (pl.program_id(0) // 2) == sides_ref[0]
        for other in range(2):
            own_ref, far_ref = refs[other], refs[2 + other]
            chosen = here if other == 0 else jnp.logical_not(here)

            @pl.when(chosen & (core_ref[0] == 0))
            def _():
                first_ref[...] = own_ref[...]
                second_ref[...] = far_ref[...]

            @pl.when(chosen & (core_ref[0] != 0))
            def _():
                first_ref[...] = far_ref[...]
                second_ref[...] = own_ref[...]

    def place(other):
        def index(i, core_ref, sides_ref):
            side = sides_ref[0] if other == 0 else 1 - sides_ref[0]
            return (jnp.clip(i - side * 2, 0, 1), 0)

        return pl.BlockSpec((block, columns), index)

    shape = jax.ShapeDtypeStruct((rows, columns), jnp.float32)
    out_spec = pl.BlockSpec((block, columns), lambda i, core_ref, sides_ref: (start + i, 0))
    steps = min(4, -(-(rows - first) // block))
    kept = [] if before is None else list(before)
    return pl.pallas_call(
        kernel,
        grid_spec=pltpu.PrefetchScalarGridSpec(
            num_scalar_prefetch=2,
            grid=(steps,),
            in_specs=[place(other) for other in (0, 1, 0, 1)]
            + [pl.BlockSpec(memory_space=pl.ANY)] * len(kept),
            out_specs=(out_spec, out_spec),
        ),
        out_shape=(shape, shape),
        input_output_aliases={6 + number: number for number in range(len(kept))},
        compiler_params=limit(20),
        cost_estimate=estimate(0.02),
    )(core.reshape(1), sides, *pieces, *kept)


GELU_SCALE = (2.0 / 3.141592653589793) ** 0.5


def across(left, right):
    return lax.dot_general(
        left, right, (((1,), (1,)), ((), ())), preferred_element_type=jnp.float32
    )


def inner_rows(left, right):
    return lax.dot_general(
        left, right, (((0,), (0,)), ((), ())), preferred_element_type=jnp.float32
    )


def product(left, right):
    return jnp.dot(left, right, preferred_element_type=jnp.float32)


def normalized(values):
    center = values - jnp.mean(values, axis=-1, keepdims=True)
    spread = jnp.mean(center * center, axis=-1, keepdims=True)
    factor = lax.rsqrt(spread + norm_epsilon)
    return center * factor, factor


def norm_back(grad, normal, factor, gain):
    scaled = grad * gain
    mean_scaled = jnp.mean(scaled, axis=-1, keepdims=True)
    mean_normal = jnp.mean(scaled * normal, axis=-1, keepdims=True)
    return factor * (scaled - mean_scaled - normal * mean_normal)


def same_segment(layout_ref, row, length):
    def segment(axis):
        places = lax.broadcasted_iota(jnp.int32, (length, length), axis)
        total = jnp.zeros((length, length), jnp.int32)
        bound = 0
        for picture in range(3):
            bound = bound + layout_ref[row, picture]
            total = total + (places >= bound).astype(jnp.int32)
        return total

    return segment(0) == segment(1)


def head_probs(query, key, same):
    scores = inner_rows(query, key) * (HEAD ** (-0.5))
    scores = jnp.where(same, scores, -1000000000.0)
    exponent = jnp.exp(scores - jnp.max(scores, axis=-1, keepdims=True))
    return exponent / jnp.sum(exponent, axis=-1, keepdims=True)


def as_column(vector):
    return jnp.broadcast_to(vector[None, :], (8, vector.shape[0])).T[:, 0:1]


def lanes(count):
    return -(-count // 128) * 128


def whole(shape):
    return pl.BlockSpec(shape, lambda *_: (0,) * len(shape))


def scalars():
    return pl.BlockSpec(memory_space=pltpu.SMEM)


def estimate(microseconds):
    return pl.CostEstimate(
        flops=int(microseconds * 1.15e9), bytes_accessed=1024, transcendentals=0
    )


def limit(mebibytes):
    return pltpu.CompilerParams(vmem_limit_bytes=mebibytes * 1024 * 1024)


def low(values):
    return values.astype(jnp.bfloat16)


def attention_forward(row, layout, hidden, gain, shift, wq, bq, wk, wv, bv, wo):
    _, length, width = hidden.shape
    wide = wq.shape[0]

    def kernel(
        layout_ref, hidden_ref, gain_ref, shift_ref, wq_ref, bq_ref, wk_ref, wv_ref, bv_ref,
        wo_ref, normed_ref, q_ref, k_ref, v_ref, att_ref, branch_ref, normed_send_ref, att_send_ref,
    ):
        normal, _ = normalized(hidden_ref[0].astype(jnp.float32))
        normed = low(normal * gain_ref[...][None, :] + shift_ref[...][None, :])
        normed_ref[...] = normed
        normed_send_ref[...] = normed.astype(jnp.float32)
        queries = low(across(wq_ref[...], normed) + as_column(bq_ref[...]))
        keys = low(across(wk_ref[...], normed))
        values = low(across(wv_ref[...], normed) + as_column(bv_ref[...]))
        q_ref[...] = queries
        k_ref[...] = keys
        v_ref[...] = values
        queries, keys, values = (part.astype(jnp.float32) for part in (queries, keys, values))
        same = same_segment(layout_ref, row, length)
        parts = []
        for head in range(wide // HEAD):
            rows = slice(head * HEAD, (head + 1) * HEAD)
            probs = head_probs(low(queries[rows]), low(keys[rows]), same)
            parts.append(across(low(values[rows]), low(probs)))
        attended = low(jnp.concatenate(parts, 0))
        att_ref[...] = attended
        att_send_ref[:, :length] = attended.astype(jnp.float32)
        att_send_ref[:, length:] = jnp.zeros((wide, lanes(length) - length), jnp.float32)
        branch_ref[...] = inner_rows(attended, wo_ref[...])

    turned = jax.ShapeDtypeStruct((wide, length), jnp.bfloat16)
    return pl.pallas_call(
        kernel,
        grid=(1,),
        in_specs=[
            scalars(),
            pl.BlockSpec((1, length, width), lambda i: (row, 0, 0)),
            whole((width,)),
            whole((width,)),
            whole((wide, width)),
            whole((wide,)),
            whole((wide, width)),
            whole((wide, width)),
            whole((wide,)),
            whole((wide, width)),
        ],
        out_specs=[whole((length, width))]
        + [whole((wide, length))] * 4
        + [whole((length, width))] * 2
        + [whole((wide, lanes(length)))],
        out_shape=[
            jax.ShapeDtypeStruct((length, width), jnp.bfloat16),
            turned,
            turned,
            turned,
            turned,
            jax.ShapeDtypeStruct((length, width), jnp.float32),
            jax.ShapeDtypeStruct((length, width), jnp.float32),
            jax.ShapeDtypeStruct((wide, lanes(length)), jnp.float32),
        ],
        compiler_params=limit(56),
        cost_estimate=estimate(20),
    )(layout, hidden, gain, shift, wq, bq, wk, wv, bv, wo)


def attention_backward(row, core, layout, part, received, resid, cotangent, gain, q, k, v, wo):
    _, length, width = cotangent.shape
    wide = wo.shape[0]

    def kernel(
        core_ref, layout_ref, part_ref, received_ref, resid_ref, cot_ref, gain_ref, q_ref, k_ref, v_ref,
        wo_ref, resid_grad_ref, branch_grad_ref, terms_ref, dq_ref, dk_ref, dv_ref, send_ref,
        branch_send_ref,
    ):
        mid_grad = part_ref[...] + received_ref[...]
        normal, factor = normalized(resid_ref[...])
        terms_ref[0:1, :] = jnp.sum(mid_grad * normal, axis=0, keepdims=True)
        terms_ref[1:2, :] = jnp.sum(mid_grad, axis=0, keepdims=True)
        resid_grad = cot_ref[0].astype(jnp.float32) + norm_back(
            mid_grad, normal, factor, gain_ref[...][None, :]
        )
        resid_grad_ref[...] = resid_grad
        branch_grad = low(resid_grad)
        branch_grad_ref[...] = branch_grad
        branch_send_ref[...] = branch_grad.astype(jnp.float32)
        terms_ref[2:3, :] = jnp.sum(branch_grad.astype(jnp.float32), axis=0, keepdims=True)
        terms_ref[3:8, :] = jnp.zeros((5, width), jnp.float32)
        back = low(across(wo_ref[...], branch_grad)).astype(jnp.float32)
        same = same_segment(layout_ref, row, length)
        queries, keys, values = (
            ref[...].astype(jnp.float32) for ref in (q_ref, k_ref, v_ref)
        )
        dq, dk, dv = [], [], []
        for head in range(wide // HEAD):
            rows = slice(head * HEAD, (head + 1) * HEAD)
            query, key, value, grad = (
                low(member[rows]) for member in (queries, keys, values, back)
            )
            probs = head_probs(query, key, same)
            dv.append(product(grad, low(probs)))
            prob_grad = inner_rows(grad, value)
            inside = prob_grad - jnp.sum(prob_grad * probs, axis=-1, keepdims=True)
            score_grad = low(probs * inside)
            dq.append(across(key, score_grad) * (HEAD ** (-0.5)))
            dk.append(product(query, score_grad) * (HEAD ** (-0.5)))
        dq, dk, dv = (low(jnp.concatenate(parts, 0)) for parts in (dq, dk, dv))
        dq_ref[...] = dq
        dk_ref[...] = dk
        dv_ref[...] = dv
        send_ref[: 2 * wide, length:] = jnp.zeros((2 * wide, lanes(length) - length), jnp.float32)
        send_ref[wide : 2 * wide, :length] = dk.astype(jnp.float32)

        @pl.when(core_ref[0] == 0)
        def _():
            send_ref[:wide, :length] = dv.astype(jnp.float32)

        @pl.when(core_ref[0] != 0)
        def _():
            send_ref[:wide, :length] = dq.astype(jnp.float32)

    turned = jax.ShapeDtypeStruct((wide, length), jnp.bfloat16)
    return pl.pallas_call(
        kernel,
        grid=(1,),
        in_specs=[scalars(), scalars()]
        + [pl.BlockSpec((length, width), lambda i: (row, 0))] * 2
        + [whole((length, width))]
        + [pl.BlockSpec((1, length, width), lambda i: (row, 0, 0)), whole((width,))]
        + [whole((wide, length))] * 3
        + [whole((wide, width))],
        out_specs=[whole((length, width)), whole((length, width)), whole((8, width))]
        + [whole((wide, length))] * 3
        + [whole((2 * wide, lanes(length))), whole((length, width))],
        out_shape=[
            jax.ShapeDtypeStruct((length, width), jnp.float32),
            jax.ShapeDtypeStruct((length, width), jnp.bfloat16),
            jax.ShapeDtypeStruct((8, width), jnp.float32),
            turned,
            turned,
            turned,
            jax.ShapeDtypeStruct((2 * wide, lanes(length)), jnp.float32),
            jax.ShapeDtypeStruct((length, width), jnp.float32),
        ],
        compiler_params=limit(56),
        cost_estimate=estimate(0.02),
    )(core.reshape(1), layout, part, received, resid, cotangent, gain, q, k, v, wo)


def feed_forward(
    row, core, hidden, branch, received, out_bias, gain, shift, up, up_bias, down, cotangent,
    mid_parts=None,
):
    _, length, width = hidden.shape
    units = up.shape[0]
    kept = [] if mid_parts is None else [mid_parts]
    block = 576
    steps = -(-units // block)

    def kernel(
        core_ref, hidden_ref, branch_ref, received_ref, out_bias_ref, gain_ref, shift_ref, up_ref,
        up_bias_ref, down_ref, cot_ref, *refs,
    ):
        resid_ref, middle_ref, pair_ref, mid_part_ref, out_part_ref = refs[-7:-2]
        left_send_ref, right_send_ref = refs[-2:]
        step = pl.program_id(0)
        first_core = core_ref[0] == 0

        @pl.when(step == 0)
        def _():
            resid = hidden_ref[0].astype(jnp.float32) + (
                (branch_ref[...] + received_ref[...]) + out_bias_ref[...][None, :]
            )
            resid_ref[...] = resid
            normal, _ = normalized(resid)
            middle = low(normal * gain_ref[...][None, :] + shift_ref[...][None, :])
            middle_ref[...] = middle
            mid_part_ref[...] = jnp.zeros((length, width), jnp.float32)
            out_part_ref[...] = jnp.zeros((length, width), jnp.float32)

            @pl.when(first_core)
            def _():
                right_send_ref[...] = middle.astype(jnp.float32)

            @pl.when(jnp.logical_not(first_core))
            def _():
                right_send_ref[...] = cot_ref[0].astype(jnp.float32)

        def work(up_here, down_here, up_bias_here):
            act = across(up_here, middle_ref[...]) + up_bias_here
            act_grad = across(down_here, cot_ref[0])
            curve = jnp.tanh(GELU_SCALE * (act + 0.044715 * (act * act * act)))
            activ = low(0.5 * act * (1.0 + curve))
            slope = 0.5 * (1.0 + curve) + 0.5 * act * (1.0 - curve * curve) * (
                GELU_SCALE * (1.0 + 3.0 * 0.044715 * (act * act))
            )
            pre_grad = low(act_grad * slope)
            pair_ref[0] = activ
            pair_ref[1] = pre_grad
            left_send_ref[:, length:] = jnp.zeros((block, lanes(length) - length), jnp.float32)
            mid_part_ref[...] += inner_rows(pre_grad, up_here)
            out_part_ref[...] += inner_rows(activ, down_here)

            @pl.when(first_core)
            def _():
                left_send_ref[:, :length] = pre_grad.astype(jnp.float32)

            @pl.when(jnp.logical_not(first_core))
            def _():
                left_send_ref[:, :length] = activ.astype(jnp.float32)

        @pl.when(step < steps - 1)
        def _():
            work(up_ref[...], down_ref[...], up_bias_ref[...])

        @pl.when(step == steps - 1)
        def _():
            here = step * block + lax.broadcasted_iota(jnp.int32, (block, width), 0)
            inside = here < units
            work(
                low(jnp.where(inside, up_ref[...].astype(jnp.float32), 0.0)),
                low(jnp.where(inside, down_ref[...].astype(jnp.float32), 0.0)),
                jnp.where(inside[:, :1], up_bias_ref[...], 0.0),
            )

    flat = jax.ShapeDtypeStruct((length, width), jnp.float32)
    at_row = pl.BlockSpec((1, length, width), lambda i: (row, 0, 0))
    return pl.pallas_call(
        kernel,
        grid=(steps,),
        in_specs=[scalars(), at_row]
        + [whole((length, width))] * 2
        + [whole((width,))] * 3
        + [
            pl.BlockSpec((block, width), lambda i: (i, 0)),
            pl.BlockSpec((block, 1), lambda i: (i, 0)),
            pl.BlockSpec((block, width), lambda i: (i, 0)),
            at_row,
        ]
        + [pl.BlockSpec(memory_space=pl.ANY)] * len(kept),
        out_specs=[
            whole((length, width)),
            whole((length, width)),
            pl.BlockSpec((2, block, length), lambda i: (0, i, 0)),
            pl.BlockSpec((length, width), lambda i: (row, 0)),
            whole((length, width)),
            pl.BlockSpec((block, lanes(length)), lambda i: (i, 0)),
            whole((length, width)),
        ],
        out_shape=[
            flat,
            jax.ShapeDtypeStruct((length, width), jnp.bfloat16),
            jax.ShapeDtypeStruct((2, steps * block, length), jnp.bfloat16),
            jax.ShapeDtypeStruct((hidden.shape[0] * length, width), jnp.float32),
            flat,
            jax.ShapeDtypeStruct((steps * block, lanes(length)), jnp.float32),
            flat,
        ],
        input_output_aliases={11 + number: 3 for number in range(len(kept))},
        compiler_params=limit(56),
        cost_estimate=estimate(30),
    )(
        core.reshape(1), hidden, branch, received, out_bias, gain, shift, up, up_bias, down,
        cotangent, *kept,
    )


def ff_own(core, sides, pairs, cotangent, middles, lefts, rights, counts, base):
    rows = len(pairs)
    length, columns = middles[0].shape
    streams = len(counts)
    units = sum(counts)
    firsts = [sum(counts[:number]) for number in range(streams)]
    part = base // units

    def kernel(core_ref, sides_ref, *refs):
        pair_refs = refs[:rows]
        cot_ref = refs[rows]
        middle_refs = refs[rows + 1 : 2 * rows + 1]
        left_refs = refs[2 * rows + 1 : 3 * rows + 1]
        right_refs = refs[3 * rows + 1 : 4 * rows + 1]
        out_refs = refs[4 * rows + 1 : 4 * rows + 1 + 2 * streams]
        own_ref, other_ref = refs[4 * rows + 1 + 2 * streams :]
        step = pl.program_id(0)

        @pl.when(step == 0)
        def _():
            for row in range(rows):
                other_ref[row] = low(right_refs[row][...])

        @pl.when((step == 0) & (core_ref[0] == 0))
        def _():
            for row in range(rows):
                own_ref[row] = cot_ref[row]

        @pl.when((step == 0) & (core_ref[0] != 0))
        def _():
            for row in range(rows):
                own_ref[row] = middle_refs[row][...]

        for number in range(streams):
            half = counts[number] // 2
            for keep in range(2):

                @pl.when(step == keep * streams + number)
                def _():
                    here = sides_ref[number] if keep else 1 - sides_ref[number]
                    here = pl.ds(pl.multiple_of(firsts[number] + here * half, 16), half)
                    total = product(pair_refs[0][0, here, :], own_ref[0])
                    for row in range(1, rows):
                        total = total + product(pair_refs[row][0, here, :], own_ref[row])
                    for row in range(rows):
                        left = low(left_refs[row][here, :length])
                        total = total + product(left, other_ref[row])
                    out_refs[2 * number + keep][...] = total

    shapes = [
        jax.ShapeDtypeStruct((count // 2, columns), jnp.float32)
        for count in counts
        for _ in range(2)
    ]
    return pl.pallas_call(
        kernel,
        grid_spec=pltpu.PrefetchScalarGridSpec(
            num_scalar_prefetch=2,
            grid=(2 * streams,),
            in_specs=[
                pl.BlockSpec((1, units, length), lambda step, core_ref, _: (core_ref[0], part, 0))
            ]
            * rows
            + [whole(cotangent.shape)]
            + [whole((length, columns))] * rows
            + [pl.BlockSpec((units, lanes(length)), lambda step, core_ref, _: (part, 0))] * rows
            + [whole((length, columns))] * rows,
            out_specs=[whole(shape.shape) for shape in shapes],
            scratch_shapes=[pltpu.VMEM((rows, length, columns), jnp.bfloat16)] * 2,
        ),
        out_shape=shapes,
        compiler_params=limit(56),
        cost_estimate=estimate(4),
    )(core.reshape(1), sides, *pairs, cotangent, *middles, *lefts, *rights)


def attention_own(core, dq, dk, dv, attended, normed, branch_grad, early, late):
    rows = len(dq)
    wide, length = dq[0].shape
    columns = normed[0].shape[1]
    piece = wide // 2

    def kernel(core_ref, *refs):
        groups = [refs[rows * number : rows * (number + 1)] for number in range(10)]
        dq_refs, dk_refs, dv_refs, attended_refs, normed_refs, branch_refs = groups[:6]
        early_normed, early_attended, late_refs, late_branch = groups[6:]
        out_ref = refs[10 * rows]
        step = pl.program_id(0)
        first_core = core_ref[0] == 0
        late_step = step >= 2

        def store(lefts, rights, other_lefts, other_rights):
            total = product(lefts[0][...], rights[0][...])
            for row in range(1, rows):
                total = total + product(lefts[row][...], rights[row][...])
            for row in range(rows):
                total = total + product(low(other_lefts[row]), low(other_rights[row]))
            out_ref[...] = total

        late_left = [
            ref[pl.ds(pl.multiple_of(step * piece, 16), piece), :length] for ref in late_refs
        ]

        @pl.when(jnp.logical_not(late_step) & first_core)
        def _():
            store(dq_refs, normed_refs, late_left, [ref[...] for ref in early_normed])

        @pl.when(late_step & first_core)
        def _():
            store(dk_refs, normed_refs, late_left, [ref[...] for ref in early_normed])

        @pl.when(jnp.logical_not(late_step) & jnp.logical_not(first_core))
        def _():
            store(dv_refs, normed_refs, late_left, [ref[...] for ref in early_normed])

        @pl.when(late_step & jnp.logical_not(first_core))
        def _():
            store(
                attended_refs,
                branch_refs,
                [ref[:, :length] for ref in early_attended],
                [ref[...] for ref in late_branch],
            )

    def first_half(wide_here):
        return pl.BlockSpec((piece, wide_here), lambda step, core_ref: (jnp.minimum(step, 1), 0))

    def second_half(wide_here):
        return pl.BlockSpec(
            (piece, wide_here), lambda step, core_ref: (jnp.maximum(step - 2, 0), 0)
        )

    wholes = [whole((length, columns))] * rows
    return pl.pallas_call(
        kernel,
        grid_spec=pltpu.PrefetchScalarGridSpec(
            num_scalar_prefetch=1,
            grid=(4,),
            in_specs=([first_half(length)] * rows + [second_half(length)] * rows) * 2
            + wholes * 2
            + wholes
            + [second_half(lanes(length))] * rows
            + [whole(late[0][0].shape)] * rows
            + wholes,
            out_specs=pl.BlockSpec((piece, columns), lambda step, core_ref: (step, 0)),
        ),
        out_shape=jax.ShapeDtypeStruct((2 * wide, columns), jnp.float32),
        compiler_params=limit(56),
        cost_estimate=estimate(0.02),
    )(
        core.reshape(1), *dq, *dk, *dv, *attended, *normed, *branch_grad,
        *[member for place in range(2) for member in [part[place] for part in early]],
        *[member for place in range(2) for member in [part[place] for part in late]],
    )


def shards(
    hidden_in,
    row_layout,
    cotangent,
    pre_gain,
    pre_shift,
    query_weight,
    query_bias,
    key_weight,
    value_weight,
    value_bias,
    out_weight,
    out_bias,
    mid_gain,
    mid_shift,
    up_weight,
    up_bias,
    down_weight,
    down_bias,
):
    rows, length, width = hidden_in.shape
    tokens = rows * length
    heads_wide = query_weight.shape[1]
    hidden = up_weight.shape[1]
    side = sides()
    core = side["core"]
    order = Order()
    query_turned = query_weight.T
    key_turned = key_weight.T
    value_turned = value_weight.T
    up_turned = up_weight.T

    forward = [
        order.run(
            lambda ready: attention_forward(
                row, row_layout, ready, pre_gain, pre_shift, query_turned, query_bias, key_turned,
                value_turned, value_bias, out_weight,
            ),
            hidden_in,
        )
        for row in range(rows)
    ]

    up_column = up_bias.reshape(-1, 1)
    middle = []
    early = []
    for row in range(rows):
        if row > 0:
            with jax.named_scope("early_core_move_" + str(row - 1)):
                early.append(order.settle([swap(forward[row - 1].value[n], "core") for n in (6, 7)]))
        with jax.named_scope("branch_move_" + str(row)):
            received = swap_tensor(forward[row].value[5])
        middle.append(
            order.run(
                lambda ready: feed_forward(
                    row, core, hidden_in, ready, received, out_bias, mid_gain, mid_shift,
                    up_turned, up_column, down_weight, cotangent,
                    None if row == 0 else middle[row - 1].value[3],
                ),
                forward[row].value[5],
            )
        )
    with jax.named_scope("early_core_move_" + str(rows - 1)):
        early.append(order.settle([swap(forward[rows - 1].value[n], "core") for n in (6, 7)]))
    normed = [forward[row].value[0] for row in range(rows)]
    attended = [forward[row].value[4] for row in range(rows)]
    resid = [middle[row].value[0] for row in range(rows)]
    middles = [middle[row].value[1] for row in range(rows)]
    backward = []

    def back(row, received):
        _, q, k, v = forward[row].value[:4]
        backward.append(
            order.run(
                lambda ready: attention_backward(
                    row, core, row_layout, ready, received, resid[row], cotangent, mid_gain,
                    q, k, v, out_weight,
                ),
                middle[rows - 1].value[3],
            )
        )

    pairs = [middle[row].value[2] for row in range(rows)]
    ff_rows = (576, 576, 576, 576)
    ff_streams = [Stream("ff" + str(n), order, ORDERS[n], side) for n in range(4)]

    def ff_step(extra=None):
        moved = [stream.moved() for stream in ff_streams]
        received = lax.optimization_barrier(moved + ([] if extra is None else [extra]))
        for stream, part in zip(ff_streams, received):
            stream.step(part)
        return received[-1]

    lefts, rights = [], []

    def ff_core_move(row):
        with jax.named_scope("ff_core_move_" + str(row)):
            lefts.append(swap(middle[row].value[5], "core"))
            rights.append(swap(middle[row].value[6], "core"))

    ff_core_move(0)
    lefts[0] = order.settle(lefts[0])
    rights[0] = order.settle(rights[0])
    ff_core_move(1)
    ff_sides = jnp.stack([side[stream.pairs[0]] for stream in ff_streams])

    def ff_begin(first):
        members = ff_streams[first : first + 2]
        halves = order.run(
            lambda ready: ff_own(
                core, ff_sides[first : first + 2], [pairs[0], ready], cotangent, middles, lefts,
                rights, ff_rows[first : first + 2], sum(ff_rows[:first]),
            ),
            pairs[1],
        )
        for n, stream in enumerate(members):
            stream.begin(*halves.value[2 * n : 2 * n + 2])

    ff_begin(0)
    ff_begin(2)
    with jax.named_scope("mid_move"):
        mid_received = swap_tensor(middle[rows - 1].value[3])
    back(0, mid_received)
    back(1, mid_received)

    dq, dk, dv = ([backward[row].value[place] for row in range(rows)] for place in (3, 4, 5))
    branch_grad = [backward[row].value[1] for row in range(rows)]
    output = []

    def output_move(row):
        with jax.named_scope("output_move_" + str(row)):
            return swap_tensor(middle[row].value[4])

    def output_row(row, received):
        output.append(
            order.run(
                lambda ready: low(resid[row] + (ready + received) + down_bias),
                middle[row].value[4],
            )
        )

    def normed_move(row):
        with jax.named_scope("normed_move_" + str(row)):
            return swap_tensor(normed_part[row].value)

    output_row(0, ff_step(output_move(0)))
    late = []
    for row in range(rows):
        with jax.named_scope("late_core_move_" + str(row)):
            late.append(order.settle([swap(backward[row].value[n], "core") for n in (6, 7)]))
    at_own = order.run(
        lambda ready: attention_own(
            core, [dq[0], ready], dk, dv, attended, normed, branch_grad, early, late
        ),
        dq[1],
    )
    with jax.named_scope("at_scatter"):
        at_block = lax.psum_scatter(
            at_own.value, "dp", axis_index_groups=PLANES, scatter_dimension=0, tiled=True
        )
    normed_part = [
        order.run(
            lambda ready: inner_rows(ready, query_turned)
            + inner_rows(dk[row], key_turned)
            + inner_rows(dv[row], value_turned),
            dq[row],
        )
        for row in range(rows)
    ]
    ff_step()
    normed_received = [ff_step(normed_move(0))]
    normed_received.append(ff_step(normed_move(1)))
    normed_grad = order.run(
        lambda ready: jnp.concatenate(
            [ready + normed_received[0], normed_part[1].value + normed_received[1]], 0
        ),
        normed_part[0].value,
    )
    pre_normal, pre_factor = normalized(hidden_in.reshape(tokens, width).astype(jnp.float32))
    pre_gain_grad = jnp.sum(normed_grad.value * pre_normal, axis=0)
    pre_shift_grad = jnp.sum(normed_grad.value, axis=0)
    resid_grad = jnp.concatenate([backward[row].value[0] for row in range(rows)], 0)
    input_grad = resid_grad + norm_back(normed_grad.value, pre_normal, pre_factor, pre_gain)
    terms = sum(backward[row].value[2] for row in range(rows))

    def token_sum(members):
        return sum(jnp.sum(member.astype(jnp.float32), axis=1) for member in members)

    small = jnp.concatenate(
        [
            pre_gain_grad,
            pre_shift_grad,
            terms[2],
            terms[0],
            terms[1],
            jnp.sum(cotangent.astype(jnp.float32), axis=(0, 1)),
            token_sum(dq),
            token_sum(dv),
            token_sum([pair[1, :hidden] for pair in pairs]),
            jnp.zeros((2 * width - hidden,), jnp.float32),
        ]
    ).reshape(9, width)
    small = order.run(lambda ready: ready, small)

    def small_move(pair):
        with jax.named_scope("small_move_" + pair):
            return swap(small.value, pair)

    def small_add(received):
        return order.run(lambda ready: ready + received, small.value)

    small = small_add(ff_step(small_move("z")))
    small = small_add(ff_step(small_move("xa")))
    small = small_add(ff_step(small_move("ya")))
    at_block = order.run(lambda ready: ready + 0.0, at_block)
    with jax.named_scope("at_z_move"):
        received = swap(at_block.value, "z")
    received = ff_step(received)
    halves = [stream.halves() for stream in ff_streams]
    at_block = order.run(lambda ready: ready + received, at_block.value)
    with jax.named_scope("at_gather"):
        at_whole = lax.all_gather(
            at_block.value, "dp", axis_index_groups=PLANES, axis=0, tiled=True
        )
    others = order.settle([other for _, other in halves] + [output_move(1)])
    output_row(1, others.pop())
    far = []
    for number, other in enumerate(others):
        with jax.named_scope("ff_core_other_" + str(number)):
            far.append((swap(halves[number][0], "core"), swap(other, "core")))
    down_up = None
    for n in range(4):
        down_up = pick_halves(
            core, ff_sides[n : n + 1], (halves[n][0], others[n], *far[n]), hidden,
            sum(ff_rows[:n]), down_up,
        )
        first_down, small.value = lax.optimization_barrier((down_up[0], small.value))
        down_up = (first_down, down_up[1])
        if n < 3:
            small = small_add(small_move(("xb", "yb", "core")[n]))
    down_grad, up_grad = down_up
    input_low, small.value, at_whole, down_grad = lax.optimization_barrier(
        (low(input_grad), small.value, at_whole, down_grad)
    )
    with jax.named_scope("at_core_back"):
        received = swap(at_whole, "core")
    query_weight_grad, value_weight_grad = pick_rows(
        core, at_whole, received, heads_wide, 192, 0, 0, heads_wide
    )
    key_weight_grad, out_grad = pick_rows(
        core, at_whole, received, heads_wide, 192, heads_wide, 0, heads_wide
    )
    small = small.value
    return (
        jnp.stack([part.value for part in output]),
        input_low.reshape(hidden_in.shape),
        small[0],
        small[1],
        query_weight_grad.T,
        small[6, :heads_wide],
        key_weight_grad.T,
        value_weight_grad.T,
        small[6, heads_wide:],
        out_grad,
        small[2],
        small[3],
        small[4],
        up_grad.T,
        small[7:].reshape(-1)[:hidden],
        down_grad,
        small[5],
    )


def solution(mesh):
    placed = (
        P("dp", None, None),
        P("dp", None),
        P("dp", None, None),
        P(),
        P(),
        P(None, "tensor"),
        P("tensor"),
        P(None, "tensor"),
        P(None, "tensor"),
        P("tensor"),
        P("tensor", None),
        P(),
        P(),
        P(),
        P(None, "tensor"),
        P("tensor"),
        P("tensor", None),
        P(),
    )
    return jax.shard_map(
        shards,
        mesh=mesh,
        in_specs=placed,
        out_specs=(
            P("dp", None, None),
            P("dp", None, None),
            P(),
            P(),
            P(None, "tensor"),
            P("tensor"),
            P(None, "tensor"),
            P(None, "tensor"),
            P("tensor"),
            P("tensor", None),
            P(),
            P(),
            P(),
            P(None, "tensor"),
            P("tensor"),
            P("tensor", None),
            P(),
        ),
        check_vma=False,
    )
```

time: 598 us -> 402 us (0.67)
  waiting for transfers between devices: 267 us -> 100 us
  Pallas kernels: 0 us -> 130 us
  matrix products: 71.8 us -> 3.47 us
  other arithmetic: 81.4 us -> 36.5 us
  starting transfers between devices: 124 us -> 88.6 us
  local copies, waits for them, and re-layouts: 44 us -> 19.7 us
  between operations: 2.81 us -> 15.4 us
    pallas_call x0 -> x15, Pallas kernels: none -> 130 us  [the longest x2 28.8 us: feed_forward(): pl.pallas_call(kernel, grid=(steps,), in_specs=[scalars(), at_row] + [who...]
    ppermute x82 -> x64, waiting for transfers between devices: 156 us -> 72 us  [swap(): return lax.ppermute(values, 'dp', PAIRS[pair])]
    ppermute x4 -> x7, waiting for transfers between devices: 111 us -> 28.4 us  [swap_tensor(): return lax.ppermute(values, 'tensor', [(0, 1), (1, 0)])]
    dot_general x18 -> x0, matrix products: 39.1 us -> none  [the longest x6 18.9 us: product(): return jnp.dot(left, right, preferred_element_type=jnp.float32)]
    select_n x31 -> x12, other arithmetic: 47.3 us -> 8.89 us  [joined(): jnp.where(side == 0, jnp.concatenate([own, received], axis), jnp.concaten...]
    ppermute x82 -> x64, starting transfers between devices: 119 us -> 80.7 us  [swap(): return lax.ppermute(values, 'dp', PAIRS[pair])]
    dot_general x12 -> x6, matrix products: 32.8 us -> 3.47 us  [inner_rows(): lax.dot_general(left, right, (((0,), (0,)), ((), ())), preferred_element_...]
    unnamed x186 -> x134, local copies, waits for them, and re-layouts: 28.8 us -> 12.8 us
  transfers between devices with their start and end apart: 86 -> 73, of which waited for: 38 -> 26; matrix products, arithmetic and copies ran while one was open for 21% -> 10% of each run, Pallas kernels for 0% -> 26%
where the time goes in v3:
time: 402 us; the launch traced here: 394 us
  Pallas kernels  130 us (32%)
  waiting for transfers between devices  100 us (25%)
  starting transfers between devices  88.6 us (22%)
  other arithmetic  36.5 us (9%)
  local copies, waits for them, and re-layouts  19.7 us (5%)
  between operations  15.4 us (4%)
    ppermute x64, starting transfers between devices, swap(): return lax.ppermute(values, 'dp', PAIRS[pair])  80.7 us
    ppermute x64, waiting for transfers between devices, swap(): return lax.ppermute(values, 'dp', PAIRS[pair])  72 us
    pallas_call x2, Pallas kernels, feed_forward(): pl.pallas_call(kernel, grid=(steps,), in_specs=[scalars(), at_row] + [who...  28.8 us
    ppermute x7, waiting for transfers between devices, swap_tensor(): return lax.ppermute(values, 'tensor', [(0, 1), (1, 0)])  28.4 us
    pallas_call x2, Pallas kernels, attention_backward(): pl.pallas_call(kernel, grid=(1,), in_specs=[scalars(), scalars()] + [pl.B...  21.4 us
    pallas_call x4, Pallas kernels, pick_halves(): pl.pallas_call(kernel, grid_spec=pltpu.PrefetchScalarGridSpec(num_scalar_...  21 us
    pallas_call x2, Pallas kernels, ff_own(): pl.pallas_call(kernel, grid_spec=pltpu.PrefetchScalarGridSpec(num_scalar_...  20.4 us
    pallas_call x2, Pallas kernels, attention_forward(): pl.pallas_call(kernel, grid=(1,), in_specs=[scalars(), pl.BlockSpec((1, l...  19.5 us
  transfers between devices with their start and end apart: 73, of which 26 were waited for; matrix products, arithmetic and copies ran while one was open for 10% of the time, Pallas kernels for 26%

profile of v3, /device:TPU:1, one launch (start us, length us, event | category | flops | bytes accessed | tf_op | source)
XLA Modules:
  0.0 393.8 jit_solution(799239162675835601)
XLA Ops:
  7.2 9.7 %shard_map.305 = (bf16[192,1152]{1,0:T(8,128)(2,1)}, bf16[576,192]{1,0:T(8,128)(2,1)}, bf16[576,192]{1,0:T(8,128)(2,1)}, bf16[576,192]{1,0:T(8,128)(2,1)}, bf16[...) custom-call(s32[2,4]{1,0:T(2,128)} %layout_ref.7, ...), custom_call_target="tpu_custom_call" | custom-call | flops 23000000512 | bytes 1024 | tf_op jit(solution)/shard_map/pallas_call | solution.py:357
  20.5 9.7 %shard_map.306 = (bf16[192,1152]{1,0:T(8,128)(2,1)}, bf16[576,192]{1,0:T(8,128)(2,1)}, bf16[576,192]{1,0:T(8,128)(2,1)}, bf16[576,192]{1,0:T(8,128)(2,1)}, bf16[...) custom-call(s32[2,4]{1,0:T(2,128)} %layout_ref.7, ...), custom_call_target="tpu_custom_call" | custom-call | flops 23000000512 | bytes 1024 | tf_op jit(solution)/shard_map/pallas_call | solution.py:357
  32.2 6.9 %collective-permute-done.received_ref = f32[192,1152]{1,0:T(8,128)S(1)} collective-permute-done((f32[192,1152]{1,0:T(8,128)}, f32[192,1152]{1,0:T(8,128)S(1)}, u32[]{:S(2)}, u32[]{:S(2)}) %collective-permute-start) | collective-permute-done | bytes 884768 | tf_op jit(solution)/shard_map/branch_move_0/ppermute | solution.py:60
  41.4 14.4 %shard_map.307 = (f32[192,1152]{1,0:T(8,128)}, bf16[192,1152]{1,0:T(8,128)(2,1)}, bf16[2,2304,192]{2,1,0:T(8,128)(2,1)}, f32[384,1152]{1,0:T(8,128)}, f32[192,11...) custom-call(s32[1]{0:T(128)} %bitcast.core_ref, bf16[2,192,1152]{2,1,0:T(8,128)(2,1)} %hidden_ref.6, ...), custom_call_target="tpu_custom_call" | custom-call | flops 34500001792 | bytes 1024 | tf_op jit(solution)/shard_map/pallas_call | solution.py:552
  58.2 14.4 %shard_map.308 = (f32[192,1152]{1,0:T(8,128)}, bf16[192,1152]{1,0:T(8,128)(2,1)}, bf16[2,2304,192]{2,1,0:T(8,128)(2,1)}, f32[384,1152]{1,0:T(8,128)}, f32[192,11...) custom-call(s32[1]{0:T(128)} %bitcast.core_ref, ...), custom_call_target="tpu_custom_call", output_to_operand_aliasing={{3}: (11, {})} | custom-call | flops 34500001792 | bytes 1024 | tf_op jit(solution)/shard_map/pallas_call | solution.py:552
  79.7 10.2 %shard_map.309 = (f32[288,1152]{1,0:T(8,128)}, f32[288,1152]{1,0:T(8,128)}, f32[288,1152]{1,0:T(8,128)}, f32[288,1152]{1,0:T(8,128)}) custom-call(s32[1]{0:T(128)} %bitcast.core_ref, s32[2]{0:T(128)} %get-tuple-element.633.sides_ref, bf16[2,2304,192]{2,1,0:T(8,128)(2,1)} %get-tuple-element.340.refs_0_, bf16[2,2304,192]{2,1,0:T(8,128)(2,1)} %get-tuple-element.374.refs_1_, ...), custom_call_target="tpu_custom_call" | custom-call | flops 4600000000 | bytes 1024 | tf_op jit(solution)/shard_map/pallas_call | solution.py:646
  89.9 10.2 %shard_map.310 = (f32[288,1152]{1,0:T(8,128)}, f32[288,1152]{1,0:T(8,128)}, f32[288,1152]{1,0:T(8,128)}, f32[288,1152]{1,0:T(8,128)}) custom-call(s32[1]{0:T(128)} %bitcast.core_ref, s32[2]{0:T(128)} %get-tuple-element.632.sides_ref, bf16[2,2304,192]{2,1,0:T(8,128)(2,1)} %get-tuple-element.340.refs_0_, bf16[2,2304,192]{2,1,0:T(8,128)(2,1)} %get-tuple-element.374.refs_1_, ...), custom_call_target="tpu_custom_call" | custom-call | flops 4600000000 | bytes 1024 | tf_op jit(solution)/shard_map/pallas_call | solution.py:646
  105.3 9.4 %collective-permute-done.10.received_ref = f32[384,1152]{1,0:T(8,128)S(1)} collective-permute-done((f32[384,1152]{1,0:T(8,128)}, f32[384,1152]{1,0:T(8,128)S(1)}, u32[]{:S(2)}, u32[]{:S(2)}) %collective-permute-start.10) | collective-permute-done | bytes 1769504 | tf_op jit(solution)/shard_map/mid_move/ppermute | solution.py:60
  116.2 10.7 %shard_map.311 = (f32[192,1152]{1,0:T(8,128)}, bf16[192,1152]{1,0:T(8,128)(2,1)}, f32[8,1152]{1,0:T(8,128)}, bf16[576,192]{1,0:T(8,128)(2,1)}, bf16[576,192]{1,0...) custom-call(s32[1]{0:T(128)} %bitcast.core_ref, s32[2,4]{1,0:T(2,128)} %layout_ref.7, ...), custom_call_target="tpu_custom_call" | custom-call | flops 23000000 | bytes 1024 | tf_op jit(solution)/shard_map/pallas_call | solution.py:447
  126.9 10.7 %shard_map.312 = (f32[192,1152]{1,0:T(8,128)}, bf16[192,1152]{1,0:T(8,128)(2,1)}, f32[8,1152]{1,0:T(8,128)}, bf16[576,192]{1,0:T(8,128)(2,1)}, bf16[576,192]{1,0...) custom-call(s32[1]{0:T(128)} %bitcast.core_ref, s32[2,4]{1,0:T(2,128)} %layout_ref.7, ...), custom_call_target="tpu_custom_call" | custom-call | flops 23000000 | bytes 1024 | tf_op jit(solution)/shard_map/pallas_call | solution.py:447
  154.3 9.8 %shard_map.313 = f32[1152,1152]{1,0:T(8,128)} custom-call(s32[1]{0:T(128)} %bitcast.core_ref, bf16[576,192]{1,0:T(8,128)(2,1)} %get-tuple-element.445.refs_0_, bf16[576,192]{1,0:T(8,128)(2,1)} %get-tuple-element.446.refs_1_, bf16[576,192]{1,0:T(8,128)(2,1)} %get-tuple-element.430.refs_2_, bf16[576,192]{1,0:T(8,128)(2,1)} %get-tuple-element.397.refs_3_, ...), custom_call_target="tpu_custom_call" | custom-call | flops 23000000 | bytes 1024 | tf_op jit(solution)/shard_map/pallas_call | solution.py:725
  182.2 9.3 %collective-permute-done.23 = f32[2,72,1152]{2,1,0:T(8,128)S(1)} collective-permute-done((f32[2,72,1152]{2,1,0:T(8,128)}, f32[2,72,1152]{2,1,0:T(8,128)S(1)}, u32[]{:S(2)}, u32[]{:S(2)}) %collective-permute-start.23) | collective-permute-done | bytes 663584 | tf_op jit(solution)/shard_map/ff3_move_2/ppermute | solution.py:56
  194.6 4.3 %collective-permute-done.21 = f32[2,72,1152]{2,1,0:T(8,128)S(1)} collective-permute-done((f32[2,72,1152]{2,1,0:T(8,128)S(1)}, f32[2,72,1152]{2,1,0:T(8,128)S(1)}, u32[]{:S(2)}, u32[]{:S(2)}) %collective-permute-start.21) | collective-permute-done | bytes 663584 | tf_op jit(solution)/shard_map/ff1_move_2/ppermute | solution.py:56
  204.0 8.9 %collective-permute-done.27 = f32[1,72,1152]{2,1,0:T(8,128)S(1)} collective-permute-done((f32[1,72,1152]{2,1,0:T(8,128)S(1)}, f32[1,72,1152]{2,1,0:T(8,128)S(1)}, u32[]{:S(2)}, u32[]{:S(2)}) %collective-permute-start.27) | collective-permute-done | bytes 331808 | tf_op jit(solution)/shard_map/ff3_move_3/ppermute | solution.py:56
  239.0 7.8 %collective-permute-done.38 = f32[9,1152]{1,0:T(8,128)S(1)} collective-permute-done((f32[9,1152]{1,0:T(8,128)S(1)}, f32[9,1152]{1,0:T(8,128)S(1)}, u32[]{:S(2)}, u32[]{:S(2)}) %collective-permute-start.38) | collective-permute-done | bytes 41504 | tf_op jit(solution)/shard_map/small_move_z/ppermute | solution.py:56
  290.8 9.1 %collective-permute-done.58 = f32[192,1152]{1,0:T(8,128)S(1)} collective-permute-done((f32[192,1152]{1,0:T(8,128)}, f32[192,1152]{1,0:T(8,128)S(1)}, u32[]{:S(2)}, u32[]{:S(2)}) %collective-permute-start.58) | collective-permute-done | bytes 884768 | tf_op jit(solution)/shard_map/output_move_1/ppermute | solution.py:60
  300.9 10.2 %collective-permute-start.59 = (f32[288,1152]{1,0:T(8,128)S(1)}, f32[288,1152]{1,0:T(8,128)S(1)}, u32[]{:S(2)}, u32[]{:S(2)}) collective-permute-start(f32[288,1152]{1,0:T(8,128)S(1)} %bitcast.59), channel_id=1, source_target_pairs={{0,2},{2,0},{4,6},{6,4},{8,10},{10,8},{12,14},{14,12},{16,18},{18,... | collective-permute-start | bytes 3981320 | tf_op jit(solution)/shard_map/ff_core_other_0/ppermute | solution.py:56
  315.2 13.1 %collective-permute-start.60 = (f32[288,1152]{1,0:T(8,128)}, f32[288,1152]{1,0:T(8,128)}, u32[]{:S(2)}, u32[]{:S(2)}) collective-permute-start(f32[288,1152]{1,0:T(8,128)} %bitcast.19.refs_1_), channel_id=1, source_target_pairs={{0,2},{2,0},{4,6},{6,4},{8,10},{10,8},{12,14},{14,12},{16,18},{18,... | collective-permute-start | bytes 3981320 | tf_op jit(solution)/shard_map/ff_core_other_0/ppermute | solution.py:56
  335.8 5.6 %shard_map.314 = (f32[2152,1152]{1,0:T(8,128)}, f32[2152,1152]{1,0:T(8,128)}) custom-call(s32[1]{0:T(128)} %bitcast.core_ref, s32[1]{0:T(128)} %bitcast.7.sides_ref, f32[288,1152]{1,0:T(8,128)S(1)} %bitcast.60, f32[288,1152]{1,0:T(8,128)} %bitcast.19.refs_1_, f32[288,1152]{1,0:T(8,128)S(1)} %copy-done.4, f32[288,1152]{1,0:T(8,128)} %collective-permute-done.60.refs_3_), custom_call_target="tpu_custom_call" | custom-call | flops 23000000 | bytes 1024 | tf_op jit(solution)/shard_map/pallas_call | solution.py:226
  344.4 5.7 %shard_map.315 = (f32[2152,1152]{1,0:T(8,128)}, f32[2152,1152]{1,0:T(8,128)}) custom-call(s32[1]{0:T(128)} %bitcast.core_ref, s32[1]{0:T(128)} %bitcast.8.sides_ref, f32[288,1152]{1,0:T(8,128)S(1)} %bitcast.66, f32[288,1152]{1,0:T(8,128)} %bitcast.20.refs_1_, ...), custom_call_target="tpu_custom_call", output_to_operand_aliasing={{0}: (6, {}), {1}: (7, {})} | custom-call | flops 23000000 | bytes 1024 | tf_op jit(solution)/shard_map/pallas_call | solution.py:226
  352.9 5.8 %shard_map.316 = (f32[2152,1152]{1,0:T(8,128)}, f32[2152,1152]{1,0:T(8,128)}) custom-call(s32[1]{0:T(128)} %bitcast.core_ref, s32[1]{0:T(128)} %bitcast.5.sides_ref, f32[288,1152]{1,0:T(8,128)S(1)} %bitcast.64, f32[288,1152]{1,0:T(8,128)} %bitcast.21.refs_1_, ...), custom_call_target="tpu_custom_call", output_to_operand_aliasing={{0}: (6, {}), {1}: (7, {})} | custom-call | flops 23000000 | bytes 1024 | tf_op jit(solution)/shard_map/pallas_call | solution.py:226
  369.0 6.1 %collective-permute-done.70.other_ref = f32[1152,1152]{1,0:T(8,128)} collective-permute-done((f32[1152,1152]{1,0:T(8,128)}, f32[1152,1152]{1,0:T(8,128)}, u32[]{:S(2)}, u32[]{:S(2)}) %collective-permute-start.70) | collective-permute-done | bytes 5308448 | tf_op jit(solution)/shard_map/at_core_back/ppermute | solution.py:56
  377.6 4.5 %shard_map.319 = (f32[576,1152]{1,0:T(8,128)}, f32[576,1152]{1,0:T(8,128)}) custom-call(s32[1]{0:T(128)} %bitcast.core_ref, f32[1152,1152]{1,0:T(8,128)S(1)} %copy-done, f32[1152,1152]{1,0:T(8,128)} %collective-permute-done.70.other_ref), custom_call_target="tpu_custom_call" | custom-call | flops 23000000 | bytes 1024 | tf_op jit(solution)/shard_map/pallas_call | solution.py:178
  382.1 4.5 %shard_map.318 = (f32[576,1152]{1,0:T(8,128)}, f32[576,1152]{1,0:T(8,128)}) custom-call(s32[1]{0:T(128)} %bitcast.core_ref, f32[1152,1152]{1,0:T(8,128)S(1)} %copy-done, f32[1152,1152]{1,0:T(8,128)} %collective-permute-done.70.other_ref), custom_call_target="tpu_custom_call" | custom-call | flops 23000000 | bytes 1024 | tf_op jit(solution)/shard_map/pallas_call | solution.py:178
  (357 shorter events, 167.4 us)
Async XLA Ops:
  7.2 261.7 %reduce-scatter.4.cloned.1.call-start = ((), (), s32[]{:S(2)}) async-start(), calls=%async_computation.2 | async-start | bytes 5640192
  19.5 36.3 %collective-permute-start.1 = (f32[192,1152]{1,0:T(8,128)}, f32[192,1152]{1,0:T(8,128)S(1)}, u32[]{:S(2)}, u32[]{:S(2)}) collective-permute-start(f32[192,1152]{1,0:T(8,128)} %get-tuple-element.329), channel_id=1, source_target_pairs={{0,2},{2,0},{4,6},{6,4},{8,10},{10,8},{12,14},{14,12},{16,18},{18,... | collective-permute-start | bytes 2654216 | tf_op jit(solution)/shard_map/early_core_move_0/ppermute | solution.py:56
  20.5 35.3 %collective-permute-start.2 = (f32[576,256]{1,0:T(8,128)}, f32[576,256]{1,0:T(8,128)S(1)}, u32[]{:S(2)}, u32[]{:S(2)}) collective-permute-start(f32[576,256]{1,0:T(8,128)} %get-tuple-element.330), channel_id=1, source_target_pairs={{0,2},{2,0},{4,6},{6,4},{8,10},{10,8},{12,14},{14,12},{16,18},{18,... | collective-permute-start | bytes 1769480 | tf_op jit(solution)/shard_map/early_core_move_0/ppermute | solution.py:56
  30.2 27.9 %collective-permute-start.3 = (f32[192,1152]{1,0:T(8,128)}, f32[192,1152]{1,0:T(8,128)}, u32[]{:S(2)}, u32[]{:S(2)}) collective-permute-start(f32[192,1152]{1,0:T(8,128)} %get-tuple-element.341.branch_ref), channel_id=1, source_target_pairs={{0,1},{1,0},{2,3},{3,2},{4,5},{5,4},{6,7},{7,6},{8,9},{9,8},{10,11... | collective-permute-start | bytes 2654216 | tf_op jit(solution)/shard_map/branch_move_1/ppermute | solution.py:60
  30.2 42.4 %collective-permute-start.4 = (f32[192,1152]{1,0:T(8,128)}, f32[192,1152]{1,0:T(8,128)S(1)}, u32[]{:S(2)}, u32[]{:S(2)}) collective-permute-start(f32[192,1152]{1,0:T(8,128)} %get-tuple-element.350), channel_id=1, source_target_pairs={{0,2},{2,0},{4,6},{6,4},{8,10},{10,8},{12,14},{14,12},{16,18},{18,... | collective-permute-start | bytes 2654216 | tf_op jit(solution)/shard_map/early_core_move_1/ppermute | solution.py:56
  39.1 33.5 %collective-permute-start.5 = (f32[576,256]{1,0:T(8,128)}, f32[576,256]{1,0:T(8,128)S(1)}, u32[]{:S(2)}, u32[]{:S(2)}) collective-permute-start(f32[576,256]{1,0:T(8,128)} %get-tuple-element.351), channel_id=1, source_target_pairs={{0,2},{2,0},{4,6},{6,4},{8,10},{10,8},{12,14},{14,12},{16,18},{18,... | collective-permute-start | bytes 1769480 | tf_op jit(solution)/shard_map/early_core_move_1/ppermute | solution.py:56
  74.8 39.9 %collective-permute-start.10 = (f32[384,1152]{1,0:T(8,128)}, f32[384,1152]{1,0:T(8,128)S(1)}, u32[]{:S(2)}, u32[]{:S(2)}) collective-permute-start(f32[384,1152]{1,0:T(8,128)} %get-tuple-element.389.part_ref), channel_id=1, source_target_pairs={{0,1},{1,0},{2,3},{3,2},{4,5},{5,4},{6,7},{7,6},{8,9},{9,8},{10,11... | collective-permute-start | bytes 5308424 | tf_op jit(solution)/shard_map/mid_move/ppermute | solution.py:60
  100.1 39.5 %collective-permute-start.14 = (f32[4,72,1152]{2,1,0:T(8,128)}, f32[4,72,1152]{2,1,0:T(8,128)S(1)}, u32[]{:S(2)}, u32[]{:S(2)}) collective-permute-start(f32[4,72,1152]{2,1,0:T(8,128)} %bitcast.89), channel_id=1, source_target_pairs={{0,12},{2,14},{4,8},{6,10},{8,4},{10,6},{12,0},{14,2},{16,28},{18,... | collective-permute-start | bytes 3981320 | tf_op jit(solution)/shard_map/ff3_move_1/ppermute | solution.py:56
  102.8 36.9 %collective-permute-start.13 = (f32[4,72,1152]{2,1,0:T(8,128)}, f32[4,72,1152]{2,1,0:T(8,128)}, u32[]{:S(2)}, u32[]{:S(2)}) collective-permute-start(f32[4,72,1152]{2,1,0:T(8,128)} %bitcast.88), channel_id=1, source_target_pairs={{0,48},{2,50},{4,52},{6,54},{8,56},{10,58},{12,60},{14,62},{16,32}... | collective-permute-start | bytes 3981320 | tf_op jit(solution)/shard_map/ff2_move_1/ppermute | solution.py:56
  105.3 34.8 %collective-permute-start.12 = (f32[4,72,1152]{2,1,0:T(8,128)}, f32[4,72,1152]{2,1,0:T(8,128)}, u32[]{:S(2)}, u32[]{:S(2)}) collective-permute-start(f32[4,72,1152]{2,1,0:T(8,128)} %bitcast.9), channel_id=1, source_target_pairs={{0,4},{2,6},{4,0},{6,2},{8,12},{10,14},{12,8},{14,10},{16,20},{18,... | collective-permute-start | bytes 3981320 | tf_op jit(solution)/shard_map/ff1_move_1/ppermute | solution.py:56
  105.3 34.9 %collective-permute-start.11 = (f32[4,72,1152]{2,1,0:T(8,128)}, f32[4,72,1152]{2,1,0:T(8,128)}, u32[]{:S(2)}, u32[]{:S(2)}) collective-permute-start(f32[4,72,1152]{2,1,0:T(8,128)} %bitcast.12), channel_id=1, source_target_pairs={{0,16},{2,18},{4,20},{6,22},{8,24},{10,26},{12,28},{14,30},{16,0},... | collective-permute-start | bytes 3981320 | tf_op jit(solution)/shard_map/ff0_move_1/ppermute | solution.py:56
  114.7 22.9 %collective-permute-start.15 = (f32[192,1152]{1,0:T(8,128)}, f32[192,1152]{1,0:T(8,128)}, u32[]{:S(2)}, u32[]{:S(2)}) collective-permute-start(f32[192,1152]{1,0:T(8,128)} %get-tuple-element.418), channel_id=1, source_target_pairs={{0,1},{1,0},{2,3},{3,2},{4,5},{5,4},{6,7},{7,6},{8,9},{9,8},{10,11... | collective-permute-start | bytes 2654216 | tf_op jit(solution)/shard_map/output_move_0/ppermute | solution.py:60
  164.2 201.7 %all-gather.2.cloned.1.call-start = ((), (), s32[]{:S(2)}) async-start(), calls=%async_computation.1 | async-start | bytes 5640192 | tf_op jit(solution)/shard_map/at_gather/all_gather | solution.py:969
  170.9 23.7 %collective-permute-start.22 = (f32[2,72,1152]{2,1,0:T(8,128)S(1)}, f32[2,72,1152]{2,1,0:T(8,128)S(1)}, u32[]{:S(2)}, u32[]{:S(2)}) collective-permute-start(f32[2,72,1152]{2,1,0:T(8,128)S(1)} %copy-done.49), channel_id=1, source_target_pairs={{0,12},{2,14},{4,8},{6,10},{8,4},{10,6},{12,0},{14,2},{16,28},{18,... | collective-permute-start | bytes 1990664 | tf_op jit(solution)/shard_map/ff2_move_2/ppermute | solution.py:56
  173.7 25.2 %collective-permute-start.21 = (f32[2,72,1152]{2,1,0:T(8,128)S(1)}, f32[2,72,1152]{2,1,0:T(8,128)S(1)}, u32[]{:S(2)}, u32[]{:S(2)}) collective-permute-start(f32[2,72,1152]{2,1,0:T(8,128)S(1)} %copy-done.48), channel_id=1, source_target_pairs={{0,48},{2,50},{4,52},{6,54},{8,56},{10,58},{12,60},{14,62},{16,32}... | collective-permute-start | bytes 1990664 | tf_op jit(solution)/shard_map/ff1_move_2/ppermute | solution.py:56
  175.5 24.0 %collective-permute-start.20 = (f32[2,72,1152]{2,1,0:T(8,128)S(1)}, f32[2,72,1152]{2,1,0:T(8,128)S(1)}, u32[]{:S(2)}, u32[]{:S(2)}) collective-permute-start(f32[2,72,1152]{2,1,0:T(8,128)S(1)} %copy-done.47), channel_id=1, source_target_pairs={{0,4},{2,6},{4,0},{6,2},{8,12},{10,14},{12,8},{14,10},{16,20},{18,... | collective-permute-start | bytes 1990664 | tf_op jit(solution)/shard_map/ff0_move_2/ppermute | solution.py:56
  288.0 23.3 %collective-permute-start.57 = (f32[4,72,1152]{2,1,0:T(8,128)S(1)}, f32[4,72,1152]{2,1,0:T(8,128)}, u32[]{:S(2)}, u32[]{:S(2)}) collective-permute-start(f32[4,72,1152]{2,1,0:T(8,128)S(1)} %maximum_select_fusion.3), channel_id=1, source_target_pairs={{0,12},{2,14},{4,8},{6,10},{8,4},{10,6},{12,0},{14,2},{16,28},{18,... | collective-permute-start | bytes 3981320 | tf_op jit(solution)/shard_map/ff3_move_9/ppermute | solution.py:56
  289.9 25.3 %collective-permute-start.56 = (f32[4,72,1152]{2,1,0:T(8,128)}, f32[4,72,1152]{2,1,0:T(8,128)}, u32[]{:S(2)}, u32[]{:S(2)}) collective-permute-start(f32[4,72,1152]{2,1,0:T(8,128)} %maximum_select_fusion.2), channel_id=1, source_target_pairs={{0,48},{2,50},{4,52},{6,54},{8,56},{10,58},{12,60},{14,62},{16,32}... | collective-permute-start | bytes 3981320 | tf_op jit(solution)/shard_map/ff2_move_9/ppermute | solution.py:56
  290.5 24.7 %collective-permute-start.55 = (f32[4,72,1152]{2,1,0:T(8,128)}, f32[4,72,1152]{2,1,0:T(8,128)}, u32[]{:S(2)}, u32[]{:S(2)}) collective-permute-start(f32[4,72,1152]{2,1,0:T(8,128)} %maximum_select_fusion.1), channel_id=1, source_target_pairs={{0,4},{2,6},{4,0},{6,2},{8,12},{10,14},{12,8},{14,10},{16,20},{18,... | collective-permute-start | bytes 3981320 | tf_op jit(solution)/shard_map/ff1_move_9/ppermute | solution.py:56
  290.8 24.4 %collective-permute-start.54 = (f32[4,72,1152]{2,1,0:T(8,128)S(1)}, f32[4,72,1152]{2,1,0:T(8,128)}, u32[]{:S(2)}, u32[]{:S(2)}) collective-permute-start(f32[4,72,1152]{2,1,0:T(8,128)S(1)} %maximum_select_fusion), channel_id=1, source_target_pairs={{0,16},{2,18},{4,20},{6,22},{8,24},{10,26},{12,28},{14,30},{16,0},... | collective-permute-start | bytes 3981320 | tf_op jit(solution)/shard_map/ff0_move_9/ppermute | solution.py:56
  300.9 28.1 %collective-permute-start.59 = (f32[288,1152]{1,0:T(8,128)S(1)}, f32[288,1152]{1,0:T(8,128)S(1)}, u32[]{:S(2)}, u32[]{:S(2)}) collective-permute-start(f32[288,1152]{1,0:T(8,128)S(1)} %bitcast.59), channel_id=1, source_target_pairs={{0,2},{2,0},{4,6},{6,4},{8,10},{10,8},{12,14},{14,12},{16,18},{18,... | collective-permute-start | bytes 3981320 | tf_op jit(solution)/shard_map/ff_core_other_0/ppermute | solution.py:56
  328.8 24.0 %collective-permute-start.63 = (f32[288,1152]{1,0:T(8,128)}, f32[288,1152]{1,0:T(8,128)}, u32[]{:S(2)}, u32[]{:S(2)}) collective-permute-start(f32[288,1152]{1,0:T(8,128)} %bitcast.63), channel_id=1, source_target_pairs={{0,2},{2,0},{4,6},{6,4},{8,10},{10,8},{12,14},{14,12},{16,18},{18,... | collective-permute-start | bytes 3981320 | tf_op jit(solution)/shard_map/ff_core_other_2/ppermute | solution.py:56
  330.0 22.8 %collective-permute-start.64 = (f32[288,1152]{1,0:T(8,128)}, f32[288,1152]{1,0:T(8,128)}, u32[]{:S(2)}, u32[]{:S(2)}) collective-permute-start(f32[288,1152]{1,0:T(8,128)} %bitcast.21.refs_1_), channel_id=1, source_target_pairs={{0,2},{2,0},{4,6},{6,4},{8,10},{10,8},{12,14},{14,12},{16,18},{18,... | collective-permute-start | bytes 3981320 | tf_op jit(solution)/shard_map/ff_core_other_2/ppermute | solution.py:56
  334.4 27.6 %collective-permute-start.61 = (f32[288,1152]{1,0:T(8,128)S(1)}, f32[288,1152]{1,0:T(8,128)}, u32[]{:S(2)}, u32[]{:S(2)}) collective-permute-start(f32[288,1152]{1,0:T(8,128)S(1)} %bitcast.61), channel_id=1, source_target_pairs={{0,2},{2,0},{4,6},{6,4},{8,10},{10,8},{12,14},{14,12},{16,18},{18,... | collective-permute-start | bytes 3981320 | tf_op jit(solution)/shard_map/ff_core_other_3/ppermute | solution.py:56
  (116 other events, 1065.0 us)
Sparse Core Ops, SparseCore 0:
  164.3 86.9 reduce-scatter.3
  287.9 67.5 all-gather.1

commit v4 on v3

--- a/solution.py
+++ b/solution.py
@@ -186,7 +186,7 @@
         out_shape=(shape, shape),
         input_output_aliases={3 + number: number for number in range(len(kept))},
         compiler_params=limit(20),
-        cost_estimate=estimate(0.02),
+        cost_estimate=estimate(8),
     )(core.reshape(1), own, other, *kept)
 
 
@@ -235,7 +235,7 @@
         out_shape=(shape, shape),
         input_output_aliases={6 + number: number for number in range(len(kept))},
         compiler_params=limit(20),
-        cost_estimate=estimate(0.02),
+        cost_estimate=estimate(4),
     )(core.reshape(1), sides, *pieces, *kept)
 
 
@@ -478,7 +478,7 @@
     _, length, width = hidden.shape
     units = up.shape[0]
     kept = [] if mid_parts is None else [mid_parts]
-    block = 576
+    block = 768
     steps = -(-units // block)
 
     def kernel(
@@ -851,20 +851,14 @@
     ff_core_move(1)
     ff_sides = jnp.stack([side[stream.pairs[0]] for stream in ff_streams])
 
-    def ff_begin(first):
-        members = ff_streams[first : first + 2]
-        halves = order.run(
-            lambda ready: ff_own(
-                core, ff_sides[first : first + 2], [pairs[0], ready], cotangent, middles, lefts,
-                rights, ff_rows[first : first + 2], sum(ff_rows[:first]),
-            ),
-            pairs[1],
-        )
-        for n, stream in enumerate(members):
-            stream.begin(*halves.value[2 * n : 2 * n + 2])
-
-    ff_begin(0)
-    ff_begin(2)
+    halves = order.run(
+        lambda ready: ff_own(
+            core, ff_sides, [pairs[0], ready], cotangent, middles, lefts, rights, ff_rows, 0
+        ),
+        pairs[1],
+    )
+    for n, stream in enumerate(ff_streams):
+        stream.begin(*halves.value[2 * n : 2 * n + 2])
     with jax.named_scope("mid_move"):
         mid_received = swap_tensor(middle[rows - 1].value[3])
     back(0, mid_received)
@@ -890,7 +884,7 @@
         with jax.named_scope("normed_move_" + str(row)):
             return swap_tensor(normed_part[row].value)
 
-    output_row(0, ff_step(output_move(0)))
+    output_received = ff_step(output_move(0))
     late = []
     for row in range(rows):
         with jax.named_scope("late_core_move_" + str(row)):
@@ -915,6 +909,7 @@
         for row in range(rows)
     ]
     ff_step()
+    output_row(0, output_received)
     normed_received = [ff_step(normed_move(0))]
     normed_received.append(ff_step(normed_move(1)))
     normed_grad = order.run(
@@ -923,6 +918,10 @@
         ),
         normed_part[0].value,
     )
+    normed_grad.value, sum_dq, sum_dv, sum_pairs, sum_cotangent = lax.optimization_barrier(
+        (normed_grad.value, dq, dv, pairs, cotangent)
+    )
+
     pre_normal, pre_factor = normalized(hidden_in.reshape(tokens, width).astype(jnp.float32))
     pre_gain_grad = jnp.sum(normed_grad.value * pre_normal, axis=0)
     pre_shift_grad = jnp.sum(normed_grad.value, axis=0)
@@ -940,10 +939,10 @@
             terms[2],
             terms[0],
             terms[1],
-            jnp.sum(cotangent.astype(jnp.float32), axis=(0, 1)),
-            token_sum(dq),
-            token_sum(dv),
-            token_sum([pair[1, :hidden] for pair in pairs]),
+            jnp.sum(sum_cotangent.astype(jnp.float32), axis=(0, 1)),
+            token_sum(sum_dq),
+            token_sum(sum_dv),
+            token_sum([pair[1, :hidden] for pair in sum_pairs]),
             jnp.zeros((2 * width - hidden,), jnp.float32),
         ]
     ).reshape(9, width)

time: 402 us -> 393 us (0.978)
  Pallas kernels: 130 us -> 115 us
  waiting for transfers between devices: 100 us -> 105 us
  local copies, waits for them, and re-layouts: 19.7 us -> 15.6 us
    pallas_call x4, Pallas kernels: 21 us -> 10.6 us  [pick_halves(): pl.pallas_call(kernel, grid_spec=pltpu.PrefetchScalarGridSpec(num_scalar_...]
    all_gather x1, waiting for transfers between devices: 0.02 us -> 5.43 us  [shards(): lax.all_gather(at_block.value, 'dp', axis_index_groups=PLANES, axis=0, ti...]
    ppermute x64, waiting for transfers between devices: 72 us -> 66.6 us  [swap(): return lax.ppermute(values, 'dp', PAIRS[pair])]
    ppermute x7, waiting for transfers between devices: 28.4 us -> 32.7 us  [swap_tensor(): return lax.ppermute(values, 'tensor', [(0, 1), (1, 0)])]
    pallas_call x2 -> x1, Pallas kernels: 20.4 us -> 17.1 us  [ff_own(): pl.pallas_call(kernel, grid_spec=pltpu.PrefetchScalarGridSpec(num_scalar_...]
    unnamed x134 -> x132, local copies, waits for them, and re-layouts: 12.8 us -> 10.2 us
  transfers between devices with their start and end apart: 73 -> 73, of which waited for: 26 -> 31; matrix products, arithmetic and copies ran while one was open for 10% -> 10% of each run, Pallas kernels for 26% -> 22%
where the time goes in v4:
time: 393 us; the launch traced here: 385 us
  Pallas kernels  115 us (29%)
  waiting for transfers between devices  105 us (27%)
  starting transfers between devices  92.1 us (23%)
  other arithmetic  37.7 us (10%)
  local copies, waits for them, and re-layouts  15.6 us (4%)
  between operations  15.4 us (4%)
  matrix products  4.38 us (1%)
    ppermute x64, starting transfers between devices, swap(): return lax.ppermute(values, 'dp', PAIRS[pair])  83.9 us
    ppermute x64, waiting for transfers between devices, swap(): return lax.ppermute(values, 'dp', PAIRS[pair])  66.6 us
    ppermute x7, waiting for transfers between devices, swap_tensor(): return lax.ppermute(values, 'tensor', [(0, 1), (1, 0)])  32.7 us
    pallas_call x2, Pallas kernels, feed_forward(): pl.pallas_call(kernel, grid=(steps,), in_specs=[scalars(), at_row] + [who...  27.6 us
    pallas_call x2, Pallas kernels, attention_backward(): pl.pallas_call(kernel, grid=(1,), in_specs=[scalars(), scalars()] + [pl.B...  21.5 us
    pallas_call x2, Pallas kernels, attention_forward(): pl.pallas_call(kernel, grid=(1,), in_specs=[scalars(), pl.BlockSpec((1, l...  19.5 us
    pallas_call x1, Pallas kernels, ff_own(): pl.pallas_call(kernel, grid_spec=pltpu.PrefetchScalarGridSpec(num_scalar_...  17.1 us
    add x12, other arithmetic, step(): self.keep = take(keep, side) + take(received, side)  11.2 us
  transfers between devices with their start and end apart: 73, of which 31 were waited for; matrix products, arithmetic and copies ran while one was open for 10% of the time, Pallas kernels for 22%

profile of v4, /device:TPU:1, one launch (start us, length us, event | category | flops | bytes accessed | tf_op | source)
XLA Modules:
  0.0 385.2 jit_solution(17714421360093791072)
XLA Ops:
  7.2 9.7 %shard_map.305 = (bf16[192,1152]{1,0:T(8,128)(2,1)}, bf16[576,192]{1,0:T(8,128)(2,1)}, bf16[576,192]{1,0:T(8,128)(2,1)}, bf16[576,192]{1,0:T(8,128)(2,1)}, bf16[...) custom-call(s32[2,4]{1,0:T(2,128)} %layout_ref.7, ...), custom_call_target="tpu_custom_call" | custom-call | flops 23000000512 | bytes 1024 | tf_op jit(solution)/shard_map/pallas_call | solution.py:357
  20.5 9.7 %shard_map.306 = (bf16[192,1152]{1,0:T(8,128)(2,1)}, bf16[576,192]{1,0:T(8,128)(2,1)}, bf16[576,192]{1,0:T(8,128)(2,1)}, bf16[576,192]{1,0:T(8,128)(2,1)}, bf16[...) custom-call(s32[2,4]{1,0:T(2,128)} %layout_ref.7, ...), custom_call_target="tpu_custom_call" | custom-call | flops 23000000512 | bytes 1024 | tf_op jit(solution)/shard_map/pallas_call | solution.py:357
  32.2 6.9 %collective-permute-done.received_ref = f32[192,1152]{1,0:T(8,128)S(1)} collective-permute-done((f32[192,1152]{1,0:T(8,128)}, f32[192,1152]{1,0:T(8,128)S(1)}, u32[]{:S(2)}, u32[]{:S(2)}) %collective-permute-start) | collective-permute-done | bytes 884768 | tf_op jit(solution)/shard_map/branch_move_0/ppermute | solution.py:60
  41.4 13.8 %shard_map.307 = (f32[192,1152]{1,0:T(8,128)}, bf16[192,1152]{1,0:T(8,128)(2,1)}, bf16[2,2304,192]{2,1,0:T(8,128)(2,1)}, f32[384,1152]{1,0:T(8,128)}, f32[192,11...) custom-call(s32[1]{0:T(128)} %bitcast.core_ref, bf16[2,192,1152]{2,1,0:T(8,128)(2,1)} %hidden_ref.6, ...), custom_call_target="tpu_custom_call" | custom-call | flops 34500001792 | bytes 1024 | tf_op jit(solution)/shard_map/pallas_call | solution.py:552
  58.2 13.8 %shard_map.308 = (f32[192,1152]{1,0:T(8,128)}, bf16[192,1152]{1,0:T(8,128)(2,1)}, bf16[2,2304,192]{2,1,0:T(8,128)(2,1)}, f32[384,1152]{1,0:T(8,128)}, f32[192,11...) custom-call(s32[1]{0:T(128)} %bitcast.core_ref, ...), custom_call_target="tpu_custom_call", output_to_operand_aliasing={{3}: (11, {})} | custom-call | flops 34500001792 | bytes 1024 | tf_op jit(solution)/shard_map/pallas_call | solution.py:552
  80.0 17.1 %shard_map.309 = (f32[288,1152]{1,0:T(8,128)}, f32[288,1152]{1,0:T(8,128)}, f32[288,1152]{1,0:T(8,128)}, f32[288,1152]{1,0:T(8,128)}, f32[288,1152]{1,0:T(8,128)...) custom-call(s32[1]{0:T(128)} %bitcast.core_ref, s32[4]{0:T(128)} %pad_add_fusion.sides_ref, ...), custom_call_target="tpu_custom_call" | custom-call | flops 4600000000 | bytes 1024 | tf_op jit(solution)/shard_map/pallas_call | solution.py:646
  102.8 11.7 %collective-permute-done.10.received_ref = f32[384,1152]{1,0:T(8,128)S(1)} collective-permute-done((f32[384,1152]{1,0:T(8,128)}, f32[384,1152]{1,0:T(8,128)S(1)}, u32[]{:S(2)}, u32[]{:S(2)}) %collective-permute-start.10) | collective-permute-done | bytes 1769504 | tf_op jit(solution)/shard_map/mid_move/ppermute | solution.py:60
  116.1 10.8 %shard_map.310 = (f32[192,1152]{1,0:T(8,128)}, bf16[192,1152]{1,0:T(8,128)(2,1)}, f32[8,1152]{1,0:T(8,128)}, bf16[576,192]{1,0:T(8,128)(2,1)}, bf16[576,192]{1,0...) custom-call(s32[1]{0:T(128)} %bitcast.core_ref, s32[2,4]{1,0:T(2,128)} %layout_ref.7, ...), custom_call_target="tpu_custom_call" | custom-call | flops 23000000 | bytes 1024 | tf_op jit(solution)/shard_map/pallas_call | solution.py:447
  126.9 10.7 %shard_map.311 = (f32[192,1152]{1,0:T(8,128)}, bf16[192,1152]{1,0:T(8,128)(2,1)}, f32[8,1152]{1,0:T(8,128)}, bf16[576,192]{1,0:T(8,128)(2,1)}, bf16[576,192]{1,0...) custom-call(s32[1]{0:T(128)} %bitcast.core_ref, s32[2,4]{1,0:T(2,128)} %layout_ref.7, ...), custom_call_target="tpu_custom_call" | custom-call | flops 23000000 | bytes 1024 | tf_op jit(solution)/shard_map/pallas_call | solution.py:447
  150.5 9.8 %shard_map.312 = f32[1152,1152]{1,0:T(8,128)} custom-call(s32[1]{0:T(128)} %bitcast.core_ref, bf16[576,192]{1,0:T(8,128)(2,1)} %get-tuple-element.496.refs_0_, bf16[576,192]{1,0:T(8,128)(2,1)} %get-tuple-element.497.refs_1_, bf16[576,192]{1,0:T(8,128)(2,1)} %get-tuple-element.431.refs_2_, bf16[576,192]{1,0:T(8,128)(2,1)} %get-tuple-element.403.refs_3_, ...), custom_call_target="tpu_custom_call" | custom-call | flops 23000000 | bytes 1024 | tf_op jit(solution)/shard_map/pallas_call | solution.py:725
  175.9 6.5 %collective-permute-done.23 = f32[2,72,1152]{2,1,0:T(8,128)S(1)} collective-permute-done((f32[2,72,1152]{2,1,0:T(8,128)}, f32[2,72,1152]{2,1,0:T(8,128)S(1)}, u32[]{:S(2)}, u32[]{:S(2)}) %collective-permute-start.23) | collective-permute-done | bytes 663584 | tf_op jit(solution)/shard_map/ff3_move_2/ppermute | solution.py:56
  185.6 3.5 collective-permute-done.21
  196.0 7.3 %collective-permute-done.27 = f32[1,72,1152]{2,1,0:T(8,128)S(1)} collective-permute-done((f32[1,72,1152]{2,1,0:T(8,128)S(1)}, f32[1,72,1152]{2,1,0:T(8,128)S(1)}, u32[]{:S(2)}, u32[]{:S(2)}) %collective-permute-start.27) | collective-permute-done | bytes 331808 | tf_op jit(solution)/shard_map/ff3_move_3/ppermute | solution.py:56
  235.5 4.3 %collective-permute-done.38 = f32[9,1152]{1,0:T(8,128)S(1)} collective-permute-done((f32[9,1152]{1,0:T(8,128)S(1)}, f32[9,1152]{1,0:T(8,128)S(1)}, u32[]{:S(2)}, u32[]{:S(2)}) %collective-permute-start.38) | collective-permute-done | bytes 41504 | tf_op jit(solution)/shard_map/small_move_z/ppermute | solution.py:56
  240.0 4.2 %collective-permute-start.42 = (f32[1,36,1152]{2,1,0:T(8,128)S(1)}, f32[1,36,1152]{2,1,0:T(8,128)S(1)}, u32[]{:S(2)}, u32[]{:S(2)}) collective-permute-start(f32[1,36,1152]{2,1,0:T(8,128)S(1)} %add.321), channel_id=1, source_target_pairs={{0,48},{2,50},{4,52},{6,54},{8,56},{10,58},{12,60},{14,62},{16,32}... | collective-permute-start | bytes 497672 | tf_op jit(solution)/shard_map/ff3_move_6/ppermute | solution.py:56
  266.0 6.5 %collective-permute-done.52 = f32[2,72,1152]{2,1,0:T(8,128)} collective-permute-done((f32[2,72,1152]{2,1,0:T(8,128)S(1)}, f32[2,72,1152]{2,1,0:T(8,128)}, u32[]{:S(2)}, u32[]{:S(2)}) %collective-permute-start.52) | collective-permute-done | bytes 663584 | tf_op jit(solution)/shard_map/ff3_move_8/ppermute | solution.py:56
  287.8 11.5 %collective-permute-done.58 = f32[192,1152]{1,0:T(8,128)S(1)} collective-permute-done((f32[192,1152]{1,0:T(8,128)}, f32[192,1152]{1,0:T(8,128)S(1)}, u32[]{:S(2)}, u32[]{:S(2)}) %collective-permute-start.58) | collective-permute-done | bytes 884768 | tf_op jit(solution)/shard_map/output_move_1/ppermute | solution.py:60
  299.3 16.1 %collective-permute-start.59 = (f32[288,1152]{1,0:T(8,128)}, f32[288,1152]{1,0:T(8,128)S(1)}, u32[]{:S(2)}, u32[]{:S(2)}) collective-permute-start(f32[288,1152]{1,0:T(8,128)} %bitcast.62), channel_id=1, source_target_pairs={{0,2},{2,0},{4,6},{6,4},{8,10},{10,8},{12,14},{14,12},{16,18},{18,... | collective-permute-start | bytes 3981320 | tf_op jit(solution)/shard_map/ff_core_other_0/ppermute | solution.py:56
  315.4 8.4 %collective-permute-start.65 = (f32[288,1152]{1,0:T(8,128)}, f32[288,1152]{1,0:T(8,128)S(1)}, u32[]{:S(2)}, u32[]{:S(2)}) collective-permute-start(f32[288,1152]{1,0:T(8,128)} %bitcast.60), channel_id=1, source_target_pairs={{0,2},{2,0},{4,6},{6,4},{8,10},{10,8},{12,14},{14,12},{16,18},{18,... | collective-permute-start | bytes 3981320 | tf_op jit(solution)/shard_map/ff_core_other_1/ppermute | solution.py:56
  325.4 3.7 fusion
  351.6 5.4 %all-gather.2.cloned.1.call-done.own_ref = f32[1152,1152]{1,0:T(8,128)} async-done(((f32[72,1152]{1,0:T(8,128)}), f32[1152,1152]{1,0:T(8,128)}) %all-gather.2.cloned.1.call-update) | async-done | bytes 5308432 | tf_op jit(solution)/shard_map/at_gather/all_gather | solution.py:968
  360.7 5.7 %collective-permute-done.70.other_ref = f32[1152,1152]{1,0:T(8,128)} collective-permute-done((f32[1152,1152]{1,0:T(8,128)}, f32[1152,1152]{1,0:T(8,128)}, u32[]{:S(2)}, u32[]{:S(2)}) %collective-permute-start.70) | collective-permute-done | bytes 5308448 | tf_op jit(solution)/shard_map/at_core_back/ppermute | solution.py:56
  368.9 4.5 %shard_map.318 = (f32[576,1152]{1,0:T(8,128)}, f32[576,1152]{1,0:T(8,128)}) custom-call(s32[1]{0:T(128)} %bitcast.core_ref, f32[1152,1152]{1,0:T(8,128)S(1)} %copy-done.2, f32[1152,1152]{1,0:T(8,128)} %collective-permute-done.70.other_ref), custom_call_target="tpu_custom_call" | custom-call | flops 9200000000 | bytes 1024 | tf_op jit(solution)/shard_map/pallas_call | solution.py:178
  373.4 4.5 %shard_map.317 = (f32[576,1152]{1,0:T(8,128)}, f32[576,1152]{1,0:T(8,128)}) custom-call(s32[1]{0:T(128)} %bitcast.core_ref, f32[1152,1152]{1,0:T(8,128)S(1)} %copy-done.2, f32[1152,1152]{1,0:T(8,128)} %collective-permute-done.70.other_ref), custom_call_target="tpu_custom_call" | custom-call | flops 9200000000 | bytes 1024 | tf_op jit(solution)/shard_map/pallas_call | solution.py:178
  (348 shorter events, 163.4 us)
Async XLA Ops:
  7.2 257.3 %reduce-scatter.4.cloned.1.call-start = ((), (), s32[]{:S(2)}) async-start(), calls=%async_computation.2 | async-start | bytes 5640192
  17.0 22.1 %collective-permute-start = (f32[192,1152]{1,0:T(8,128)}, f32[192,1152]{1,0:T(8,128)S(1)}, u32[]{:S(2)}, u32[]{:S(2)}) collective-permute-start(f32[192,1152]{1,0:T(8,128)} %get-tuple-element.328.branch_ref), channel_id=1, source_target_pairs={{0,1},{1,0},{2,3},{3,2},{4,5},{5,4},{6,7},{7,6},{8,9},{9,8},{10,11... | collective-permute-start | bytes 2654216 | tf_op jit(solution)/shard_map/branch_move_0/ppermute | solution.py:60
  19.5 35.7 %collective-permute-start.1 = (f32[192,1152]{1,0:T(8,128)}, f32[192,1152]{1,0:T(8,128)S(1)}, u32[]{:S(2)}, u32[]{:S(2)}) collective-permute-start(f32[192,1152]{1,0:T(8,128)} %get-tuple-element.336), channel_id=1, source_target_pairs={{0,2},{2,0},{4,6},{6,4},{8,10},{10,8},{12,14},{14,12},{16,18},{18,... | collective-permute-start | bytes 2654216 | tf_op jit(solution)/shard_map/early_core_move_0/ppermute | solution.py:56
  20.5 34.7 %collective-permute-start.2 = (f32[576,256]{1,0:T(8,128)}, f32[576,256]{1,0:T(8,128)S(1)}, u32[]{:S(2)}, u32[]{:S(2)}) collective-permute-start(f32[576,256]{1,0:T(8,128)} %get-tuple-element.337), channel_id=1, source_target_pairs={{0,2},{2,0},{4,6},{6,4},{8,10},{10,8},{12,14},{14,12},{16,18},{18,... | collective-permute-start | bytes 1769480 | tf_op jit(solution)/shard_map/early_core_move_0/ppermute | solution.py:56
  30.2 27.9 %collective-permute-start.3 = (f32[192,1152]{1,0:T(8,128)}, f32[192,1152]{1,0:T(8,128)}, u32[]{:S(2)}, u32[]{:S(2)}) collective-permute-start(f32[192,1152]{1,0:T(8,128)} %get-tuple-element.348.branch_ref), channel_id=1, source_target_pairs={{0,1},{1,0},{2,3},{3,2},{4,5},{5,4},{6,7},{7,6},{8,9},{9,8},{10,11... | collective-permute-start | bytes 2654216 | tf_op jit(solution)/shard_map/branch_move_1/ppermute | solution.py:60
  30.2 41.8 %collective-permute-start.4 = (f32[192,1152]{1,0:T(8,128)}, f32[192,1152]{1,0:T(8,128)S(1)}, u32[]{:S(2)}, u32[]{:S(2)}) collective-permute-start(f32[192,1152]{1,0:T(8,128)} %get-tuple-element.357), channel_id=1, source_target_pairs={{0,2},{2,0},{4,6},{6,4},{8,10},{10,8},{12,14},{14,12},{16,18},{18,... | collective-permute-start | bytes 2654216 | tf_op jit(solution)/shard_map/early_core_move_1/ppermute | solution.py:56
  39.1 32.9 %collective-permute-start.5 = (f32[576,256]{1,0:T(8,128)}, f32[576,256]{1,0:T(8,128)S(1)}, u32[]{:S(2)}, u32[]{:S(2)}) collective-permute-start(f32[576,256]{1,0:T(8,128)} %get-tuple-element.358), channel_id=1, source_target_pairs={{0,2},{2,0},{4,6},{6,4},{8,10},{10,8},{12,14},{14,12},{16,18},{18,... | collective-permute-start | bytes 1769480 | tf_op jit(solution)/shard_map/early_core_move_1/ppermute | solution.py:56
  74.2 40.4 %collective-permute-start.10 = (f32[384,1152]{1,0:T(8,128)}, f32[384,1152]{1,0:T(8,128)S(1)}, u32[]{:S(2)}, u32[]{:S(2)}) collective-permute-start(f32[384,1152]{1,0:T(8,128)} %get-tuple-element.395.part_ref), channel_id=1, source_target_pairs={{0,1},{1,0},{2,3},{3,2},{4,5},{5,4},{6,7},{7,6},{8,9},{9,8},{10,11... | collective-permute-start | bytes 5308424 | tf_op jit(solution)/shard_map/mid_move/ppermute | solution.py:60
  97.1 41.7 %collective-permute-start.14 = (f32[4,72,1152]{2,1,0:T(8,128)}, f32[4,72,1152]{2,1,0:T(8,128)S(1)}, u32[]{:S(2)}, u32[]{:S(2)}) collective-permute-start(f32[4,72,1152]{2,1,0:T(8,128)} %bitcast.92), channel_id=1, source_target_pairs={{0,12},{2,14},{4,8},{6,10},{8,4},{10,6},{12,0},{14,2},{16,28},{18,... | collective-permute-start | bytes 3981320 | tf_op jit(solution)/shard_map/ff3_move_1/ppermute | solution.py:56
  99.8 39.8 %collective-permute-start.11 = (f32[4,72,1152]{2,1,0:T(8,128)}, f32[4,72,1152]{2,1,0:T(8,128)}, u32[]{:S(2)}, u32[]{:S(2)}) collective-permute-start(f32[4,72,1152]{2,1,0:T(8,128)} %bitcast.91), channel_id=1, source_target_pairs={{0,16},{2,18},{4,20},{6,22},{8,24},{10,26},{12,28},{14,30},{16,0},... | collective-permute-start | bytes 3981320 | tf_op jit(solution)/shard_map/ff0_move_1/ppermute | solution.py:56
  101.0 38.7 %collective-permute-start.12 = (f32[4,72,1152]{2,1,0:T(8,128)}, f32[4,72,1152]{2,1,0:T(8,128)}, u32[]{:S(2)}, u32[]{:S(2)}) collective-permute-start(f32[4,72,1152]{2,1,0:T(8,128)} %bitcast.90), channel_id=1, source_target_pairs={{0,4},{2,6},{4,0},{6,2},{8,12},{10,14},{12,8},{14,10},{16,20},{18,... | collective-permute-start | bytes 3981320 | tf_op jit(solution)/shard_map/ff1_move_1/ppermute | solution.py:56
  101.0 39.1 %collective-permute-start.13 = (f32[4,72,1152]{2,1,0:T(8,128)}, f32[4,72,1152]{2,1,0:T(8,128)}, u32[]{:S(2)}, u32[]{:S(2)}) collective-permute-start(f32[4,72,1152]{2,1,0:T(8,128)} %bitcast.89), channel_id=1, source_target_pairs={{0,48},{2,50},{4,52},{6,54},{8,56},{10,58},{12,60},{14,62},{16,32}... | collective-permute-start | bytes 3981320 | tf_op jit(solution)/shard_map/ff2_move_1/ppermute | solution.py:56
  114.6 23.0 %collective-permute-start.15 = (f32[192,1152]{1,0:T(8,128)S(1)}, f32[192,1152]{1,0:T(8,128)S(1)}, u32[]{:S(2)}, u32[]{:S(2)}) collective-permute-start(f32[192,1152]{1,0:T(8,128)S(1)} %copy-done.35), channel_id=1, source_target_pairs={{0,1},{1,0},{2,3},{3,2},{4,5},{5,4},{6,7},{7,6},{8,9},{9,8},{10,11... | collective-permute-start | bytes 2654216 | tf_op jit(solution)/shard_map/output_move_0/ppermute | solution.py:60
  160.4 196.6 %all-gather.2.cloned.1.call-start = ((), (), s32[]{:S(2)}) async-start(), calls=%async_computation.1 | async-start | bytes 5640192 | tf_op jit(solution)/shard_map/at_gather/all_gather | solution.py:968
  162.1 20.2 %collective-permute-start.23 = (f32[2,72,1152]{2,1,0:T(8,128)}, f32[2,72,1152]{2,1,0:T(8,128)S(1)}, u32[]{:S(2)}, u32[]{:S(2)}) collective-permute-start(f32[2,72,1152]{2,1,0:T(8,128)} %get-tuple-element.452), channel_id=1, source_target_pairs={{0,16},{2,18},{4,20},{6,22},{8,24},{10,26},{12,28},{14,30},{16,0},... | collective-permute-start | bytes 1990664 | tf_op jit(solution)/shard_map/ff3_move_2/ppermute | solution.py:56
  163.4 22.2 %collective-permute-start.22 = (f32[2,72,1152]{2,1,0:T(8,128)}, f32[2,72,1152]{2,1,0:T(8,128)S(1)}, u32[]{:S(2)}, u32[]{:S(2)}) collective-permute-start(f32[2,72,1152]{2,1,0:T(8,128)} %get-tuple-element.451), channel_id=1, source_target_pairs={{0,12},{2,14},{4,8},{6,10},{8,4},{10,6},{12,0},{14,2},{16,28},{18,... | collective-permute-start | bytes 1990664 | tf_op jit(solution)/shard_map/ff2_move_2/ppermute | solution.py:56
  166.2 22.9 %collective-permute-start.21 = (f32[2,72,1152]{2,1,0:T(8,128)}, f32[2,72,1152]{2,1,0:T(8,128)S(1)}, u32[]{:S(2)}, u32[]{:S(2)}) collective-permute-start(f32[2,72,1152]{2,1,0:T(8,128)} %get-tuple-element.450), channel_id=1, source_target_pairs={{0,48},{2,50},{4,52},{6,54},{8,56},{10,58},{12,60},{14,62},{16,32}... | collective-permute-start | bytes 1990664 | tf_op jit(solution)/shard_map/ff1_move_2/ppermute | solution.py:56
  168.0 22.7 %collective-permute-start.20 = (f32[2,72,1152]{2,1,0:T(8,128)}, f32[2,72,1152]{2,1,0:T(8,128)S(1)}, u32[]{:S(2)}, u32[]{:S(2)}) collective-permute-start(f32[2,72,1152]{2,1,0:T(8,128)} %get-tuple-element.449), channel_id=1, source_target_pairs={{0,4},{2,6},{4,0},{6,2},{8,12},{10,14},{12,8},{14,10},{16,20},{18,... | collective-permute-start | bytes 1990664 | tf_op jit(solution)/shard_map/ff0_move_2/ppermute | solution.py:56
  174.9 20.1 %collective-permute-start.28 = (f32[192,1152]{1,0:T(8,128)S(1)}, f32[192,1152]{1,0:T(8,128)S(1)}, u32[]{:S(2)}, u32[]{:S(2)}) collective-permute-start(f32[192,1152]{1,0:T(8,128)S(1)} %convolution_add_fusion.2), channel_id=1, source_target_pairs={{0,1},{1,0},{2,3},{3,2},{4,5},{5,4},{6,7},{7,6},{8,9},{9,8},{10,11... | collective-permute-start | bytes 2654216 | tf_op jit(solution)/shard_map/normed_move_0/ppermute | solution.py:60
  285.6 29.8 %collective-permute-start.57 = (f32[4,72,1152]{2,1,0:T(8,128)S(1)}, f32[4,72,1152]{2,1,0:T(8,128)S(1)}, u32[]{:S(2)}, u32[]{:S(2)}) collective-permute-start(f32[4,72,1152]{2,1,0:T(8,128)S(1)} %maximum_select_fusion.3), channel_id=1, source_target_pairs={{0,12},{2,14},{4,8},{6,10},{8,4},{10,6},{12,0},{14,2},{16,28},{18,... | collective-permute-start | bytes 3981320 | tf_op jit(solution)/shard_map/ff3_move_9/ppermute | solution.py:56
  286.6 37.2 %collective-permute-start.56 = (f32[4,72,1152]{2,1,0:T(8,128)S(1)}, f32[4,72,1152]{2,1,0:T(8,128)S(1)}, u32[]{:S(2)}, u32[]{:S(2)}) collective-permute-start(f32[4,72,1152]{2,1,0:T(8,128)S(1)} %maximum_select_fusion.2), channel_id=1, source_target_pairs={{0,48},{2,50},{4,52},{6,54},{8,56},{10,58},{12,60},{14,62},{16,32}... | collective-permute-start | bytes 3981320 | tf_op jit(solution)/shard_map/ff2_move_9/ppermute | solution.py:56
  287.1 36.6 %collective-permute-start.55 = (f32[4,72,1152]{2,1,0:T(8,128)}, f32[4,72,1152]{2,1,0:T(8,128)S(1)}, u32[]{:S(2)}, u32[]{:S(2)}) collective-permute-start(f32[4,72,1152]{2,1,0:T(8,128)} %maximum_select_fusion.1), channel_id=1, source_target_pairs={{0,4},{2,6},{4,0},{6,2},{8,12},{10,14},{12,8},{14,10},{16,20},{18,... | collective-permute-start | bytes 3981320 | tf_op jit(solution)/shard_map/ff1_move_9/ppermute | solution.py:56
  287.1 36.6 %collective-permute-start.54 = (f32[4,72,1152]{2,1,0:T(8,128)}, f32[4,72,1152]{2,1,0:T(8,128)S(1)}, u32[]{:S(2)}, u32[]{:S(2)}) collective-permute-start(f32[4,72,1152]{2,1,0:T(8,128)} %maximum_select_fusion), channel_id=1, source_target_pairs={{0,16},{2,18},{4,20},{6,22},{8,24},{10,26},{12,28},{14,30},{16,0},... | collective-permute-start | bytes 3981320 | tf_op jit(solution)/shard_map/ff0_move_9/ppermute | solution.py:56
  299.3 30.4 %collective-permute-start.59 = (f32[288,1152]{1,0:T(8,128)}, f32[288,1152]{1,0:T(8,128)S(1)}, u32[]{:S(2)}, u32[]{:S(2)}) collective-permute-start(f32[288,1152]{1,0:T(8,128)} %bitcast.62), channel_id=1, source_target_pairs={{0,2},{2,0},{4,6},{6,4},{8,10},{10,8},{12,14},{14,12},{16,18},{18,... | collective-permute-start | bytes 3981320 | tf_op jit(solution)/shard_map/ff_core_other_0/ppermute | solution.py:56
  (115 other events, 867.7 us)
Sparse Core Ops, SparseCore 0:
  160.5 86.7 reduce-scatter.3
  285.7 71.2 all-gather.1

commit v5 on v4

--- a/solution.py
+++ b/solution.py
@@ -988,13 +988,16 @@
     input_low, small.value, at_whole, down_grad = lax.optimization_barrier(
         (low(input_grad), small.value, at_whole, down_grad)
     )
-    with jax.named_scope("at_core_back"):
-        received = swap(at_whole, "core")
+    at_parts = [at_whole[:heads_wide], at_whole[heads_wide:]]
+    at_others = []
+    for number, part in enumerate(at_parts):
+        with jax.named_scope("at_core_back_" + str(number)):
+            at_others.append(swap(part, "core"))
     query_weight_grad, value_weight_grad = pick_rows(
-        core, at_whole, received, heads_wide, 192, 0, 0, heads_wide
+        core, at_parts[0], at_others[0], heads_wide, 192, 0, 0, heads_wide
     )
     key_weight_grad, out_grad = pick_rows(
-        core, at_whole, received, heads_wide, 192, heads_wide, 0, heads_wide
+        core, at_parts[1], at_others[1], heads_wide, 192, 0, 0, heads_wide
     )
     small = small.value
     return (

time: 393 us -> 401 us (1.020)
  other arithmetic: 37.7 us -> 44.9 us
    slice x0 -> x1, local copies, waits for them, and re-layouts: none -> 4.39 us  [shards(): at_parts = [at_whole[:heads_wide], at_whole[heads_wide:]]]
    unnamed x132 -> x118, local copies, waits for them, and re-layouts: 10.2 us -> 6.41 us
    ppermute x64 -> x65, waiting for transfers between devices: 66.6 us -> 68.7 us  [swap(): return lax.ppermute(values, 'dp', PAIRS[pair])]
    ppermute x64 -> x65, starting transfers between devices: 83.9 us -> 83.2 us  [swap(): return lax.ppermute(values, 'dp', PAIRS[pair])]
  transfers between devices with their start and end apart: 73 -> 74, of which waited for: 31 -> 29; matrix products, arithmetic and copies ran while one was open for 10% -> 12% of each run, Pallas kernels for 22% -> 23%
where the time goes in v5:
time: 401 us; the launch traced here: 394 us
  Pallas kernels  116 us (29%)
  waiting for transfers between devices  106 us (26%)
  starting transfers between devices  91 us (23%)
  other arithmetic  44.9 us (11%)
  local copies, waits for them, and re-layouts  17.1 us (4%)
  between operations  15.4 us (4%)
    ppermute x65, starting transfers between devices, swap(): return lax.ppermute(values, 'dp', PAIRS[pair])  83.2 us
    ppermute x65, waiting for transfers between devices, swap(): return lax.ppermute(values, 'dp', PAIRS[pair])  68.7 us
    ppermute x7, waiting for transfers between devices, swap_tensor(): return lax.ppermute(values, 'tensor', [(0, 1), (1, 0)])  32.6 us
    pallas_call x2, Pallas kernels, feed_forward(): pl.pallas_call(kernel, grid=(steps,), in_specs=[scalars(), at_row] + [who...  27.5 us
    pallas_call x2, Pallas kernels, attention_backward(): pl.pallas_call(kernel, grid=(1,), in_specs=[scalars(), scalars()] + [pl.B...  21.4 us
    pallas_call x2, Pallas kernels, attention_forward(): pl.pallas_call(kernel, grid=(1,), in_specs=[scalars(), pl.BlockSpec((1, l...  19.5 us
    pallas_call x1, Pallas kernels, ff_own(): pl.pallas_call(kernel, grid_spec=pltpu.PrefetchScalarGridSpec(num_scalar_...  17.1 us
    add x12, other arithmetic, step(): self.keep = take(keep, side) + take(received, side)  12.8 us
  transfers between devices with their start and end apart: 74, of which 29 were waited for; matrix products, arithmetic and copies ran while one was open for 12% of the time, Pallas kernels for 23%

profile of v5, /device:TPU:1, one launch (start us, length us, event | category | flops | bytes accessed | tf_op | source)
XLA Modules:
  0.0 393.7 jit_solution(6225251486469751338)
XLA Ops:
  7.2 9.7 %shard_map.305 = (bf16[192,1152]{1,0:T(8,128)(2,1)}, bf16[576,192]{1,0:T(8,128)(2,1)}, bf16[576,192]{1,0:T(8,128)(2,1)}, bf16[576,192]{1,0:T(8,128)(2,1)}, bf16[...) custom-call(s32[2,4]{1,0:T(2,128)} %layout_ref.7, ...), custom_call_target="tpu_custom_call" | custom-call | flops 23000000512 | bytes 1024 | tf_op jit(solution)/shard_map/pallas_call | solution.py:357
  20.5 9.7 %shard_map.306 = (bf16[192,1152]{1,0:T(8,128)(2,1)}, bf16[576,192]{1,0:T(8,128)(2,1)}, bf16[576,192]{1,0:T(8,128)(2,1)}, bf16[576,192]{1,0:T(8,128)(2,1)}, bf16[...) custom-call(s32[2,4]{1,0:T(2,128)} %layout_ref.7, ...), custom_call_target="tpu_custom_call" | custom-call | flops 23000000512 | bytes 1024 | tf_op jit(solution)/shard_map/pallas_call | solution.py:357
  32.2 6.9 %collective-permute-done.received_ref = f32[192,1152]{1,0:T(8,128)S(1)} collective-permute-done((f32[192,1152]{1,0:T(8,128)}, f32[192,1152]{1,0:T(8,128)S(1)}, u32[]{:S(2)}, u32[]{:S(2)}) %collective-permute-start) | collective-permute-done | bytes 884768 | tf_op jit(solution)/shard_map/branch_move_0/ppermute | solution.py:60
  41.4 13.8 %shard_map.307 = (f32[192,1152]{1,0:T(8,128)}, bf16[192,1152]{1,0:T(8,128)(2,1)}, bf16[2,2304,192]{2,1,0:T(8,128)(2,1)}, f32[384,1152]{1,0:T(8,128)}, f32[192,11...) custom-call(s32[1]{0:T(128)} %bitcast.core_ref, bf16[2,192,1152]{2,1,0:T(8,128)(2,1)} %hidden_ref.6, ...), custom_call_target="tpu_custom_call" | custom-call | flops 34500001792 | bytes 1024 | tf_op jit(solution)/shard_map/pallas_call | solution.py:552
  58.2 13.8 %shard_map.308 = (f32[192,1152]{1,0:T(8,128)}, bf16[192,1152]{1,0:T(8,128)(2,1)}, bf16[2,2304,192]{2,1,0:T(8,128)(2,1)}, f32[384,1152]{1,0:T(8,128)}, f32[192,11...) custom-call(s32[1]{0:T(128)} %bitcast.core_ref, ...), custom_call_target="tpu_custom_call", output_to_operand_aliasing={{3}: (11, {})} | custom-call | flops 34500001792 | bytes 1024 | tf_op jit(solution)/shard_map/pallas_call | solution.py:552
  80.0 17.1 %shard_map.309 = (f32[288,1152]{1,0:T(8,128)}, f32[288,1152]{1,0:T(8,128)}, f32[288,1152]{1,0:T(8,128)}, f32[288,1152]{1,0:T(8,128)}, f32[288,1152]{1,0:T(8,128)...) custom-call(s32[1]{0:T(128)} %bitcast.core_ref, s32[4]{0:T(128)} %pad_add_fusion.sides_ref, ...), custom_call_target="tpu_custom_call" | custom-call | flops 4600000000 | bytes 1024 | tf_op jit(solution)/shard_map/pallas_call | solution.py:646
  102.9 11.7 %collective-permute-done.10.received_ref = f32[384,1152]{1,0:T(8,128)S(1)} collective-permute-done((f32[384,1152]{1,0:T(8,128)}, f32[384,1152]{1,0:T(8,128)S(1)}, u32[]{:S(2)}, u32[]{:S(2)}) %collective-permute-start.10) | collective-permute-done | bytes 1769504 | tf_op jit(solution)/shard_map/mid_move/ppermute | solution.py:60
  116.0 10.7 %shard_map.310 = (f32[192,1152]{1,0:T(8,128)}, bf16[192,1152]{1,0:T(8,128)(2,1)}, f32[8,1152]{1,0:T(8,128)}, bf16[576,192]{1,0:T(8,128)(2,1)}, bf16[576,192]{1,0...) custom-call(s32[1]{0:T(128)} %bitcast.core_ref, s32[2,4]{1,0:T(2,128)} %layout_ref.7, ...), custom_call_target="tpu_custom_call" | custom-call | flops 23000000 | bytes 1024 | tf_op jit(solution)/shard_map/pallas_call | solution.py:447
  126.8 10.7 %shard_map.311 = (f32[192,1152]{1,0:T(8,128)}, bf16[192,1152]{1,0:T(8,128)(2,1)}, f32[8,1152]{1,0:T(8,128)}, bf16[576,192]{1,0:T(8,128)(2,1)}, bf16[576,192]{1,0...) custom-call(s32[1]{0:T(128)} %bitcast.core_ref, s32[2,4]{1,0:T(2,128)} %layout_ref.7, ...), custom_call_target="tpu_custom_call" | custom-call | flops 23000000 | bytes 1024 | tf_op jit(solution)/shard_map/pallas_call | solution.py:447
  150.4 9.8 %shard_map.312 = f32[1152,1152]{1,0:T(8,128)} custom-call(s32[1]{0:T(128)} %bitcast.core_ref, bf16[576,192]{1,0:T(8,128)(2,1)} %get-tuple-element.496.refs_0_, bf16[576,192]{1,0:T(8,128)(2,1)} %get-tuple-element.497.refs_1_, bf16[576,192]{1,0:T(8,128)(2,1)} %get-tuple-element.431.refs_2_, bf16[576,192]{1,0:T(8,128)(2,1)} %get-tuple-element.403.refs_3_, ...), custom_call_target="tpu_custom_call" | custom-call | flops 23000000 | bytes 1024 | tf_op jit(solution)/shard_map/pallas_call | solution.py:725
  174.6 7.6 %collective-permute-done.23 = f32[2,72,1152]{2,1,0:T(8,128)S(1)} collective-permute-done((f32[2,72,1152]{2,1,0:T(8,128)}, f32[2,72,1152]{2,1,0:T(8,128)S(1)}, u32[]{:S(2)}, u32[]{:S(2)}) %collective-permute-start.23) | collective-permute-done | bytes 663584 | tf_op jit(solution)/shard_map/ff3_move_2/ppermute | solution.py:56
  185.5 3.5 collective-permute-done.21
  195.4 7.8 %collective-permute-done.27 = f32[1,72,1152]{2,1,0:T(8,128)S(1)} collective-permute-done((f32[1,72,1152]{2,1,0:T(8,128)S(1)}, f32[1,72,1152]{2,1,0:T(8,128)S(1)}, u32[]{:S(2)}, u32[]{:S(2)}) %collective-permute-start.27) | collective-permute-done | bytes 331808 | tf_op jit(solution)/shard_map/ff3_move_3/ppermute | solution.py:56
  212.7 3.5 collective-permute-done.32
  240.0 5.6 %collective-permute-done.38 = f32[9,1152]{1,0:T(8,128)S(1)} collective-permute-done((f32[9,1152]{1,0:T(8,128)S(1)}, f32[9,1152]{1,0:T(8,128)S(1)}, u32[]{:S(2)}, u32[]{:S(2)}) %collective-permute-start.38) | collective-permute-done | bytes 41504 | tf_op jit(solution)/shard_map/small_move_z/ppermute | solution.py:56
  270.9 7.2 %collective-permute-done.52 = f32[2,72,1152]{2,1,0:T(8,128)} collective-permute-done((f32[2,72,1152]{2,1,0:T(8,128)S(1)}, f32[2,72,1152]{2,1,0:T(8,128)}, u32[]{:S(2)}, u32[]{:S(2)}) %collective-permute-start.52) | collective-permute-done | bytes 663584 | tf_op jit(solution)/shard_map/ff3_move_8/ppermute | solution.py:56
  292.7 11.7 %collective-permute-done.58 = f32[192,1152]{1,0:T(8,128)S(1)} collective-permute-done((f32[192,1152]{1,0:T(8,128)}, f32[192,1152]{1,0:T(8,128)S(1)}, u32[]{:S(2)}, u32[]{:S(2)}) %collective-permute-start.58) | collective-permute-done | bytes 884768 | tf_op jit(solution)/shard_map/output_move_1/ppermute | solution.py:60
  304.3 16.5 %collective-permute-start.59 = (f32[288,1152]{1,0:T(8,128)}, f32[288,1152]{1,0:T(8,128)S(1)}, u32[]{:S(2)}, u32[]{:S(2)}) collective-permute-start(f32[288,1152]{1,0:T(8,128)} %bitcast.62), channel_id=1, source_target_pairs={{0,2},{2,0},{4,6},{6,4},{8,10},{10,8},{12,14},{14,12},{16,18},{18,... | collective-permute-start | bytes 3981320 | tf_op jit(solution)/shard_map/ff_core_other_0/ppermute | solution.py:56
  320.9 8.1 %collective-permute-start.65 = (f32[288,1152]{1,0:T(8,128)}, f32[288,1152]{1,0:T(8,128)S(1)}, u32[]{:S(2)}, u32[]{:S(2)}) collective-permute-start(f32[288,1152]{1,0:T(8,128)} %bitcast.60), channel_id=1, source_target_pairs={{0,2},{2,0},{4,6},{6,4},{8,10},{10,8},{12,14},{14,12},{16,18},{18,... | collective-permute-start | bytes 3981320 | tf_op jit(solution)/shard_map/ff_core_other_1/ppermute | solution.py:56
  331.0 3.7 fusion
  358.1 4.4 %all-gather.2.cloned.1.call-done = f32[1152,1152]{1,0:T(8,128)} async-done(((f32[72,1152]{1,0:T(8,128)}), f32[1152,1152]{1,0:T(8,128)}) %all-gather.2.cloned.1.call-update) | async-done | bytes 5308432 | tf_op jit(solution)/shard_map/at_gather/all_gather | solution.py:968
  362.5 4.4 %fusion.6 = (f32[576,1152]{1,0:T(8,128)}, f32[576,1152]{1,0:T(8,128)S(1)}) fusion(f32[1152,1152]{1,0:T(8,128)} %all-gather.2.cloned.1.call-done), kind=kLoop, calls=%fused_computation.80 | loop fusion | bytes 10616832 | tf_op jit(solution)/shard_map/slice | solution.py:991
  376.2 5.7 %shard_map.318 = (f32[576,1152]{1,0:T(8,128)}, f32[576,1152]{1,0:T(8,128)}) custom-call(s32[1]{0:T(128)} %bitcast.core_ref, f32[576,1152]{1,0:T(8,128)} %get-tuple-element.618.own_ref, f32[576,1152]{1,0:T(8,128)} %collective-permute-done.71.other_ref), custom_call_target="tpu_custom_call" | custom-call | flops 9200000000 | bytes 1024 | tf_op jit(solution)/shard_map/pallas_call | solution.py:178
  381.9 4.5 %shard_map.317 = (f32[576,1152]{1,0:T(8,128)}, f32[576,1152]{1,0:T(8,128)}) custom-call(s32[1]{0:T(128)} %bitcast.core_ref, f32[576,1152]{1,0:T(8,128)S(1)} %get-tuple-element.619.own_ref, f32[576,1152]{1,0:T(8,128)} %collective-permute-done.70.other_ref), custom_call_target="tpu_custom_call" | custom-call | flops 9200000000 | bytes 1024 | tf_op jit(solution)/shard_map/pallas_call | solution.py:178
  (337 shorter events, 170.1 us)
Async XLA Ops:
  7.2 262.1 %reduce-scatter.4.cloned.1.call-start = ((), (), s32[]{:S(2)}) async-start(), calls=%async_computation.2 | async-start | bytes 5640192
  17.0 22.1 %collective-permute-start = (f32[192,1152]{1,0:T(8,128)}, f32[192,1152]{1,0:T(8,128)S(1)}, u32[]{:S(2)}, u32[]{:S(2)}) collective-permute-start(f32[192,1152]{1,0:T(8,128)} %get-tuple-element.328.branch_ref), channel_id=1, source_target_pairs={{0,1},{1,0},{2,3},{3,2},{4,5},{5,4},{6,7},{7,6},{8,9},{9,8},{10,11... | collective-permute-start | bytes 2654216 | tf_op jit(solution)/shard_map/branch_move_0/ppermute | solution.py:60
  19.5 35.6 %collective-permute-start.1 = (f32[192,1152]{1,0:T(8,128)}, f32[192,1152]{1,0:T(8,128)S(1)}, u32[]{:S(2)}, u32[]{:S(2)}) collective-permute-start(f32[192,1152]{1,0:T(8,128)} %get-tuple-element.336), channel_id=1, source_target_pairs={{0,2},{2,0},{4,6},{6,4},{8,10},{10,8},{12,14},{14,12},{16,18},{18,... | collective-permute-start | bytes 2654216 | tf_op jit(solution)/shard_map/early_core_move_0/ppermute | solution.py:56
  20.5 34.7 %collective-permute-start.2 = (f32[576,256]{1,0:T(8,128)}, f32[576,256]{1,0:T(8,128)S(1)}, u32[]{:S(2)}, u32[]{:S(2)}) collective-permute-start(f32[576,256]{1,0:T(8,128)} %get-tuple-element.337), channel_id=1, source_target_pairs={{0,2},{2,0},{4,6},{6,4},{8,10},{10,8},{12,14},{14,12},{16,18},{18,... | collective-permute-start | bytes 1769480 | tf_op jit(solution)/shard_map/early_core_move_0/ppermute | solution.py:56
  30.2 27.9 %collective-permute-start.3 = (f32[192,1152]{1,0:T(8,128)}, f32[192,1152]{1,0:T(8,128)}, u32[]{:S(2)}, u32[]{:S(2)}) collective-permute-start(f32[192,1152]{1,0:T(8,128)} %get-tuple-element.348.branch_ref), channel_id=1, source_target_pairs={{0,1},{1,0},{2,3},{3,2},{4,5},{5,4},{6,7},{7,6},{8,9},{9,8},{10,11... | collective-permute-start | bytes 2654216 | tf_op jit(solution)/shard_map/branch_move_1/ppermute | solution.py:60
  30.2 41.8 %collective-permute-start.4 = (f32[192,1152]{1,0:T(8,128)}, f32[192,1152]{1,0:T(8,128)S(1)}, u32[]{:S(2)}, u32[]{:S(2)}) collective-permute-start(f32[192,1152]{1,0:T(8,128)} %get-tuple-element.357), channel_id=1, source_target_pairs={{0,2},{2,0},{4,6},{6,4},{8,10},{10,8},{12,14},{14,12},{16,18},{18,... | collective-permute-start | bytes 2654216 | tf_op jit(solution)/shard_map/early_core_move_1/ppermute | solution.py:56
  39.1 32.9 %collective-permute-start.5 = (f32[576,256]{1,0:T(8,128)}, f32[576,256]{1,0:T(8,128)S(1)}, u32[]{:S(2)}, u32[]{:S(2)}) collective-permute-start(f32[576,256]{1,0:T(8,128)} %get-tuple-element.358), channel_id=1, source_target_pairs={{0,2},{2,0},{4,6},{6,4},{8,10},{10,8},{12,14},{14,12},{16,18},{18,... | collective-permute-start | bytes 1769480 | tf_op jit(solution)/shard_map/early_core_move_1/ppermute | solution.py:56
  74.2 40.4 %collective-permute-start.10 = (f32[384,1152]{1,0:T(8,128)}, f32[384,1152]{1,0:T(8,128)S(1)}, u32[]{:S(2)}, u32[]{:S(2)}) collective-permute-start(f32[384,1152]{1,0:T(8,128)} %get-tuple-element.395.part_ref), channel_id=1, source_target_pairs={{0,1},{1,0},{2,3},{3,2},{4,5},{5,4},{6,7},{7,6},{8,9},{9,8},{10,11... | collective-permute-start | bytes 5308424 | tf_op jit(solution)/shard_map/mid_move/ppermute | solution.py:60
  97.1 41.6 %collective-permute-start.14 = (f32[4,72,1152]{2,1,0:T(8,128)}, f32[4,72,1152]{2,1,0:T(8,128)S(1)}, u32[]{:S(2)}, u32[]{:S(2)}) collective-permute-start(f32[4,72,1152]{2,1,0:T(8,128)} %bitcast.92), channel_id=1, source_target_pairs={{0,12},{2,14},{4,8},{6,10},{8,4},{10,6},{12,0},{14,2},{16,28},{18,... | collective-permute-start | bytes 3981320 | tf_op jit(solution)/shard_map/ff3_move_1/ppermute | solution.py:56
  99.9 39.7 %collective-permute-start.11 = (f32[4,72,1152]{2,1,0:T(8,128)}, f32[4,72,1152]{2,1,0:T(8,128)}, u32[]{:S(2)}, u32[]{:S(2)}) collective-permute-start(f32[4,72,1152]{2,1,0:T(8,128)} %bitcast.91), channel_id=1, source_target_pairs={{0,16},{2,18},{4,20},{6,22},{8,24},{10,26},{12,28},{14,30},{16,0},... | collective-permute-start | bytes 3981320 | tf_op jit(solution)/shard_map/ff0_move_1/ppermute | solution.py:56
  101.1 38.6 %collective-permute-start.12 = (f32[4,72,1152]{2,1,0:T(8,128)}, f32[4,72,1152]{2,1,0:T(8,128)}, u32[]{:S(2)}, u32[]{:S(2)}) collective-permute-start(f32[4,72,1152]{2,1,0:T(8,128)} %bitcast.90), channel_id=1, source_target_pairs={{0,4},{2,6},{4,0},{6,2},{8,12},{10,14},{12,8},{14,10},{16,20},{18,... | collective-permute-start | bytes 3981320 | tf_op jit(solution)/shard_map/ff1_move_1/ppermute | solution.py:56
  101.1 39.0 %collective-permute-start.13 = (f32[4,72,1152]{2,1,0:T(8,128)}, f32[4,72,1152]{2,1,0:T(8,128)}, u32[]{:S(2)}, u32[]{:S(2)}) collective-permute-start(f32[4,72,1152]{2,1,0:T(8,128)} %bitcast.89), channel_id=1, source_target_pairs={{0,48},{2,50},{4,52},{6,54},{8,56},{10,58},{12,60},{14,62},{16,32}... | collective-permute-start | bytes 3981320 | tf_op jit(solution)/shard_map/ff2_move_1/ppermute | solution.py:56
  114.6 22.9 %collective-permute-start.15 = (f32[192,1152]{1,0:T(8,128)S(1)}, f32[192,1152]{1,0:T(8,128)S(1)}, u32[]{:S(2)}, u32[]{:S(2)}) collective-permute-start(f32[192,1152]{1,0:T(8,128)S(1)} %copy-done.33), channel_id=1, source_target_pairs={{0,1},{1,0},{2,3},{3,2},{4,5},{5,4},{6,7},{7,6},{8,9},{9,8},{10,11... | collective-permute-start | bytes 2654216 | tf_op jit(solution)/shard_map/output_move_0/ppermute | solution.py:60
  160.3 202.2 %all-gather.2.cloned.1.call-start = ((), (), s32[]{:S(2)}) async-start(), calls=%async_computation.1 | async-start | bytes 5640192 | tf_op jit(solution)/shard_map/at_gather/all_gather | solution.py:968
  162.0 20.2 %collective-permute-start.23 = (f32[2,72,1152]{2,1,0:T(8,128)}, f32[2,72,1152]{2,1,0:T(8,128)S(1)}, u32[]{:S(2)}, u32[]{:S(2)}) collective-permute-start(f32[2,72,1152]{2,1,0:T(8,128)} %get-tuple-element.452), channel_id=1, source_target_pairs={{0,16},{2,18},{4,20},{6,22},{8,24},{10,26},{12,28},{14,30},{16,0},... | collective-permute-start | bytes 1990664 | tf_op jit(solution)/shard_map/ff3_move_2/ppermute | solution.py:56
  163.3 22.1 %collective-permute-start.22 = (f32[2,72,1152]{2,1,0:T(8,128)}, f32[2,72,1152]{2,1,0:T(8,128)S(1)}, u32[]{:S(2)}, u32[]{:S(2)}) collective-permute-start(f32[2,72,1152]{2,1,0:T(8,128)} %get-tuple-element.451), channel_id=1, source_target_pairs={{0,12},{2,14},{4,8},{6,10},{8,4},{10,6},{12,0},{14,2},{16,28},{18,... | collective-permute-start | bytes 1990664 | tf_op jit(solution)/shard_map/ff2_move_2/ppermute | solution.py:56
  166.1 22.9 %collective-permute-start.21 = (f32[2,72,1152]{2,1,0:T(8,128)}, f32[2,72,1152]{2,1,0:T(8,128)S(1)}, u32[]{:S(2)}, u32[]{:S(2)}) collective-permute-start(f32[2,72,1152]{2,1,0:T(8,128)} %get-tuple-element.450), channel_id=1, source_target_pairs={{0,48},{2,50},{4,52},{6,54},{8,56},{10,58},{12,60},{14,62},{16,32}... | collective-permute-start | bytes 1990664 | tf_op jit(solution)/shard_map/ff1_move_2/ppermute | solution.py:56
  167.9 22.7 %collective-permute-start.20 = (f32[2,72,1152]{2,1,0:T(8,128)}, f32[2,72,1152]{2,1,0:T(8,128)S(1)}, u32[]{:S(2)}, u32[]{:S(2)}) collective-permute-start(f32[2,72,1152]{2,1,0:T(8,128)} %get-tuple-element.449), channel_id=1, source_target_pairs={{0,4},{2,6},{4,0},{6,2},{8,12},{10,14},{12,8},{14,10},{16,20},{18,... | collective-permute-start | bytes 1990664 | tf_op jit(solution)/shard_map/ff0_move_2/ppermute | solution.py:56
  173.6 21.1 %collective-permute-start.28 = (f32[192,1152]{1,0:T(8,128)S(1)}, f32[192,1152]{1,0:T(8,128)S(1)}, u32[]{:S(2)}, u32[]{:S(2)}) collective-permute-start(f32[192,1152]{1,0:T(8,128)S(1)} %convolution_add_fusion.2), channel_id=1, source_target_pairs={{0,1},{1,0},{2,3},{3,2},{4,5},{5,4},{6,7},{7,6},{8,9},{9,8},{10,11... | collective-permute-start | bytes 2654216 | tf_op jit(solution)/shard_map/normed_move_0/ppermute | solution.py:60
  290.8 30.0 %collective-permute-start.57 = (f32[4,72,1152]{2,1,0:T(8,128)S(1)}, f32[4,72,1152]{2,1,0:T(8,128)S(1)}, u32[]{:S(2)}, u32[]{:S(2)}) collective-permute-start(f32[4,72,1152]{2,1,0:T(8,128)S(1)} %maximum_select_fusion.3), channel_id=1, source_target_pairs={{0,12},{2,14},{4,8},{6,10},{8,4},{10,6},{12,0},{14,2},{16,28},{18,... | collective-permute-start | bytes 3981320 | tf_op jit(solution)/shard_map/ff3_move_9/ppermute | solution.py:56
  292.1 36.9 %collective-permute-start.56 = (f32[4,72,1152]{2,1,0:T(8,128)S(1)}, f32[4,72,1152]{2,1,0:T(8,128)S(1)}, u32[]{:S(2)}, u32[]{:S(2)}) collective-permute-start(f32[4,72,1152]{2,1,0:T(8,128)S(1)} %maximum_select_fusion.2), channel_id=1, source_target_pairs={{0,48},{2,50},{4,52},{6,54},{8,56},{10,58},{12,60},{14,62},{16,32}... | collective-permute-start | bytes 3981320 | tf_op jit(solution)/shard_map/ff2_move_9/ppermute | solution.py:56
  292.1 36.9 %collective-permute-start.55 = (f32[4,72,1152]{2,1,0:T(8,128)}, f32[4,72,1152]{2,1,0:T(8,128)S(1)}, u32[]{:S(2)}, u32[]{:S(2)}) collective-permute-start(f32[4,72,1152]{2,1,0:T(8,128)} %maximum_select_fusion.1), channel_id=1, source_target_pairs={{0,4},{2,6},{4,0},{6,2},{8,12},{10,14},{12,8},{14,10},{16,20},{18,... | collective-permute-start | bytes 3981320 | tf_op jit(solution)/shard_map/ff1_move_9/ppermute | solution.py:56
  292.1 36.9 %collective-permute-start.54 = (f32[4,72,1152]{2,1,0:T(8,128)}, f32[4,72,1152]{2,1,0:T(8,128)S(1)}, u32[]{:S(2)}, u32[]{:S(2)}) collective-permute-start(f32[4,72,1152]{2,1,0:T(8,128)} %maximum_select_fusion), channel_id=1, source_target_pairs={{0,16},{2,18},{4,20},{6,22},{8,24},{10,26},{12,28},{14,30},{16,0},... | collective-permute-start | bytes 3981320 | tf_op jit(solution)/shard_map/ff0_move_9/ppermute | solution.py:56
  304.3 30.9 %collective-permute-start.59 = (f32[288,1152]{1,0:T(8,128)}, f32[288,1152]{1,0:T(8,128)S(1)}, u32[]{:S(2)}, u32[]{:S(2)}) collective-permute-start(f32[288,1152]{1,0:T(8,128)} %bitcast.62), channel_id=1, source_target_pairs={{0,2},{2,0},{4,6},{6,4},{8,10},{10,8},{12,14},{14,12},{16,18},{18,... | collective-permute-start | bytes 3981320 | tf_op jit(solution)/shard_map/ff_core_other_0/ppermute | solution.py:56
  (109 other events, 936.4 us)
Sparse Core Ops, SparseCore 0:
  160.4 86.0 reduce-scatter.3
  291.0 71.4 all-gather.1
